TPU v7x, 512 devices: a whole 4x4x16 slice. The times are simulated.
512 devices in a mesh: gx: 4 (over x_lo, core), gy: 8 (over x_hi, y), gz: 16 (over z).
Axes of the slice: x: 4 (x_hi: 2, x_lo: 2; x = x_hi * 2 + x_lo), y: 4, z: 16, core: 2. Of those that a mesh axis runs over, the one named last changes fastest.
Arguments:
- e_field: float32 [3, 256, 128, 1024], P(None, 'gz', 'gx', 'gy'), may hold values from -6 to 6
- h_field: float32 [3, 256, 128, 1024], P(None, 'gz', 'gx', 'gy'), may hold values from -6 to 6
- material: int32 [256, 128, 1024], P('gz', 'gx', 'gy'), may hold values from 0 to 7
- inv_permittivity: float32 [8], replicated, may hold values from 0.08 to 1
- block_cells: int32 [65536, 128], P(('gx', 'gy', 'gz')), may hold values from 0 to 65535, as said below
- block_count: int32 [512], P(('gx', 'gy', 'gz')), may hold values from 1 to 128, 33024 in all
- block_decay: float32 [65536], P(('gx', 'gy', 'gz')), may hold values from 0.6 to 0.98
- block_restore: float32 [65536], P(('gx', 'gy', 'gz')), may hold values from 0.02 to 0.3
- block_drive: float32 [65536], P(('gx', 'gy', 'gz')), may hold values from 0.05 to 0.5
- polarization: float32 [3, 65536, 128], P(None, ('gx', 'gy', 'gz')), may hold values from -6 to 6
- current: float32 [3, 65536, 128], P(None, ('gx', 'gy', 'gz')), may hold values from -6 to 6
Outputs:
- e_out: float32 [3, 256, 128, 1024], P(None, 'gz', 'gx', 'gy')
- h_out: float32 [3, 256, 128, 1024], P(None, 'gz', 'gx', 'gy')
- pol_out: float32 [3, 65536, 128], P(None, ('gx', 'gy', 'gz'))
- cur_out: float32 [3, 65536, 128], P(None, ('gx', 'gy', 'gz'))
Inputs may be any that keep to these rules, and one draw needn't show every extreme that they name: `block_cells`: each row of a device's 128 rows holds, in some order, all 128 local cells of one aligned run [s * 128, (s + 1) * 128); different rows of one device hold different runs. `block_count`: the number of live leading rows among each device's 128 rows; the counts sum to 512 * 129 // 2.
All inputs are finite; a program needn't handle non-finite values.
Results may differ from a plain program's by a relative error of at most 0.00013.
Values sent between devices are 32-bit elements; how exact they have to be, the bound alone decides.
No kernel may reach another device: no remote copies, remote signals or barrier semaphores. Data moves between devices by JAX's collectives and lax.ppermute only.
A program may use at most 128 MiB of HBM per device.

v0:
```python
import jax
import jax.numpy as jnp
from jax import lax
from jax.sharding import PartitionSpec as P

STEPS = 2


TIME_STEP = 0.5


def passed_along(value, axis, steps):
    count = lax.axis_size(axis)
    first, last = (max(0, -steps), min(count, count - steps))
    return lax.ppermute(value, axis, [(source, source + steps) for source in range(first, last)])


def rising(values, plane, along):
    length = values.shape[along]
    upper = lax.slice_in_dim(values, 1, length, axis=along)
    return jnp.concatenate([upper, plane], along) - values


def falling(values, plane, along):
    length = values.shape[along]
    lower = lax.slice_in_dim(values, 0, length - 1, axis=along)
    return values - jnp.concatenate([plane, lower], along)


def curl_forward(field, plane_x, plane_y, plane_z):
    curl_x = rising(field[2], plane_y[1][:, :, None], 2) - rising(field[1], plane_z[1][None], 0)
    curl_y = rising(field[0], plane_z[0][None], 0) - rising(field[2], plane_x[1][:, None, :], 1)
    curl_z = rising(field[1], plane_x[0][:, None, :], 1) - rising(
        field[0], plane_y[0][:, :, None], 2
    )
    return jnp.stack([curl_x, curl_y, curl_z])


def curl_backward(field, plane_x, plane_y, plane_z):
    curl_x = falling(field[2], plane_y[1][:, :, None], 2) - falling(field[1], plane_z[1][None], 0)
    curl_y = falling(field[0], plane_z[0][None], 0) - falling(field[2], plane_x[1][:, None, :], 1)
    curl_z = falling(field[1], plane_x[0][:, None, :], 1) - falling(
        field[0], plane_y[0][:, :, None], 2
    )
    return jnp.stack([curl_x, curl_y, curl_z])


def e_planes(e_field):
    first_x = jnp.stack([e_field[1][:, 0, :], e_field[2][:, 0, :]])
    first_y = jnp.stack([e_field[0][:, :, 0], e_field[2][:, :, 0]])
    first_z = e_field[0:2, 0]
    got_x = passed_along(first_x, "gx", -1)
    got_y = passed_along(first_y, "gy", -1)
    got_z = passed_along(first_z, "gz", -1)
    return (got_x, got_y, got_z)


def h_planes(h_field):
    last_x = jnp.stack([h_field[1][:, -1, :], h_field[2][:, -1, :]])
    last_y = jnp.stack([h_field[0][:, :, -1], h_field[2][:, :, -1]])
    last_z = h_field[0:2, -1]
    got_x = passed_along(last_x, "gx", 1)
    got_y = passed_along(last_y, "gy", 1)
    got_z = passed_along(last_z, "gz", 1)
    return (got_x, got_y, got_z)


def block_tables(block_cells, total_cells):
    width = block_cells.shape[1]
    run_count = total_cells // width
    run_of_row = block_cells[:, 0] // width
    offsets = block_cells % width
    run_select = (run_of_row[:, None] == jnp.arange(run_count, dtype=jnp.int32)[None, :]).astype(
        jnp.float32
    )
    order = (offsets[:, :, None] == jnp.arange(width, dtype=jnp.int32)[None, None, :]).astype(
        jnp.float32
    )
    return (run_select, order)


def pick_cells(flat, run_select, order):
    width = order.shape[2]
    runs = flat.reshape(flat.shape[0], -1, width)
    rows = jnp.einsum("bs,asc->abc", run_select, runs, precision=lax.Precision.HIGHEST)
    return jnp.einsum("bkc,abc->abk", order, rows, precision=lax.Precision.HIGHEST)


def place_cells(values, run_select, order):
    rows = jnp.einsum("bkc,abk->abc", order, values, precision=lax.Precision.HIGHEST)
    cells = jnp.einsum("bs,abc->asc", run_select, rows, precision=lax.Precision.HIGHEST)
    return cells.reshape(values.shape[0], -1)


def on_device(
    e_field,
    h_field,
    material,
    inv_permittivity,
    block_cells,
    block_count,
    block_decay,
    block_restore,
    block_drive,
    polarization,
    current,
):
    slots, width = (block_cells.shape[0], block_cells.shape[1])
    total_cells = e_field.shape[1] * e_field.shape[2] * e_field.shape[3]
    run_select, order = block_tables(block_cells, total_cells)
    live_rows = jnp.arange(slots, dtype=jnp.int32) < block_count[0]
    live = live_rows[None, :, None]
    kinds = jnp.arange(inv_permittivity.shape[0], dtype=jnp.int32)
    cell_inv = jnp.sum(
        jnp.where(
            material[None] == kinds[:, None, None, None],
            inv_permittivity[:, None, None, None],
            jnp.float32(0.0),
        ),
        0,
    )
    decay = block_decay[None, :, None]
    restore = block_restore[None, :, None]
    drive = block_drive[None, :, None]
    for step in range(STEPS):
        got = e_planes(e_field)
        h_field = h_field - TIME_STEP * curl_forward(e_field, *got)
        flat_e = e_field.reshape(3, -1)
        at_cells = pick_cells(flat_e, run_select, order)
        current = jnp.where(
            live, decay * current - restore * polarization + drive * at_cells, current
        )
        polarization = jnp.where(live, polarization + TIME_STEP * current, polarization)
        placed = jnp.where(live, current, jnp.float32(0.0))
        j_flat = place_cells(placed, run_select, order)
        j_cells = j_flat.reshape(e_field.shape)
        got_h = h_planes(h_field)
        e_field = e_field + TIME_STEP * cell_inv * (curl_backward(h_field, *got_h) - j_cells)
    return (e_field, h_field, polarization, current)


def solution(mesh):
    placed = (
        P(None, "gz", "gx", "gy"),
        P(None, "gz", "gx", "gy"),
        P("gz", "gx", "gy"),
        P(),
        P(("gx", "gy", "gz"), None),
        P(("gx", "gy", "gz")),
        P(("gx", "gy", "gz")),
        P(("gx", "gy", "gz")),
        P(("gx", "gy", "gz")),
        P(None, ("gx", "gy", "gz"), None),
        P(None, ("gx", "gy", "gz"), None),
    )
    return jax.shard_map(
        on_device,
        mesh=mesh,
        in_specs=placed,
        out_specs=(
            P(None, "gz", "gx", "gy"),
            P(None, "gz", "gx", "gy"),
            P(None, ("gx", "gy", "gz"), None),
            P(None, ("gx", "gy", "gz"), None),
        ),
        check_vma=False,
    )
```

profile of v0, /device:TPU:409, one launch (start us, length us, event | category | flops | bytes accessed | tf_op | source)
XLA Modules:
  0.0 118.8 jit_solution(17234604370478552313)
XLA Ops:
  0.6 1.2 %slice_bitcast_fusion.26 = (f32[16,32,128]{2,1,0:T(8,128)S(1)}, f32[16,32,128]{2,1,0:T(8,128)S(1)}, f32[16,32,128]{2,1,0:T(8,128)S(1)}) fusion(f32[3,16,32,128]{3,2,1,0:T(8,128)} %param.11), kind=kLoop, calls=%fused_computation.115 | loop fusion | bytes 1572864 | tf_op jit(solution)/shard_map/squeeze | solution.py:50
  2.1 2.4 %collective-permute-start = (f32[2,16,32]{2,1,0:T(8,128)S(1)}, f32[2,16,32]{2,1,0:T(8,128)S(1)}, u32[]{:S(2)}, u32[]{:S(2)}) collective-permute-start(f32[2,16,32]{2,1,0:T(8,128)S(1)} %pad_maximum_fusion), channel_id=1, source_target_pairs={{16,0},{32,16},{48,32},{64,48},{80,64},{96,80},{112,96},{17,1},{33... | collective-permute-start | bytes 12296 | tf_op jit(solution)/shard_map/ppermute | solution.py:15
  4.5 0.6 pad_maximum_fusion.1
  5.1 2.9 %collective-permute-start.2 = (f32[2,16,128]{2,1,0:T(8,128)}, f32[2,16,128]{2,1,0:T(8,128)S(1)}, u32[]{:S(2)}, u32[]{:S(2)}) collective-permute-start(f32[2,16,128]{2,1,0:T(8,128)} %pad_maximum_fusion.1), channel_id=1, source_target_pairs={{128,0},{256,128},{384,256},{129,1},{257,129},{385,257},{130,2},{2... | collective-permute-start | bytes 49160 | tf_op jit(solution)/shard_map/ppermute | solution.py:15
  8.0 3.8 %collective-permute-start.1 = (f32[2,32,128]{2,1,0:T(8,128)S(1)}, f32[2,32,128]{2,1,0:T(8,128)S(1)}, u32[]{:S(2)}, u32[]{:S(2)}) collective-permute-start(f32[2,32,128]{2,1,0:T(8,128)S(1)} %slice_bitcast_fusion.31), channel_id=1, source_target_pairs={{1,0},{2,1},{3,2},{4,3},{5,4},{6,5},{7,6},{8,7},{9,8},{10,9},{11,1... | collective-permute-start | bytes 98312 | tf_op jit(solution)/shard_map/ppermute | solution.py:15
  11.9 0.9 slice_bitcast_fusion.12
  12.8 0.8 slice_bitcast_fusion.13
  13.6 0.8 fusion.64
  15.3 0.5 convolution_bitcast_fusion.3
  15.9 9.7 %fusion.15 = f32[3,128,128]{2,0,1:T(4,128)S(1)} fusion(s32[128,128]{1,0:T(8,128)S(1)} %add_select_fusion.2, f32[3,128,128]{2,1,0:T(8,128)S(1)} %copy-done.17, f32[3,128,128]{2,1,0:T(8,128)S(1)} %copy-done.18, f32[3,128,128]{2,1,0:T(8,128)S(1)} %convolution_bitcast_fusion.3, f32[128]{0:T(128)S(1)} %copy-done.20, f32[128]{0:T(128)S(1)} %copy-done.22, ...), kind=kOutput, calls=%fused_computation.20 | convolution fusion | flops 77889536 | bytes 853632 | tf_op jit(solution)/shard_map/bkc,abc->abk/dot_general | solution.py:86
  25.6 0.7 copy-done.28
  26.3 5.9 %fusion.16 = f32[3,128,128]{2,0,1:T(4,128)S(1)} fusion(s32[128,128]{1,0:T(8,128)S(1)} %add_select_fusion.2, f32[3,128,128]{2,0,1:T(4,128)S(1)} %fusion.15, pred[128]{0:T(512)(128)(4,1)S(1)} %iota_compare_fusion.27), kind=kOutput, calls=%fused_computation.21 | convolution fusion | flops 77643776 | bytes 458880 | tf_op jit(solution)/shard_map/bkc,abk->abc/dot_general | solution.py:90
  32.3 0.6 convolution_bitcast_fusion.1
  32.9 0.4 copy-done.12
  33.3 0.3 select_reduce_fusion
  33.5 0.7 broadcast_multiply_fusion
  34.9 1.7 %fusion.25 = (f32[1,16,32,128]{3,2,1,0:T(8,128)S(1)}, f32[1,16,32,128]{3,2,1,0:T(8,128)S(1)}, f32[1,16,32,128]{3,2,1,0:T(8,128)S(1)}) fusion(f32[1,16,32,1]{3,2,1,0:T(8,128)S(1)} %copy.213, f32[1,16,32,127]{3,2,1,0:T(8,128)} %get-tuple-element.87, f32[1,1,32,128]{3,2,1,0:T(8,128)S(1)} %get-tuple-element.66, f32[1,15,32,128]{3,2,1,0:T(8,128)} %get-tuple-element.55, ...), kind=kLoop, calls=%fused_computation.65 | loop fusion | flops 983040 | bytes 3145728 | tf_op jit(solution)/shard_map/sub | solution.py:31
  36.8 0.5 copy-done.3
  37.8 0.7 slice_bitcast_fusion.10
  38.5 0.7 slice_bitcast_fusion.11
  39.5 0.7 slice_bitcast_fusion.8
  40.2 0.7 slice_bitcast_fusion.9
  40.9 0.8 fusion.63
  41.8 6.5 %collective-permute-start.3 = (f32[2,16,32]{2,1,0:T(8,128)S(1)}, f32[2,16,32]{2,1,0:T(8,128)S(1)}, u32[]{:S(2)}, u32[]{:S(2)}) collective-permute-start(f32[2,16,32]{2,1,0:T(8,128)S(1)} %pad_maximum_fusion.2), channel_id=1, source_target_pairs={{0,16},{16,32},{32,48},{48,64},{64,80},{80,96},{96,112},{1,17},{17... | collective-permute-start | bytes 12296 | tf_op jit(solution)/shard_map/ppermute | solution.py:15
  48.3 0.6 pad_maximum_fusion.3
  48.9 3.6 %collective-permute-start.5 = (f32[2,16,128]{2,1,0:T(8,128)}, f32[2,16,128]{2,1,0:T(8,128)}, u32[]{:S(2)}, u32[]{:S(2)}) collective-permute-start(f32[2,16,128]{2,1,0:T(8,128)} %pad_maximum_fusion.3), channel_id=1, source_target_pairs={{0,128},{128,256},{256,384},{1,129},{129,257},{257,385},{2,130},{1... | collective-permute-start | bytes 49160 | tf_op jit(solution)/shard_map/ppermute | solution.py:15
  52.5 1.9 %collective-permute-start.4 = (f32[2,32,128]{2,1,0:T(8,128)S(1)}, f32[2,32,128]{2,1,0:T(8,128)S(1)}, u32[]{:S(2)}, u32[]{:S(2)}) collective-permute-start(f32[2,32,128]{2,1,0:T(8,128)S(1)} %slice_bitcast_fusion.30), channel_id=1, source_target_pairs={{0,1},{1,2},{2,3},{3,4},{4,5},{5,6},{6,7},{7,8},{8,9},{9,10},{10,1... | collective-permute-start | bytes 98312 | tf_op jit(solution)/shard_map/ppermute | solution.py:15
  54.4 0.9 copy.219
  55.3 0.9 copy.223
  56.2 0.7 fusion.67
  56.9 1.8 %collective-permute-done.4 = f32[2,32,128]{2,1,0:T(8,128)S(1)} collective-permute-done((f32[2,32,128]{2,1,0:T(8,128)S(1)}, f32[2,32,128]{2,1,0:T(8,128)S(1)}, u32[]{:S(2)}, u32[]{:S(2)}) %collective-permute-start.4) | collective-permute-done | bytes 32800 | tf_op jit(solution)/shard_map/ppermute | solution.py:15
  58.8 1.8 %fusion.28 = (f32[1,16,32,128]{3,2,1,0:T(8,128)S(1)}, f32[1,16,32,128]{3,2,1,0:T(8,128)S(1)}, f32[1,16,32,128]{3,2,1,0:T(8,128)S(1)}) fusion(f32[1,16,32,127]{3,2,1,0:T(8,128)} %slice_bitcast_fusion.11, f32[1,16,32,1]{3,2,1,0:T(8,128)} %copy.219, f32[1,15,32,128]{3,2,1,0:T(8,128)} %get-tuple-element.47, f32[1,1,32,128]{3,2,1,0:T(8,128)S(1)} %get-tuple-element.64, ...), kind=kLoop, calls=%fused_computation.74 | loop fusion | flops 983040 | bytes 3145728 | tf_op jit(solution)/shard_map/sub | solution.py:40
  60.6 0.3 fusion.20
  61.3 0.9 slice_bitcast_fusion.4
  62.2 0.7 slice_bitcast_fusion.5
  62.9 0.7 slice_bitcast_fusion.6
  63.6 0.8 slice_bitcast_fusion.7
  64.4 0.8 fusion.62
  65.3 0.8 convolution_bitcast_fusion.2
  66.4 10.3 %add_select_fusion = (f32[3,128,128]{2,0,1:T(4,128)}, f32[3,128,128]{2,0,1:T(4,128)S(1)}) fusion(f32[3,128,128]{2,0,1:T(4,128)S(1)} %copy-done.29, f32[3,128,128]{2,1,0:T(8,128)S(1)} %copy-done.19, pred[128]{0:T(512)(128)(4,1)S(1)} %copy-done.27, f32[3,128,128]{2,0,1:T(4,128)S(1)} %copy.243, s32[128,128]{1,0:T(8,128)S(1)} %add_select_fusion.2, ...), kind=kOutput, calls=%fused_computation.35 | convolution fusion | flops 78184448 | bytes 1050240 | tf_op jit(solution)/shard_map/bkc,abc->abk/dot_general | solution.py:86
  76.7 5.9 %fusion.17 = f32[3,128,128]{2,0,1:T(4,128)S(1)} fusion(s32[128,128]{1,0:T(8,128)S(1)} %add_select_fusion.2, f32[3,128,128]{2,0,1:T(4,128)S(1)} %get-tuple-element.85, pred[128]{0:T(512)(128)(4,1)S(1)} %copy-done.27), kind=kOutput, calls=%fused_computation.22 | convolution fusion | flops 77643776 | bytes 458880 | tf_op jit(solution)/shard_map/bkc,abk->abc/dot_general | solution.py:90
  82.7 0.7 copy.247
  83.4 2.3 %collective-permute-start.8 = (f32[2,16,128]{2,1,0:T(8,128)S(1)}, f32[2,16,128]{2,1,0:T(8,128)S(1)}, u32[]{:S(2)}, u32[]{:S(2)}) collective-permute-start(f32[2,16,128]{2,1,0:T(8,128)S(1)} %pad_maximum_fusion.5), channel_id=1, source_target_pairs={{128,0},{256,128},{384,256},{129,1},{257,129},{385,257},{130,2},{2... | collective-permute-start | bytes 49160 | tf_op jit(solution)/shard_map/ppermute | solution.py:15
  85.7 1.9 %collective-permute-start.6 = (f32[2,16,32]{2,1,0:T(8,128)S(1)}, f32[2,16,32]{2,1,0:T(8,128)S(1)}, u32[]{:S(2)}, u32[]{:S(2)}) collective-permute-start(f32[2,16,32]{2,1,0:T(8,128)S(1)} %pad_maximum_fusion.4), channel_id=1, source_target_pairs={{16,0},{32,16},{48,32},{64,48},{80,64},{96,80},{112,96},{17,1},{33... | collective-permute-start | bytes 12296 | tf_op jit(solution)/shard_map/ppermute | solution.py:15
  87.6 2.4 %collective-permute-start.7 = (f32[2,32,128]{2,1,0:T(8,128)S(1)}, f32[2,32,128]{2,1,0:T(8,128)S(1)}, u32[]{:S(2)}, u32[]{:S(2)}) collective-permute-start(f32[2,32,128]{2,1,0:T(8,128)S(1)} %slice_bitcast_fusion.29), channel_id=1, source_target_pairs={{1,0},{2,1},{3,2},{4,3},{5,4},{6,5},{7,6},{8,7},{9,8},{10,9},{11,1... | collective-permute-start | bytes 98312 | tf_op jit(solution)/shard_map/ppermute | solution.py:15
  90.0 0.6 convolution_bitcast_fusion
  90.6 0.3 copy.245
  90.8 1.7 %copy.246 = f32[3,128,128]{2,1,0:T(8,128)} copy(f32[3,128,128]{2,0,1:T(4,128)} %get-tuple-element.84) | data formatting | bytes 393216
  92.6 1.4 %collective-permute-done.6 = f32[2,16,32]{2,1,0:T(8,128)S(1)} collective-permute-done((f32[2,16,32]{2,1,0:T(8,128)S(1)}, f32[2,16,32]{2,1,0:T(8,128)S(1)}, u32[]{:S(2)}, u32[]{:S(2)}) %collective-permute-start.6) | collective-permute-done | bytes 4128 | tf_op jit(solution)/shard_map/ppermute | solution.py:15
  93.9 0.9 copy.230
  94.8 0.9 copy.234
  95.8 1.6 %fusion.31 = (f32[1,16,32,128]{3,2,1,0:T(8,128)S(1)}, f32[1,16,32,128]{3,2,1,0:T(8,128)S(1)}, f32[1,16,32,128]{3,2,1,0:T(8,128)S(1)}) fusion(f32[1,16,32,1]{3,2,1,0:T(8,128)} %copy.230, f32[1,16,32,127]{3,2,1,0:T(8,128)} %slice_bitcast_fusion.7, f32[1,1,32,128]{3,2,1,0:T(8,128)S(1)} %get-tuple-element.62, f32[1,15,32,128]{3,2,1,0:T(8,128)} %get-tuple-element.39, ...), kind=kLoop, calls=%fused_computation.83 | loop fusion | flops 983040 | bytes 3145728 | tf_op jit(solution)/shard_map/sub | solution.py:31
  97.4 0.3 fusion.21
  98.1 0.3 slice_reduce_fusion.1
  98.4 0.7 slice_bitcast_fusion.3
  99.2 0.8 fusion.61
  100.0 5.6 %collective-permute-start.9 = (f32[2,16,32]{2,1,0:T(8,128)S(1)}, f32[2,16,32]{2,1,0:T(8,128)S(1)}, u32[]{:S(2)}, u32[]{:S(2)}) collective-permute-start(f32[2,16,32]{2,1,0:T(8,128)S(1)} %pad_maximum_fusion.6), channel_id=1, source_target_pairs={{0,16},{16,32},{32,48},{48,64},{64,80},{80,96},{96,112},{1,17},{17... | collective-permute-start | bytes 12296 | tf_op jit(solution)/shard_map/ppermute | solution.py:15
  105.6 4.5 %collective-permute-start.11 = (f32[2,16,128]{2,1,0:T(8,128)S(1)}, f32[2,16,128]{2,1,0:T(8,128)S(1)}, u32[]{:S(2)}, u32[]{:S(2)}) collective-permute-start(f32[2,16,128]{2,1,0:T(8,128)S(1)} %pad_maximum_fusion.7), channel_id=1, source_target_pairs={{0,128},{128,256},{256,384},{1,129},{129,257},{257,385},{2,130},{1... | collective-permute-start | bytes 49160 | tf_op jit(solution)/shard_map/ppermute | solution.py:15
  110.1 2.5 %collective-permute-start.10 = (f32[2,32,128]{2,1,0:T(8,128)S(1)}, f32[2,32,128]{2,1,0:T(8,128)S(1)}, u32[]{:S(2)}, u32[]{:S(2)}) collective-permute-start(f32[2,32,128]{2,1,0:T(8,128)S(1)} %slice_bitcast_fusion.28), channel_id=1, source_target_pairs={{0,1},{1,2},{2,3},{3,4},{4,5},{5,6},{6,7},{7,8},{8,9},{9,10},{10,1... | collective-permute-start | bytes 98312 | tf_op jit(solution)/shard_map/ppermute | solution.py:15
  112.7 0.9 copy.235
  113.5 0.9 copy.239
  114.4 1.5 %collective-permute-done.10 = f32[2,32,128]{2,1,0:T(8,128)S(1)} collective-permute-done((f32[2,32,128]{2,1,0:T(8,128)S(1)}, f32[2,32,128]{2,1,0:T(8,128)S(1)}, u32[]{:S(2)}, u32[]{:S(2)}) %collective-permute-start.10) | collective-permute-done | bytes 32800 | tf_op jit(solution)/shard_map/ppermute | solution.py:15
  116.0 1.6 %fusion.34 = (f32[1,16,32,128]{3,2,1,0:T(8,128)S(1)}, f32[1,16,32,128]{3,2,1,0:T(8,128)S(1)}, f32[1,16,32,128]{3,2,1,0:T(8,128)S(1)}) fusion(f32[1,16,32,127]{3,2,1,0:T(8,128)} %slice_bitcast_fusion.3, f32[1,16,32,1]{3,2,1,0:T(8,128)} %copy.235, f32[1,15,32,128]{3,2,1,0:T(8,128)} %get-tuple-element.31, f32[1,1,32,128]{3,2,1,0:T(8,128)S(1)} %get-tuple-element.60, ...), kind=kLoop, calls=%fused_computation.92 | loop fusion | flops 983040 | bytes 3145728 | tf_op jit(solution)/shard_map/sub | solution.py:40
  117.6 1.2 fusion.23
  (115 shorter events, 3.0 us)
Async XLA Ops:
  0.6 7.4 %copy-start = (f32[3,16,32,128]{3,2,1,0:T(8,128)S(1)}, f32[3,16,32,128]{3,2,1,0:T(8,128)}, u32[]{:S(2)}) copy-start(f32[3,16,32,128]{3,2,1,0:T(8,128)} %param.11) | copy-start | bytes 2359300
  2.1 32.4 %collective-permute-start = (f32[2,16,32]{2,1,0:T(8,128)S(1)}, f32[2,16,32]{2,1,0:T(8,128)S(1)}, u32[]{:S(2)}, u32[]{:S(2)}) collective-permute-start(f32[2,16,32]{2,1,0:T(8,128)S(1)} %pad_maximum_fusion), channel_id=1, source_target_pairs={{16,0},{32,16},{48,32},{64,48},{80,64},{96,80},{112,96},{17,1},{33... | collective-permute-start | bytes 12296 | tf_op jit(solution)/shard_map/ppermute | solution.py:15
  5.1 29.8 %collective-permute-start.2 = (f32[2,16,128]{2,1,0:T(8,128)}, f32[2,16,128]{2,1,0:T(8,128)S(1)}, u32[]{:S(2)}, u32[]{:S(2)}) collective-permute-start(f32[2,16,128]{2,1,0:T(8,128)} %pad_maximum_fusion.1), channel_id=1, source_target_pairs={{128,0},{256,128},{384,256},{129,1},{257,129},{385,257},{130,2},{2... | collective-permute-start | bytes 49160 | tf_op jit(solution)/shard_map/ppermute | solution.py:15
  8.0 26.9 %collective-permute-start.1 = (f32[2,32,128]{2,1,0:T(8,128)S(1)}, f32[2,32,128]{2,1,0:T(8,128)S(1)}, u32[]{:S(2)}, u32[]{:S(2)}) collective-permute-start(f32[2,32,128]{2,1,0:T(8,128)S(1)} %slice_bitcast_fusion.31), channel_id=1, source_target_pairs={{1,0},{2,1},{3,2},{4,3},{5,4},{6,5},{7,6},{8,7},{9,8},{10,9},{11,1... | collective-permute-start | bytes 98312 | tf_op jit(solution)/shard_map/ppermute | solution.py:15
  12.8 1.7 %copy-start.13 = (s32[128,128]{1,0:T(8,128)S(1)}, s32[128,128]{1,0:T(8,128)}, u32[]{:S(2)}) copy-start(s32[128,128]{1,0:T(8,128)} %param.15) | copy-start | bytes 196612
  14.4 1.4 %copy-start.17 = (f32[3,128,128]{2,1,0:T(8,128)S(1)}, f32[3,128,128]{2,1,0:T(8,128)}, u32[]{:S(2)}) copy-start(f32[3,128,128]{2,1,0:T(8,128)} %param.21) | copy-start | bytes 589828
  14.4 1.4 %copy-start.18 = (f32[3,128,128]{2,1,0:T(8,128)S(1)}, f32[3,128,128]{2,1,0:T(8,128)}, u32[]{:S(2)}) copy-start(f32[3,128,128]{2,1,0:T(8,128)} %param.20) | copy-start | bytes 589828
  14.4 1.4 %copy-start.20 = (f32[128]{0:T(128)S(1)}, f32[128]{0:T(128)}, u32[]{:S(2)}) copy-start(f32[128]{0:T(128)} %param.19) | copy-start | bytes 1540
  14.4 1.4 %copy-start.22 = (f32[128]{0:T(128)S(1)}, f32[128]{0:T(128)}, u32[]{:S(2)}) copy-start(f32[128]{0:T(128)} %param.18) | copy-start | bytes 1540
  14.5 1.4 %copy-start.24 = (f32[128]{0:T(128)S(1)}, f32[128]{0:T(128)}, u32[]{:S(2)}) copy-start(f32[128]{0:T(128)} %param.17) | copy-start | bytes 1540
  14.6 17.7 %copy-start.14 = (s32[128]{0:T(128)}, s32[128]{0:T(128)S(1)}, u32[]{:S(2)}) copy-start(s32[128]{0:T(128)S(1)} %fusion.56) | copy-start | bytes 1540
  15.3 10.3 %copy-start.26 = (pred[128]{0:T(512)(128)(4,1)}, pred[128]{0:T(512)(128)(4,1)S(1)}, u32[]{:S(2)}) copy-start(pred[128]{0:T(512)(128)(4,1)S(1)} %iota_compare_fusion.27) | copy-start | bytes 388
  25.6 0.7 copy-start.28
  32.3 1.0 copy-start.12
  32.3 1.0 copy-start.16
  34.9 1.7 %copy-start.2 = (f32[3,16,32,128]{3,2,1,0:T(8,128)S(1)}, f32[3,16,32,128]{3,2,1,0:T(8,128)}, u32[]{:S(2)}) copy-start(f32[3,16,32,128]{3,2,1,0:T(8,128)} %param.12) | copy-start | bytes 2359300
  36.6 0.7 copy-start.3
  36.6 0.8 copy-start.5
  41.8 12.6 %collective-permute-start.3 = (f32[2,16,32]{2,1,0:T(8,128)S(1)}, f32[2,16,32]{2,1,0:T(8,128)S(1)}, u32[]{:S(2)}, u32[]{:S(2)}) collective-permute-start(f32[2,16,32]{2,1,0:T(8,128)S(1)} %pad_maximum_fusion.2), channel_id=1, source_target_pairs={{0,16},{16,32},{32,48},{48,64},{64,80},{80,96},{96,112},{1,17},{17... | collective-permute-start | bytes 12296 | tf_op jit(solution)/shard_map/ppermute | solution.py:15
  48.9 7.3 %collective-permute-start.5 = (f32[2,16,128]{2,1,0:T(8,128)}, f32[2,16,128]{2,1,0:T(8,128)}, u32[]{:S(2)}, u32[]{:S(2)}) collective-permute-start(f32[2,16,128]{2,1,0:T(8,128)} %pad_maximum_fusion.3), channel_id=1, source_target_pairs={{0,128},{128,256},{256,384},{1,129},{129,257},{257,385},{2,130},{1... | collective-permute-start | bytes 49160 | tf_op jit(solution)/shard_map/ppermute | solution.py:15
  52.5 6.3 %collective-permute-start.4 = (f32[2,32,128]{2,1,0:T(8,128)S(1)}, f32[2,32,128]{2,1,0:T(8,128)S(1)}, u32[]{:S(2)}, u32[]{:S(2)}) collective-permute-start(f32[2,32,128]{2,1,0:T(8,128)S(1)} %slice_bitcast_fusion.30), channel_id=1, source_target_pairs={{0,1},{1,2},{2,3},{3,4},{4,5},{5,6},{6,7},{7,8},{8,9},{9,10},{10,1... | collective-permute-start | bytes 98312 | tf_op jit(solution)/shard_map/ppermute | solution.py:15
  58.8 1.8 %copy-start.7 = (f32[16,32,128]{2,1,0:T(8,128)S(1)}, f32[16,32,128]{2,1,0:T(8,128)}, u32[]{:S(2)}) copy-start(f32[16,32,128]{2,1,0:T(8,128)} %broadcast_multiply_fusion) | copy-start | bytes 786436
  63.6 1.7 %copy-start.15 = (s32[128]{0:T(128)S(1)}, s32[128]{0:T(128)}, u32[]{:S(2)}) copy-start(s32[128]{0:T(128)} %copy-done.14) | copy-start | bytes 1540
  65.3 1.0 copy-start.19
  65.3 1.1 copy-start.21
  65.3 1.1 copy-start.23
  65.3 1.1 copy-start.25
  65.3 1.1 copy-start.27
  65.3 1.1 copy-start.29
  83.4 12.3 %collective-permute-start.8 = (f32[2,16,128]{2,1,0:T(8,128)S(1)}, f32[2,16,128]{2,1,0:T(8,128)S(1)}, u32[]{:S(2)}, u32[]{:S(2)}) collective-permute-start(f32[2,16,128]{2,1,0:T(8,128)S(1)} %pad_maximum_fusion.5), channel_id=1, source_target_pairs={{128,0},{256,128},{384,256},{129,1},{257,129},{385,257},{130,2},{2... | collective-permute-start | bytes 49160 | tf_op jit(solution)/shard_map/ppermute | solution.py:15
  85.7 8.3 %collective-permute-start.6 = (f32[2,16,32]{2,1,0:T(8,128)S(1)}, f32[2,16,32]{2,1,0:T(8,128)S(1)}, u32[]{:S(2)}, u32[]{:S(2)}) collective-permute-start(f32[2,16,32]{2,1,0:T(8,128)S(1)} %pad_maximum_fusion.4), channel_id=1, source_target_pairs={{16,0},{32,16},{48,32},{64,48},{80,64},{96,80},{112,96},{17,1},{33... | collective-permute-start | bytes 12296 | tf_op jit(solution)/shard_map/ppermute | solution.py:15
  87.6 8.1 %collective-permute-start.7 = (f32[2,32,128]{2,1,0:T(8,128)S(1)}, f32[2,32,128]{2,1,0:T(8,128)S(1)}, u32[]{:S(2)}, u32[]{:S(2)}) collective-permute-start(f32[2,32,128]{2,1,0:T(8,128)S(1)} %slice_bitcast_fusion.29), channel_id=1, source_target_pairs={{1,0},{2,1},{3,2},{4,3},{5,4},{6,5},{7,6},{8,7},{9,8},{10,9},{11,1... | collective-permute-start | bytes 98312 | tf_op jit(solution)/shard_map/ppermute | solution.py:15
  90.8 4.9 %copy-start.9 = (f32[1,16,32,127]{3,2,1,0:T(8,128)S(1)}, f32[1,16,32,127]{3,2,1,0:T(8,128)}, u32[]{:S(2)}) copy-start(f32[1,16,32,127]{3,2,1,0:T(8,128)} %slice_bitcast_fusion.4) | copy-start | bytes 780292
  90.8 4.9 %copy-start.10 = (f32[1,16,31,128]{3,2,1,0:T(8,128)S(1)}, f32[1,16,31,128]{3,2,1,0:T(8,128)}, u32[]{:S(2)}) copy-start(f32[1,16,31,128]{3,2,1,0:T(8,128)} %slice_bitcast_fusion.5) | copy-start | bytes 761860
  90.8 4.9 %copy-start.11 = (f32[1,16,31,128]{3,2,1,0:T(8,128)S(1)}, f32[1,16,31,128]{3,2,1,0:T(8,128)}, u32[]{:S(2)}) copy-start(f32[1,16,31,128]{3,2,1,0:T(8,128)} %slice_bitcast_fusion.6) | copy-start | bytes 761860
  95.8 1.7 %copy-start.4 = (f32[1,16,32,128]{3,2,1,0:T(8,128)S(1)}, f32[1,16,32,128]{3,2,1,0:T(8,128)}, u32[]{:S(2)}) copy-start(f32[1,16,32,128]{3,2,1,0:T(8,128)} %copy-done.3) | copy-start | bytes 786436
  95.8 1.7 %copy-start.6 = (f32[1,16,32,128]{3,2,1,0:T(8,128)S(1)}, f32[1,16,32,128]{3,2,1,0:T(8,128)}, u32[]{:S(2)}) copy-start(f32[1,16,32,128]{3,2,1,0:T(8,128)} %copy-done.5) | copy-start | bytes 786436
  97.7 18.3 %copy-start.1 = (f32[3,16,32,128]{3,2,1,0:T(8,128)}, f32[3,16,32,128]{3,2,1,0:T(8,128)S(1)}, u32[]{:S(2)}) copy-start(f32[3,16,32,128]{3,2,1,0:T(8,128)S(1)} %fusion.21) | copy-start | bytes 2359300
  100.0 12.7 %collective-permute-start.9 = (f32[2,16,32]{2,1,0:T(8,128)S(1)}, f32[2,16,32]{2,1,0:T(8,128)S(1)}, u32[]{:S(2)}, u32[]{:S(2)}) collective-permute-start(f32[2,16,32]{2,1,0:T(8,128)S(1)} %pad_maximum_fusion.6), channel_id=1, source_target_pairs={{0,16},{16,32},{32,48},{48,64},{64,80},{80,96},{96,112},{1,17},{17... | collective-permute-start | bytes 12296 | tf_op jit(solution)/shard_map/ppermute | solution.py:15
  105.6 8.8 %collective-permute-start.11 = (f32[2,16,128]{2,1,0:T(8,128)S(1)}, f32[2,16,128]{2,1,0:T(8,128)S(1)}, u32[]{:S(2)}, u32[]{:S(2)}) collective-permute-start(f32[2,16,128]{2,1,0:T(8,128)S(1)} %pad_maximum_fusion.7), channel_id=1, source_target_pairs={{0,128},{128,256},{256,384},{1,129},{129,257},{257,385},{2,130},{1... | collective-permute-start | bytes 49160 | tf_op jit(solution)/shard_map/ppermute | solution.py:15
  110.1 5.9 %collective-permute-start.10 = (f32[2,32,128]{2,1,0:T(8,128)S(1)}, f32[2,32,128]{2,1,0:T(8,128)S(1)}, u32[]{:S(2)}, u32[]{:S(2)}) collective-permute-start(f32[2,32,128]{2,1,0:T(8,128)S(1)} %slice_bitcast_fusion.28), channel_id=1, source_target_pairs={{0,1},{1,2},{2,3},{3,4},{4,5},{5,6},{6,7},{7,8},{8,9},{9,10},{10,1... | collective-permute-start | bytes 98312 | tf_op jit(solution)/shard_map/ppermute | solution.py:15
  116.0 1.6 %copy-start.8 = (f32[16,32,128]{2,1,0:T(8,128)S(1)}, f32[16,32,128]{2,1,0:T(8,128)}, u32[]{:S(2)}) copy-start(f32[16,32,128]{2,1,0:T(8,128)} %broadcast_multiply_fusion) | copy-start | bytes 786436
where the time goes:
time: 119 us
  starting transfers between devices  40.3 us (34%)
  matrix products  34.4 us (29%)
  local copies, waits for them, and re-layouts  26.1 us (22%)
  other arithmetic  11.1 us (9%)
  waiting for transfers between devices  4.77 us (4%)
  between operations  2.14 us (2%)
    ppermute x12, starting transfers between devices, passed_along(): lax.ppermute(value, axis, [(source, source + steps) for source in range(f...  40.3 us
    dot_general x2, matrix products, pick_cells(): jnp.einsum('bkc,abc->abk', order, rows, precision=lax.Precision.HIGHEST)  20.1 us
    dot_general x2, matrix products, place_cells(): jnp.einsum('bkc,abk->abc', order, values, precision=lax.Precision.HIGHEST)  11.9 us
    concatenate x16, local copies, waits for them, and re-layouts, falling(): return values - jnp.concatenate([plane, lower], along)  7.2 us
    concatenate x14, local copies, waits for them, and re-layouts, rising(): return jnp.concatenate([upper, plane], along) - values  7 us
    ppermute x12, waiting for transfers between devices, passed_along(): lax.ppermute(value, axis, [(source, source + steps) for source in range(f...  4.77 us
    unnamed x62, local copies, waits for them, and re-layouts  4.25 us
    sub x2, other arithmetic, curl_backward(): falling(field[2], plane_y[1][:, :, None], 2)  3.46 us
  transfers between devices with their start and end apart: 12, of which 3 were waited for; matrix products, arithmetic and copies ran while one was open for 26% of the time, Pallas kernels for 0%

commit v1 on v0

v1 whole, which is shorter than its diff:
```python
import functools

import jax
import jax.numpy as jnp
from jax import lax
from jax.experimental import pallas as pl
from jax.experimental.pallas import tpu as pltpu
from jax.sharding import PartitionSpec as P

STEPS = 2
TIME_STEP = 0.5
VMEM_LIMIT = 48 * 1024 * 1024


def passed_along(value, axis, steps):
    count = lax.axis_size(axis)
    first, last = (max(0, -steps), min(count, count - steps))
    return lax.ppermute(value, axis, [(source, source + steps) for source in range(first, last)])


def rising(values, plane, along):
    length = values.shape[along]
    upper = lax.slice_in_dim(values, 1, length, axis=along)
    return jnp.concatenate([upper, plane], along) - values


def falling(values, plane, along):
    length = values.shape[along]
    lower = lax.slice_in_dim(values, 0, length - 1, axis=along)
    return values - jnp.concatenate([plane, lower], along)


def curl(step_of, field, plane_x, plane_y, plane_z):
    curl_x = step_of(field[2], plane_y[1][:, :, None], 2) - step_of(field[1], plane_z[1][None], 0)
    curl_y = step_of(field[0], plane_z[0][None], 0) - step_of(field[2], plane_x[1][:, None, :], 1)
    curl_z = step_of(field[1], plane_x[0][:, None, :], 1) - step_of(
        field[0], plane_y[0][:, :, None], 2
    )
    return jnp.stack([curl_x, curl_y, curl_z])


def e_planes(e_field):
    first_x = jnp.stack([e_field[1][:, 0, :], e_field[2][:, 0, :]])
    first_y = jnp.stack([e_field[0][:, :, 0], e_field[2][:, :, 0]])
    first_z = e_field[0:2, 0]
    got_x = passed_along(first_x, "gx", -1)
    got_y = passed_along(first_y, "gy", -1)
    got_z = passed_along(first_z, "gz", -1)
    return (got_x, got_y, got_z)


def h_planes(h_field):
    last_x = jnp.stack([h_field[1][:, -1, :], h_field[2][:, -1, :]])
    last_y = jnp.stack([h_field[0][:, :, -1], h_field[2][:, :, -1]])
    last_z = h_field[0:2, -1]
    got_x = passed_along(last_x, "gx", 1)
    got_y = passed_along(last_y, "gy", 1)
    got_z = passed_along(last_z, "gz", 1)
    return (got_x, got_y, got_z)


def as_column(row_ref, eye):
    return jnp.sum(jnp.where(eye, row_ref[...], 0.0), axis=1, keepdims=True)


def advance_blocks(e, cells, inverse, runs, count, decay, restore, drive, pol, cur, pol_out, cur_out, rows, j_rows):
    slots, width = cells.shape
    for b in range(slots):
        run = runs[0, b]
        for comp in range(3):
            rows[comp, pl.ds(b, 1), :] = e[comp, pl.ds(run, 1), :]
    j_rows[...] = jnp.zeros_like(j_rows)
    offsets = lax.bitwise_and(cells[...], width - 1)
    down = lax.broadcasted_iota(jnp.int32, (slots, width), 0)
    across = lax.broadcasted_iota(jnp.int32, (slots, width), 1)
    eye = down == across
    live = down < count[0]
    decay_c, restore_c, drive_c = (as_column(ref, eye) for ref in (decay, restore, drive))
    back = inverse[...]
    for comp in range(3):
        at_cells = jnp.take_along_axis(rows[comp], offsets, axis=1)
        held, polar = cur[comp], pol[comp]
        new = jnp.where(live, decay_c * held - restore_c * polar + drive_c * at_cells, held)
        cur_out[comp] = new
        pol_out[comp] = jnp.where(live, polar + TIME_STEP * new, polar)
        rows[comp] = jnp.take_along_axis(jnp.where(live, new, 0.0), back, axis=1)
    for b in range(slots):
        run = runs[0, b]
        for comp in range(3):
            j_rows[comp, pl.ds(run, 1), :] = rows[comp, pl.ds(b, 1), :]


def first_blocks(
    e, material, inv_perm, cells, count, decay, restore, drive, pol, cur,
    pol_out, cur_out, a_out, scale_out, inverse_out, runs_out, rows, j_rows, run_row, runs, sem,
):
    slots, width = cells.shape
    down = lax.broadcasted_iota(jnp.int32, (slots, width), 0)
    across = lax.broadcasted_iota(jnp.int32, (slots, width), 1)
    run_of = lax.shift_right_logical(cells[...], width.bit_length() - 1)
    run_row[...] = jnp.sum(jnp.where(down == across, run_of, 0), axis=0, keepdims=True)
    runs_out[...] = run_row[...]
    copy = pltpu.make_async_copy(run_row, runs, sem)
    copy.start()
    offsets = lax.bitwise_and(cells[...], width - 1)
    for block in range(slots // 8):
        part = offsets[block * 8 : block * 8 + 8]
        lanes = across[:8]
        found = jnp.zeros((8, width), jnp.int32)
        for k in range(width):
            found = jnp.where(part[:, k : k + 1] == lanes, k, found)
        inverse_out[block * 8 : block * 8 + 8, :] = found
    table = jnp.zeros((8, width), jnp.float32)
    for kind in range(inv_perm.shape[0]):
        table = jnp.where(across[:8] == kind, TIME_STEP * inv_perm[kind], table)
    for row in range(0, material.shape[0], 8):
        scale_out[row : row + 8, :] = jnp.take_along_axis(table, material[row : row + 8, :], axis=1)
    copy.wait()
    advance_blocks(e, cells, inverse_out, runs, count, decay, restore, drive, pol, cur, pol_out, cur_out, rows, j_rows)
    for comp in range(3):
        a_out[comp] = e[comp] - scale_out[...] * j_rows[comp]


def next_blocks(
    e, scale, inverse, runs, cells, count, decay, restore, drive, pol, cur,
    pol_out, cur_out, a_out, rows, j_rows,
):
    advance_blocks(e, cells, inverse, runs, count, decay, restore, drive, pol, cur, pol_out, cur_out, rows, j_rows)
    for comp in range(3):
        a_out[comp] = e[comp] - scale[...] * j_rows[comp]


def on_device(
    e_field, h_field, material, inv_permittivity, block_cells, block_count,
    block_decay, block_restore, block_drive, polarization, current,
):
    slots, width = block_cells.shape
    shape = e_field.shape
    runs_all = shape[1] * shape[2] * shape[3] // width
    f32, i32 = jnp.float32, jnp.int32
    vmem, smem = pl.BlockSpec(memory_space=pltpu.VMEM), pl.BlockSpec(memory_space=pltpu.SMEM)
    flat = (3, runs_all, width)
    coefficients = [v.reshape(1, slots) for v in (block_decay, block_restore, block_drive)]
    blocks = jax.ShapeDtypeStruct((3, slots, width), f32)
    params = pltpu.CompilerParams(vmem_limit_bytes=VMEM_LIMIT)
    scratch = [pltpu.VMEM((3, slots, width), f32), pltpu.VMEM(flat, f32)]
    pol1, cur1, a1, scale, inverse, runs = pl.pallas_call(
        first_blocks,
        out_shape=[
            blocks, blocks, jax.ShapeDtypeStruct(flat, f32), jax.ShapeDtypeStruct((runs_all, width), f32),
            jax.ShapeDtypeStruct((slots, width), i32), jax.ShapeDtypeStruct((1, slots), i32),
        ],
        in_specs=[vmem, vmem, smem, vmem, smem, vmem, vmem, vmem, vmem, vmem],
        out_specs=[vmem] * 6,
        scratch_shapes=scratch + [pltpu.VMEM((1, slots), i32), pltpu.SMEM((1, slots), i32), pltpu.SemaphoreType.DMA],
        compiler_params=params,
        name="first_blocks",
    )(
        e_field.reshape(flat), material.reshape(runs_all, width), inv_permittivity, block_cells, block_count,
        *coefficients, polarization, current,
    )
    scale_cells = scale.reshape(shape[1:])
    got = e_planes(e_field)
    h_field = h_field - TIME_STEP * curl(rising, e_field, *got)
    got_h = h_planes(h_field)
    e_field = a1.reshape(shape) + scale_cells * curl(falling, h_field, *got_h)
    pol2, cur2, a2 = pl.pallas_call(
        next_blocks,
        out_shape=[blocks, blocks, jax.ShapeDtypeStruct(flat, f32)],
        in_specs=[vmem, vmem, vmem, smem, vmem, smem, vmem, vmem, vmem, vmem, vmem],
        out_specs=[vmem] * 3,
        scratch_shapes=scratch,
        compiler_params=params,
        name="next_blocks",
    )(e_field.reshape(flat), scale, inverse, runs, block_cells, block_count, *coefficients, pol1, cur1)
    got = e_planes(e_field)
    h_field = h_field - TIME_STEP * curl(rising, e_field, *got)
    got_h = h_planes(h_field)
    e_field = a2.reshape(shape) + scale_cells * curl(falling, h_field, *got_h)
    return (e_field, h_field, pol2, cur2)


def solution(mesh):
    grid = P(None, "gz", "gx", "gy")
    rows = ("gx", "gy", "gz")
    return jax.shard_map(
        on_device,
        mesh=mesh,
        in_specs=(
            grid, grid, P("gz", "gx", "gy"), P(), P(rows, None), P(rows), P(rows), P(rows), P(rows),
            P(None, rows, None), P(None, rows, None),
        ),
        out_specs=(grid, grid, P(None, rows, None), P(None, rows, None)),
        check_vma=False,
    )
```

time: 119 us -> 81.7 us (0.69)
  the two profiles are of different devices: /device:TPU:409 before, /device:TPU:102 now
where the time goes in v1:
time: 81.7 us; the launch traced here: 81.1 us
  starting transfers between devices  35.6 us (44%)
  local copies, waits for them, and re-layouts  17.6 us (22%)
  waiting for transfers between devices  10.2 us (12%)
  other arithmetic  8.21 us (10%)
  Pallas kernels  7.46 us (9%)
  between operations  2 us (2%)
    ppermute x12, starting transfers between devices, passed_along(): lax.ppermute(value, axis, [(source, source + steps) for source in range(f...  35.6 us
    ppermute x12, waiting for transfers between devices, passed_along(): lax.ppermute(value, axis, [(source, source + steps) for source in range(f...  10.2 us
    sub x4, other arithmetic, curl(): step_of(field[2], plane_y[1][:, :, None], 2)  6.3 us
    concatenate x14, local copies, waits for them, and re-layouts, rising(): return jnp.concatenate([upper, plane], along) - values  6.28 us
    pallas_call x1, Pallas kernels, on_device(): pl.pallas_call(first_blocks, out_shape=[blocks, blocks, jax.ShapeDtypeStr...  5.57 us
    concatenate x16, local copies, waits for them, and re-layouts, falling(): return values - jnp.concatenate([plane, lower], along)  2.98 us
    pallas_call x1, Pallas kernels, on_device(): pl.pallas_call(next_blocks, out_shape=[blocks, blocks, jax.ShapeDtypeStru...  1.89 us
    slice x2, local copies, waits for them, and re-layouts, falling(): lower = lax.slice_in_dim(values, 0, length - 1, axis=along)  1.72 us
  transfers between devices with their start and end apart: 12, of which 2 were waited for; matrix products, arithmetic and copies ran while one was open for 10% of the time, Pallas kernels for 9%

profile of v1, /device:TPU:102, one launch (start us, length us, event | category | flops | bytes accessed | tf_op | source)
XLA Modules:
  0.0 81.1 jit_solution(15200610369107621321)
XLA Ops:
  0.6 0.8 slice_bitcast_fusion.31
  1.4 2.0 %collective-permute-start.1 = (f32[2,32,128]{2,1,0:T(8,128)S(1)}, f32[2,32,128]{2,1,0:T(8,128)S(1)}, u32[]{:S(2)}, u32[]{:S(2)}) collective-permute-start(f32[2,32,128]{2,1,0:T(8,128)S(1)} %slice_bitcast_fusion.31), channel_id=1, source_target_pairs={{1,0},{2,1},{3,2},{4,3},{5,4},{6,5},{7,6},{8,7},{9,8},{10,9},{11,1... | collective-permute-start | bytes 98312 | tf_op jit(solution)/shard_map/ppermute | solution.py:18
  3.4 1.2 %slice_bitcast_fusion.26 = (f32[16,32,128]{2,1,0:T(8,128)S(1)}, f32[16,32,128]{2,1,0:T(8,128)S(1)}, f32[16,32,128]{2,1,0:T(8,128)S(1)}) fusion(f32[3,16,32,128]{3,2,1,0:T(8,128)} %param.11), kind=kLoop, calls=%fused_computation.80 | loop fusion | bytes 1572864 | tf_op jit(solution)/shard_map/squeeze | solution.py:44
  4.6 0.2 slice_reduce_fusion.6
  4.8 5.8 %collective-permute-start = (f32[2,16,32]{2,1,0:T(8,128)S(1)}, f32[2,16,32]{2,1,0:T(8,128)S(1)}, u32[]{:S(2)}, u32[]{:S(2)}) collective-permute-start(f32[2,16,32]{2,1,0:T(8,128)S(1)} %pad_maximum_fusion), channel_id=1, source_target_pairs={{16,0},{32,16},{48,32},{64,48},{80,64},{96,80},{112,96},{17,1},{33... | collective-permute-start | bytes 12296 | tf_op jit(solution)/shard_map/ppermute | solution.py:18
  10.6 0.0 copy-start
  10.6 2.1 %collective-permute-start.2 = (f32[2,16,128]{2,1,0:T(8,128)S(1)}, f32[2,16,128]{2,1,0:T(8,128)S(1)}, u32[]{:S(2)}, u32[]{:S(2)}) collective-permute-start(f32[2,16,128]{2,1,0:T(8,128)S(1)} %pad_maximum_fusion.1), channel_id=1, source_target_pairs={{128,0},{256,128},{384,256},{129,1},{257,129},{385,257},{130,2},{2... | collective-permute-start | bytes 49160 | tf_op jit(solution)/shard_map/ppermute | solution.py:18
  12.7 0.9 %slice_bitcast_fusion.12 = (f32[1,16,32,127]{3,2,1,0:T(8,128)S(1)}, f32[1,16,32,127]{3,2,1,0:T(8,128)}) fusion(f32[16,32,128]{2,1,0:T(8,128)S(1)} %get-tuple-element.51, f32[16,32,128]{2,1,0:T(8,128)S(1)} %get-tuple-element.53), kind=kLoop, calls=%fused_computation.28 | loop fusion | bytes 1040384 | tf_op jit(solution)/shard_map/concatenate | solution.py:24
  13.6 0.8 %slice_bitcast_fusion.13 = (f32[1,16,31,128]{3,2,1,0:T(8,128)}, f32[1,16,31,128]{3,2,1,0:T(8,128)}) fusion(f32[16,32,128]{2,1,0:T(8,128)S(1)} %get-tuple-element.52, f32[16,32,128]{2,1,0:T(8,128)S(1)} %get-tuple-element.53), kind=kLoop, calls=%fused_computation.29 | loop fusion | bytes 1015808 | tf_op jit(solution)/shard_map/concatenate | solution.py:24
  14.4 0.0 copy-start.4
  14.5 0.8 %fusion.20 = (f32[1,15,32,128]{3,2,1,0:T(8,128)}, f32[1,15,32,128]{3,2,1,0:T(8,128)}) fusion(f32[3,16,32,128]{3,2,1,0:T(8,128)S(1)} %copy-done), kind=kLoop, calls=%fused_computation.113 | loop fusion | bytes 983040 | tf_op jit(solution)/shard_map/slice | solution.py:23
  15.9 0.0 copy-start.5
  16.0 0.6 copy-done.5
  16.6 0.0 copy-done.6
  16.6 0.0 copy-done.7
  16.6 5.6 %first_blocks.1 = (f32[3,128,128]{2,1,0:T(8,128)S(1)}, f32[3,128,128]{2,1,0:T(8,128)S(1)}, f32[3,512,128]{2,1,0:T(8,128)S(1)}, f32[512,128]{1,0:T(8,128)S(1)}, s...) custom-call(f32[3,512,128]{2,1,0:T(8,128)S(1)} %bitcast.157, s32[512,128]{1,0:T(8,128)S(1)} %bitcast.162, f32[8]{0:T(128)S(1)} %copy-done.8, ...), custom_call_target="tpu_custom_call" | custom-call | tf_op jit(solution)/shard_map/first_blocks/pallas_call | solution.py:147
  22.2 0.2 copy.133
  22.4 0.2 copy.138
  22.6 1.7 %fusion.5 = (f32[1,16,32,128]{3,2,1,0:T(8,128)S(1)}, f32[1,16,32,128]{3,2,1,0:T(8,128)S(1)}, f32[1,16,32,128]{3,2,1,0:T(8,128)S(1)}) fusion(f32[1,16,32,1]{3,2,1,0:T(8,128)S(1)} %copy.133, f32[1,16,32,127]{3,2,1,0:T(8,128)} %get-tuple-element.79, f32[1,1,32,128]{3,2,1,0:T(8,128)S(1)} %get-tuple-element.60, f32[1,15,32,128]{3,2,1,0:T(8,128)} %get-tuple-element.49, ...), kind=kLoop, calls=%fused_computation.35 | loop fusion | flops 983040 | bytes 3145728 | tf_op jit(solution)/shard_map/sub | solution.py:34
  24.3 0.2 fusion
  24.5 0.5 copy-done.12
  25.0 0.1 copy-done.14
  25.1 0.8 %fusion.19 = (f32[1,15,32,128]{3,2,1,0:T(8,128)}, f32[1,15,32,128]{3,2,1,0:T(8,128)}) fusion(f32[3,16,32,128]{3,2,1,0:T(8,128)S(1)} %fusion), kind=kLoop, calls=%fused_computation.112 | loop fusion | bytes 983040 | tf_op jit(solution)/shard_map/slice | solution.py:29
  25.9 0.1 slice_bitcast_fusion.23
  26.0 0.3 slice_reduce_fusion.5
  26.4 0.3 slice_reduce_fusion.4
  26.6 0.7 slice_bitcast_fusion.11
  27.4 5.0 %collective-permute-start.4 = (f32[2,32,128]{2,1,0:T(8,128)S(1)}, f32[2,32,128]{2,1,0:T(8,128)S(1)}, u32[]{:S(2)}, u32[]{:S(2)}) collective-permute-start(f32[2,32,128]{2,1,0:T(8,128)S(1)} %slice_bitcast_fusion.30), channel_id=1, source_target_pairs={{0,1},{1,2},{2,3},{3,4},{4,5},{5,6},{6,7},{7,8},{8,9},{9,10},{10,1... | collective-permute-start | bytes 98312 | tf_op jit(solution)/shard_map/ppermute | solution.py:18
  32.4 1.9 %collective-permute-start.3 = (f32[2,16,32]{2,1,0:T(8,128)S(1)}, f32[2,16,32]{2,1,0:T(8,128)S(1)}, u32[]{:S(2)}, u32[]{:S(2)}) collective-permute-start(f32[2,16,32]{2,1,0:T(8,128)S(1)} %pad_maximum_fusion.2), channel_id=1, source_target_pairs={{0,16},{16,32},{32,48},{48,64},{64,80},{80,96},{96,112},{1,17},{17... | collective-permute-start | bytes 12296 | tf_op jit(solution)/shard_map/ppermute | solution.py:18
  34.3 2.1 %collective-permute-start.5 = (f32[2,16,128]{2,1,0:T(8,128)S(1)}, f32[2,16,128]{2,1,0:T(8,128)S(1)}, u32[]{:S(2)}, u32[]{:S(2)}) collective-permute-start(f32[2,16,128]{2,1,0:T(8,128)S(1)} %pad_maximum_fusion.3), channel_id=1, source_target_pairs={{0,128},{128,256},{256,384},{1,129},{129,257},{257,385},{2,130},{1... | collective-permute-start | bytes 49160 | tf_op jit(solution)/shard_map/ppermute | solution.py:18
  36.5 5.2 %collective-permute-done.3 = f32[2,16,32]{2,1,0:T(8,128)S(1)} collective-permute-done((f32[2,16,32]{2,1,0:T(8,128)S(1)}, f32[2,16,32]{2,1,0:T(8,128)S(1)}, u32[]{:S(2)}, u32[]{:S(2)}) %collective-permute-start.3) | collective-permute-done | bytes 4128 | tf_op jit(solution)/shard_map/ppermute | solution.py:18
  41.7 0.9 %copy.139 = f32[1,16,32,1]{3,2,1,0:T(8,128)} copy(f32[1,16,32,1]{2,1,3,0:T(8,128)S(1)} %get-tuple-element.70) | data formatting | bytes 4096 | tf_op jit(solution)/shard_map/concatenate | solution.py:30
  42.5 0.9 %copy.143 = f32[1,16,32,1]{3,2,1,0:T(8,128)} copy(f32[1,16,32,1]{2,1,3,0:T(8,128)S(1)} %get-tuple-element.71) | data formatting | bytes 4096 | tf_op jit(solution)/shard_map/concatenate | solution.py:30
  43.4 1.6 %fusion.8 = (f32[1,16,32,128]{3,2,1,0:T(8,128)S(1)}, f32[1,16,32,128]{3,2,1,0:T(8,128)S(1)}, f32[1,16,32,128]{3,2,1,0:T(8,128)S(1)}) fusion(f32[1,16,32,127]{3,2,1,0:T(8,128)} %slice_bitcast_fusion.11, f32[1,16,32,1]{3,2,1,0:T(8,128)} %copy.139, f32[1,15,32,128]{3,2,1,0:T(8,128)} %get-tuple-element.41, f32[1,1,32,128]{3,2,1,0:T(8,128)S(1)} %get-tuple-element.58, ...), kind=kLoop, calls=%fused_computation.44 | loop fusion | flops 983040 | bytes 3145728 | tf_op jit(solution)/shard_map/sub | solution.py:34
  45.0 0.2 fusion.2
  45.2 0.8 %fusion.18 = (f32[1,15,32,128]{3,2,1,0:T(8,128)}, f32[1,15,32,128]{3,2,1,0:T(8,128)}) fusion(f32[3,16,32,128]{3,2,1,0:T(8,128)S(1)} %fusion.2), kind=kLoop, calls=%fused_computation.111 | loop fusion | bytes 983040 | tf_op jit(solution)/shard_map/slice | solution.py:23
  46.1 0.1 slice_bitcast_fusion.20
  46.1 0.1 slice_reduce_fusion.3
  46.3 0.9 %slice_bitcast_fusion.4 = f32[1,16,32,127]{3,2,1,0:T(8,128)} fusion(f32[16,32,128]{2,1,0:T(8,128)S(1)} %get-tuple-element.35), kind=kLoop, calls=%fused_computation.16 | loop fusion | bytes 520192 | tf_op jit(solution)/shard_map/concatenate | solution.py:24
  47.1 0.7 slice_bitcast_fusion.5
  47.9 0.1 slice_reduce_fusion.2
  48.0 0.7 slice_bitcast_fusion.6
  48.8 0.1 slice_bitcast_fusion.7
  48.9 1.9 %collective-permute-start.7 = (f32[2,32,128]{2,1,0:T(8,128)S(1)}, f32[2,32,128]{2,1,0:T(8,128)S(1)}, u32[]{:S(2)}, u32[]{:S(2)}) collective-permute-start(f32[2,32,128]{2,1,0:T(8,128)S(1)} %slice_bitcast_fusion.29), channel_id=1, source_target_pairs={{1,0},{2,1},{3,2},{4,3},{5,4},{6,5},{7,6},{8,7},{9,8},{10,9},{11,1... | collective-permute-start | bytes 98312 | tf_op jit(solution)/shard_map/ppermute | solution.py:18
  50.8 3.5 %collective-permute-start.6 = (f32[2,16,32]{2,1,0:T(8,128)S(1)}, f32[2,16,32]{2,1,0:T(8,128)S(1)}, u32[]{:S(2)}, u32[]{:S(2)}) collective-permute-start(f32[2,16,32]{2,1,0:T(8,128)S(1)} %pad_maximum_fusion.4), channel_id=1, source_target_pairs={{16,0},{32,16},{48,32},{64,48},{80,64},{96,80},{112,96},{17,1},{33... | collective-permute-start | bytes 12296 | tf_op jit(solution)/shard_map/ppermute | solution.py:18
  54.4 1.9 %collective-permute-start.8 = (f32[2,16,128]{2,1,0:T(8,128)S(1)}, f32[2,16,128]{2,1,0:T(8,128)S(1)}, u32[]{:S(2)}, u32[]{:S(2)}) collective-permute-start(f32[2,16,128]{2,1,0:T(8,128)S(1)} %pad_maximum_fusion.5), channel_id=1, source_target_pairs={{128,0},{256,128},{384,256},{129,1},{257,129},{385,257},{130,2},{2... | collective-permute-start | bytes 49160 | tf_op jit(solution)/shard_map/ppermute | solution.py:18
  56.3 0.2 fusion.1.e
  56.5 1.9 %next_blocks.1 = (f32[3,128,128]{2,1,0:T(8,128)}, f32[3,128,128]{2,1,0:T(8,128)}, f32[3,512,128]{2,1,0:T(8,128)S(1)}) custom-call(f32[3,512,128]{2,1,0:T(8,128)S(1)} %fusion.1.e, f32[512,128]{1,0:T(8,128)S(1)} %get-tuple-element.14.scale, s32[128,128]{1,0:T(8,128)S(1)} %get-tuple-element.15.inverse, s32[1,128]{1,0:T(1,128)S(1)} %get-tuple-element.16.runs, ...), custom_call_target="tpu_custom_call" | custom-call | tf_op jit(solution)/shard_map/next_blocks/pallas_call | solution.py:167
  58.4 0.9 %copy.144 = f32[1,16,32,1]{3,2,1,0:T(8,128)} copy(f32[1,16,32,1]{2,1,3,0:T(8,128)S(1)} %get-tuple-element.66) | data formatting | bytes 4096 | tf_op jit(solution)/shard_map/concatenate | solution.py:24
  59.3 0.9 %copy.148 = f32[1,16,32,1]{3,2,1,0:T(8,128)} copy(f32[1,16,32,1]{2,1,3,0:T(8,128)S(1)} %get-tuple-element.67) | data formatting | bytes 4096 | tf_op jit(solution)/shard_map/concatenate | solution.py:24
  60.2 1.7 %fusion.11 = (f32[1,16,32,128]{3,2,1,0:T(8,128)S(1)}, f32[1,16,32,128]{3,2,1,0:T(8,128)S(1)}, f32[1,16,32,128]{3,2,1,0:T(8,128)S(1)}) fusion(f32[1,16,32,1]{3,2,1,0:T(8,128)} %copy.144, f32[1,16,32,127]{3,2,1,0:T(8,128)S(1)} %slice_bitcast_fusion.7, f32[1,1,32,128]{3,2,1,0:T(8,128)S(1)} %get-tuple-element.56, f32[1,15,32,128]{3,2,1,0:T(8,128)} %get-tuple-element.33, ...), kind=kLoop, calls=%fused_computation.53 | loop fusion | flops 983040 | bytes 3145728 | tf_op jit(solution)/shard_map/sub | solution.py:34
  61.9 0.3 fusion.3
  62.2 0.9 %fusion.17 = (f32[1,15,32,128]{3,2,1,0:T(8,128)}, f32[1,15,32,128]{3,2,1,0:T(8,128)}) fusion(f32[3,16,32,128]{3,2,1,0:T(8,128)S(1)} %fusion.3), kind=kLoop, calls=%fused_computation.110 | loop fusion | bytes 983040 | tf_op jit(solution)/shard_map/slice | solution.py:29
  63.1 0.1 slice_bitcast_fusion.17
  63.1 0.3 slice_reduce_fusion.1
  63.5 0.3 slice_reduce_fusion
  63.8 5.1 %collective-permute-start.10 = (f32[2,32,128]{2,1,0:T(8,128)S(1)}, f32[2,32,128]{2,1,0:T(8,128)S(1)}, u32[]{:S(2)}, u32[]{:S(2)}) collective-permute-start(f32[2,32,128]{2,1,0:T(8,128)S(1)} %slice_bitcast_fusion.28), channel_id=1, source_target_pairs={{0,1},{1,2},{2,3},{3,4},{4,5},{5,6},{6,7},{7,8},{8,9},{9,10},{10,1... | collective-permute-start | bytes 98312 | tf_op jit(solution)/shard_map/ppermute | solution.py:18
  69.0 2.3 %collective-permute-start.9 = (f32[2,16,32]{2,1,0:T(8,128)S(1)}, f32[2,16,32]{2,1,0:T(8,128)S(1)}, u32[]{:S(2)}, u32[]{:S(2)}) collective-permute-start(f32[2,16,32]{2,1,0:T(8,128)S(1)} %pad_maximum_fusion.6), channel_id=1, source_target_pairs={{0,16},{16,32},{32,48},{48,64},{64,80},{80,96},{96,112},{1,17},{17... | collective-permute-start | bytes 12296 | tf_op jit(solution)/shard_map/ppermute | solution.py:18
  71.3 1.9 %collective-permute-start.11 = (f32[2,16,128]{2,1,0:T(8,128)S(1)}, f32[2,16,128]{2,1,0:T(8,128)S(1)}, u32[]{:S(2)}, u32[]{:S(2)}) collective-permute-start(f32[2,16,128]{2,1,0:T(8,128)S(1)} %pad_maximum_fusion.7), channel_id=1, source_target_pairs={{0,128},{128,256},{256,384},{1,129},{129,257},{257,385},{2,130},{1... | collective-permute-start | bytes 49160 | tf_op jit(solution)/shard_map/ppermute | solution.py:18
  73.2 5.0 %collective-permute-done.9 = f32[2,16,32]{2,1,0:T(8,128)S(1)} collective-permute-done((f32[2,16,32]{2,1,0:T(8,128)S(1)}, f32[2,16,32]{2,1,0:T(8,128)S(1)}, u32[]{:S(2)}, u32[]{:S(2)}) %collective-permute-start.9) | collective-permute-done | bytes 4128 | tf_op jit(solution)/shard_map/ppermute | solution.py:18
  78.2 0.2 copy.149
  78.4 0.2 copy.153
  78.6 1.4 %fusion.14 = (f32[1,16,32,128]{3,2,1,0:T(8,128)S(1)}, f32[1,16,32,128]{3,2,1,0:T(8,128)S(1)}, f32[1,16,32,128]{3,2,1,0:T(8,128)S(1)}) fusion(f32[1,16,32,127]{3,2,1,0:T(8,128)S(1)} %slice_bitcast_fusion.3, f32[1,16,32,1]{3,2,1,0:T(8,128)S(1)} %copy.149, f32[1,15,32,128]{3,2,1,0:T(8,128)} %get-tuple-element.25, f32[1,1,32,128]{3,2,1,0:T(8,128)S(1)} %get-tuple-element.54, ...), kind=kLoop, calls=%fused_computation.62 | loop fusion | flops 983040 | bytes 3145728 | tf_op jit(solution)/shard_map/sub | solution.py:34
  80.0 1.1 %fusion.4 = f32[3,16,32,128]{3,2,1,0:T(8,128)} fusion(f32[3,16,32,128]{3,2,1,0:T(8,128)S(1)} %bitcast.161, f32[1,16,32,128]{3,2,1,0:T(8,128)S(1)} %get-tuple-element.24, f32[1,16,32,128]{3,2,1,0:T(8,128)S(1)} %get-tuple-element.23, f32[1,16,32,128]{3,2,1,0:T(8,128)S(1)} %get-tuple-element.22, f32[16,32,128]{2,1,0:T(8,128)S(1)} %bitcast.159), kind=kLoop, calls=%fused_computation.9 | loop fusion | flops 786432 | bytes 2621440 | tf_op jit(solution)/shard_map/add | solution.py:179
  (78 shorter events, 0.4 us)
Async XLA Ops:
  1.4 21.2 %collective-permute-start.1 = (f32[2,32,128]{2,1,0:T(8,128)S(1)}, f32[2,32,128]{2,1,0:T(8,128)S(1)}, u32[]{:S(2)}, u32[]{:S(2)}) collective-permute-start(f32[2,32,128]{2,1,0:T(8,128)S(1)} %slice_bitcast_fusion.31), channel_id=1, source_target_pairs={{1,0},{2,1},{3,2},{4,3},{5,4},{6,5},{7,6},{8,7},{9,8},{10,9},{11,1... | collective-permute-start | bytes 98312 | tf_op jit(solution)/shard_map/ppermute | solution.py:18
  4.8 17.4 %collective-permute-start = (f32[2,16,32]{2,1,0:T(8,128)S(1)}, f32[2,16,32]{2,1,0:T(8,128)S(1)}, u32[]{:S(2)}, u32[]{:S(2)}) collective-permute-start(f32[2,16,32]{2,1,0:T(8,128)S(1)} %pad_maximum_fusion), channel_id=1, source_target_pairs={{16,0},{32,16},{48,32},{64,48},{80,64},{96,80},{112,96},{17,1},{33... | collective-permute-start | bytes 12296 | tf_op jit(solution)/shard_map/ppermute | solution.py:18
  10.6 3.8 %copy-start = (f32[3,16,32,128]{3,2,1,0:T(8,128)S(1)}, f32[3,16,32,128]{3,2,1,0:T(8,128)}, u32[]{:S(2)}) copy-start(f32[3,16,32,128]{3,2,1,0:T(8,128)} %param.11) | copy-start | bytes 2359300
  10.6 11.9 %collective-permute-start.2 = (f32[2,16,128]{2,1,0:T(8,128)S(1)}, f32[2,16,128]{2,1,0:T(8,128)S(1)}, u32[]{:S(2)}, u32[]{:S(2)}) collective-permute-start(f32[2,16,128]{2,1,0:T(8,128)S(1)} %pad_maximum_fusion.1), channel_id=1, source_target_pairs={{128,0},{256,128},{384,256},{129,1},{257,129},{385,257},{130,2},{2... | collective-permute-start | bytes 49160 | tf_op jit(solution)/shard_map/ppermute | solution.py:18
  14.4 1.6 %copy-start.1 = (s32[128,128]{1,0:T(8,128)S(1)}, s32[128,128]{1,0:T(8,128)}, u32[]{:S(2)}) copy-start(s32[128,128]{1,0:T(8,128)} %cells.3) | copy-start | bytes 196612
  14.4 1.6 %copy-start.2 = (s32[16,32,128]{2,1,0:T(8,128)S(1)}, s32[16,32,128]{2,1,0:T(8,128)}, u32[]{:S(2)}) copy-start(s32[16,32,128]{2,1,0:T(8,128)} %param.13) | copy-start | bytes 786436
  14.4 1.6 %copy-start.3 = (f32[3,128,128]{2,1,0:T(8,128)S(1)}, f32[3,128,128]{2,1,0:T(8,128)}, u32[]{:S(2)}) copy-start(f32[3,128,128]{2,1,0:T(8,128)} %pol.1) | copy-start | bytes 589828
  14.4 1.6 %copy-start.4 = (f32[3,128,128]{2,1,0:T(8,128)S(1)}, f32[3,128,128]{2,1,0:T(8,128)}, u32[]{:S(2)}) copy-start(f32[3,128,128]{2,1,0:T(8,128)} %cur.1) | copy-start | bytes 589828
  14.4 1.6 %copy-start.8 = (f32[8]{0:T(128)S(1)}, f32[8]{0:T(128)}, u32[]{:S(2)}) copy-start(f32[8]{0:T(128)} %inv_perm.1) | copy-start | bytes 100
  15.9 0.7 copy-start.5
  15.9 0.7 copy-start.6
  16.0 0.7 copy-start.7
  22.6 1.7 %copy-start.10 = (f32[3,16,32,128]{3,2,1,0:T(8,128)S(1)}, f32[3,16,32,128]{3,2,1,0:T(8,128)}, u32[]{:S(2)}) copy-start(f32[3,16,32,128]{3,2,1,0:T(8,128)} %param.12) | copy-start | bytes 2359300
  24.3 0.7 copy-start.12
  24.3 0.8 copy-start.14
  27.4 16.1 %collective-permute-start.4 = (f32[2,32,128]{2,1,0:T(8,128)S(1)}, f32[2,32,128]{2,1,0:T(8,128)S(1)}, u32[]{:S(2)}, u32[]{:S(2)}) collective-permute-start(f32[2,32,128]{2,1,0:T(8,128)S(1)} %slice_bitcast_fusion.30), channel_id=1, source_target_pairs={{0,1},{1,2},{2,3},{3,4},{4,5},{5,6},{6,7},{7,8},{8,9},{9,10},{10,1... | collective-permute-start | bytes 98312 | tf_op jit(solution)/shard_map/ppermute | solution.py:18
  32.4 9.2 %collective-permute-start.3 = (f32[2,16,32]{2,1,0:T(8,128)S(1)}, f32[2,16,32]{2,1,0:T(8,128)S(1)}, u32[]{:S(2)}, u32[]{:S(2)}) collective-permute-start(f32[2,16,32]{2,1,0:T(8,128)S(1)} %pad_maximum_fusion.2), channel_id=1, source_target_pairs={{0,16},{16,32},{32,48},{48,64},{64,80},{80,96},{96,112},{1,17},{17... | collective-permute-start | bytes 12296 | tf_op jit(solution)/shard_map/ppermute | solution.py:18
  34.3 9.1 %collective-permute-start.5 = (f32[2,16,128]{2,1,0:T(8,128)S(1)}, f32[2,16,128]{2,1,0:T(8,128)S(1)}, u32[]{:S(2)}, u32[]{:S(2)}) collective-permute-start(f32[2,16,128]{2,1,0:T(8,128)S(1)} %pad_maximum_fusion.3), channel_id=1, source_target_pairs={{0,128},{128,256},{256,384},{1,129},{129,257},{257,385},{2,130},{1... | collective-permute-start | bytes 49160 | tf_op jit(solution)/shard_map/ppermute | solution.py:18
  48.9 11.3 %collective-permute-start.7 = (f32[2,32,128]{2,1,0:T(8,128)S(1)}, f32[2,32,128]{2,1,0:T(8,128)S(1)}, u32[]{:S(2)}, u32[]{:S(2)}) collective-permute-start(f32[2,32,128]{2,1,0:T(8,128)S(1)} %slice_bitcast_fusion.29), channel_id=1, source_target_pairs={{1,0},{2,1},{3,2},{4,3},{5,4},{6,5},{7,6},{8,7},{9,8},{10,9},{11,1... | collective-permute-start | bytes 98312 | tf_op jit(solution)/shard_map/ppermute | solution.py:18
  50.8 7.5 %collective-permute-start.6 = (f32[2,16,32]{2,1,0:T(8,128)S(1)}, f32[2,16,32]{2,1,0:T(8,128)S(1)}, u32[]{:S(2)}, u32[]{:S(2)}) collective-permute-start(f32[2,16,32]{2,1,0:T(8,128)S(1)} %pad_maximum_fusion.4), channel_id=1, source_target_pairs={{16,0},{32,16},{48,32},{64,48},{80,64},{96,80},{112,96},{17,1},{33... | collective-permute-start | bytes 12296 | tf_op jit(solution)/shard_map/ppermute | solution.py:18
  54.4 5.8 %collective-permute-start.8 = (f32[2,16,128]{2,1,0:T(8,128)S(1)}, f32[2,16,128]{2,1,0:T(8,128)S(1)}, u32[]{:S(2)}, u32[]{:S(2)}) collective-permute-start(f32[2,16,128]{2,1,0:T(8,128)S(1)} %pad_maximum_fusion.5), channel_id=1, source_target_pairs={{128,0},{256,128},{384,256},{129,1},{257,129},{385,257},{130,2},{2... | collective-permute-start | bytes 49160 | tf_op jit(solution)/shard_map/ppermute | solution.py:18
  56.5 3.7 %copy-start.18 = (f32[1,16,31,128]{3,2,1,0:T(8,128)S(1)}, f32[1,16,31,128]{3,2,1,0:T(8,128)}, u32[]{:S(2)}) copy-start(f32[1,16,31,128]{3,2,1,0:T(8,128)} %slice_bitcast_fusion.6) | copy-start | bytes 761860
  58.4 1.8 %copy-start.16 = (f32[1,16,32,127]{3,2,1,0:T(8,128)S(1)}, f32[1,16,32,127]{3,2,1,0:T(8,128)}, u32[]{:S(2)}) copy-start(f32[1,16,32,127]{3,2,1,0:T(8,128)} %slice_bitcast_fusion.4) | copy-start | bytes 780292
  58.4 1.8 %copy-start.17 = (f32[1,16,31,128]{3,2,1,0:T(8,128)S(1)}, f32[1,16,31,128]{3,2,1,0:T(8,128)}, u32[]{:S(2)}) copy-start(f32[1,16,31,128]{3,2,1,0:T(8,128)} %slice_bitcast_fusion.5) | copy-start | bytes 761860
  60.2 1.7 %copy-start.11 = (f32[3,16,32,128]{3,2,1,0:T(8,128)S(1)}, f32[3,16,32,128]{3,2,1,0:T(8,128)}, u32[]{:S(2)}) copy-start(f32[3,16,32,128]{3,2,1,0:T(8,128)} %param.12) | copy-start | bytes 2359300
  60.2 1.7 %copy-start.13 = (f32[1,16,32,128]{3,2,1,0:T(8,128)S(1)}, f32[1,16,32,128]{3,2,1,0:T(8,128)}, u32[]{:S(2)}) copy-start(f32[1,16,32,128]{3,2,1,0:T(8,128)} %copy-done.12) | copy-start | bytes 786436
  60.2 1.7 %copy-start.15 = (f32[1,16,32,128]{3,2,1,0:T(8,128)S(1)}, f32[1,16,32,128]{3,2,1,0:T(8,128)}, u32[]{:S(2)}) copy-start(f32[1,16,32,128]{3,2,1,0:T(8,128)} %copy-done.14) | copy-start | bytes 786436
  62.2 16.4 %copy-start.9 = (f32[3,16,32,128]{3,2,1,0:T(8,128)}, f32[3,16,32,128]{3,2,1,0:T(8,128)S(1)}, u32[]{:S(2)}) copy-start(f32[3,16,32,128]{3,2,1,0:T(8,128)S(1)} %fusion.3) | copy-start | bytes 2359300
  63.8 14.8 %collective-permute-start.10 = (f32[2,32,128]{2,1,0:T(8,128)S(1)}, f32[2,32,128]{2,1,0:T(8,128)S(1)}, u32[]{:S(2)}, u32[]{:S(2)}) collective-permute-start(f32[2,32,128]{2,1,0:T(8,128)S(1)} %slice_bitcast_fusion.28), channel_id=1, source_target_pairs={{0,1},{1,2},{2,3},{3,4},{4,5},{5,6},{6,7},{7,8},{8,9},{9,10},{10,1... | collective-permute-start | bytes 98312 | tf_op jit(solution)/shard_map/ppermute | solution.py:18
  69.0 9.2 %collective-permute-start.9 = (f32[2,16,32]{2,1,0:T(8,128)S(1)}, f32[2,16,32]{2,1,0:T(8,128)S(1)}, u32[]{:S(2)}, u32[]{:S(2)}) collective-permute-start(f32[2,16,32]{2,1,0:T(8,128)S(1)} %pad_maximum_fusion.6), channel_id=1, source_target_pairs={{0,16},{16,32},{32,48},{48,64},{64,80},{80,96},{96,112},{1,17},{17... | collective-permute-start | bytes 12296 | tf_op jit(solution)/shard_map/ppermute | solution.py:18
  71.3 7.3 %collective-permute-start.11 = (f32[2,16,128]{2,1,0:T(8,128)S(1)}, f32[2,16,128]{2,1,0:T(8,128)S(1)}, u32[]{:S(2)}, u32[]{:S(2)}) collective-permute-start(f32[2,16,128]{2,1,0:T(8,128)S(1)} %pad_maximum_fusion.7), channel_id=1, source_target_pairs={{0,128},{128,256},{256,384},{1,129},{129,257},{257,385},{2,130},{1... | collective-permute-start | bytes 49160 | tf_op jit(solution)/shard_map/ppermute | solution.py:18

commit v2 on v1

v2 whole, which is shorter than its diff:
```python
import jax
import jax.numpy as jnp
from jax import lax
from jax.experimental import pallas as pl
from jax.experimental.pallas import tpu as pltpu
from jax.sharding import PartitionSpec as P

TIME_STEP = 0.5
VMEM_LIMIT = 32 * 1024 * 1024

SLABS, ROWS, HALO, LANES, COLUMNS = 16, 32, 8, 128, 7
EXT = ROWS + HALO

FIELDS = 10
UP_X = [(f, 30, 6) for f in (0, 1, 2, 4, 5)] + [(f, 31, 7) for f in range(FIELDS)]
DOWN_X = [(f, 0, 0) for f in (0, 1, 2, 3, 4, 5, 7, 8, 9)] + [(f, 1, 1) for f in (1, 2)]


def passed_along(value, axis, steps):
    count = lax.axis_size(axis)
    first, last = (max(0, -steps), min(count, count - steps))
    return lax.ppermute(value, axis, [(source, source + steps) for source in range(first, last)])


def lanes_by(value, shift):
    shift = shift % LANES
    return pltpu.roll(value, shift, 1) if shift else value


def x_next(value):
    return pltpu.roll(value, EXT - 1, 0)


def x_before(value):
    return pltpu.roll(value, 1, 0)


def lane_ids(rows=EXT):
    return lax.broadcasted_iota(jnp.int32, (rows, LANES), 1)


def column_of(packed, z, slot, lane):
    return lanes_by(packed, lane - ((z + 1) * COLUMNS + slot))


def row_factor(flags):
    row = lax.broadcasted_iota(jnp.int32, (EXT, LANES), 0)
    return jnp.where(row >= ROWS + 4, TIME_STEP * flags[0], TIME_STEP)


def packed_places(rows=EXT):
    lane = lane_ids(rows)
    z_at = lax.shift_right_logical(lane * 9363, 16)
    return z_at, lane - z_at * COLUMNS


def h_slab(h, e, e_above, e_y, factor):
    return (
        h[0] - factor * ((e_y[1] - e[2]) - (e_above[1] - e[1])),
        h[1] - factor * ((e_above[0] - e[0]) - (x_next(e[2]) - e[2])),
        h[2] - factor * ((x_next(e[1]) - e[1]) - (e_y[0] - e[0])),
    )


def e_slab(a, scale, h, h_below, h_y):
    return (
        a[0] + scale * ((h[2] - h_y[1]) - (h[1] - h_below[1])),
        a[1] + scale * ((h[0] - h_below[0]) - (h[2] - x_before(h[2]))),
        a[2] + scale * ((h[1] - x_before(h[1])) - (h[0] - h_y[0])),
    )


def y_next_pair(e, packed_e, z, last):
    return tuple(
        jnp.where(last, column_of(packed_e[c], z, 5, LANES - 1), lanes_by(e[c], -1)) for c in (0, 2)
    )


def y_before_pair(h, packed_h, z, first):
    return tuple(jnp.where(first, column_of(packed_h[c], z, 1, 0), lanes_by(h[c], 1)) for c in (0, 2))


def as_column(row_ref, eye):
    return jnp.sum(jnp.where(eye, row_ref[...], 0.0), axis=1, keepdims=True)


def advance_blocks(e, pitch, cells, inverse, runs, count, decay, restore, drive, pol, cur, pol_out, cur_out, rows, j_rows):
    slots, width = cells.shape
    for b in range(slots):
        run = runs[0, b]
        at = run + lax.shift_right_logical(run, 5) * (pitch - ROWS)
        for comp in range(3):
            rows[comp, pl.ds(b, 1), :] = e[comp, pl.ds(at, 1), :]
    j_rows[...] = jnp.zeros_like(j_rows)
    offsets = lax.bitwise_and(cells[...], width - 1)
    down = lax.broadcasted_iota(jnp.int32, (slots, width), 0)
    across = lax.broadcasted_iota(jnp.int32, (slots, width), 1)
    eye = down == across
    live = down < count[0]
    decay_c, restore_c, drive_c = (as_column(ref, eye) for ref in (decay, restore, drive))
    back = inverse[...]
    for comp in range(3):
        at_cells = jnp.take_along_axis(rows[comp], offsets, axis=1)
        held, polar = cur[comp], pol[comp]
        new = jnp.where(live, decay_c * held - restore_c * polar + drive_c * at_cells, held)
        cur_out[comp] = new
        pol_out[comp] = jnp.where(live, polar + TIME_STEP * new, polar)
        rows[comp] = jnp.take_along_axis(jnp.where(live, new, 0.0), back, axis=1)
    for b in range(slots):
        run = runs[0, b]
        for comp in range(3):
            j_rows[comp, pl.ds(run, 1), :] = rows[comp, pl.ds(b, 1), :]


def spread(value):
    return value * 0x01010101


def invert_rows(offsets, lane):
    words = jnp.full(lane.shape, -0x7F7F7F80, jnp.int32)
    for t, part in enumerate(offsets):
        words = lax.bitwise_or(words, lax.shift_left(lax.bitwise_and(part - lane, LANES - 1), 8 * t))
    low, high = {}, {}
    for s in range(1, LANES):
        misses = lax.bitwise_xor(pltpu.roll(words, s, 1), spread(s)) - spread(1)
        for table, at in ((low, s % 8), (high, s // 8)):
            table[at] = lax.bitwise_and(table[at], misses) if at in table else misses
    found = jnp.zeros(lane.shape, jnp.int32)
    for bit in range(7):
        table, mask = (low, 1 << bit) if bit < 3 else (high, 1 << (bit - 3))
        every = None
        for at, value in table.items():
            if at & mask:
                every = value if every is None else lax.bitwise_and(every, value)
        hit = lax.bitwise_and(lax.shift_right_logical(lax.bitwise_xor(every, -1), 7), spread(1))
        found = lax.bitwise_or(found, lax.shift_left(hit, bit))
    return [
        lax.bitwise_and(lane - lax.bitwise_and(lax.shift_right_logical(found, 8 * t), LANES - 1), LANES - 1)
        for t in range(len(offsets))
    ]


def first_kernel(
    e_in, h_in, material_in, inv_perm_in, cells_in, count, decay_in, restore_in, drive_in, pol_in, cur_in,
    e, h, pol_out, cur_out, a_out, scale_out, inverse_out, cells, runs_out, decay, restore, drive, up_out, down_out,
    material, inv_perm, pol, cur, rows, j_rows, run_row, runs, sems,
):
    copies = {}
    for i, (name, source, target) in enumerate(
        (
            ("cells", cells_in, cells), ("inv_perm", inv_perm_in, inv_perm), ("material", material_in, material),
            ("decay", decay_in, decay), ("restore", restore_in, restore), ("drive", drive_in, drive),
            ("e", e_in, e), ("cur", cur_in, cur), ("pol", pol_in, pol), ("h", h_in, h),
        )
    ):
        copies[name] = pltpu.make_async_copy(source, target, sems.at[i])
        copies[name].start()
    slots, width = cells.shape
    down = lax.broadcasted_iota(jnp.int32, (slots, width), 0)
    across = lax.broadcasted_iota(jnp.int32, (slots, width), 1)
    lane = lane_ids(8)
    copies["cells"].wait()
    run_of = lax.shift_right_logical(cells[...], 7)
    run_row[...] = jnp.sum(jnp.where(down == across, run_of, 0), axis=0, keepdims=True)
    runs_out[...] = run_row[...]
    copy = pltpu.make_async_copy(run_row, runs, sems.at[10])
    copy.start()
    for row in range(0, slots, 32):
        parts = [lax.bitwise_and(cells[row + 8 * t : row + 8 * t + 8, :], width - 1) for t in range(4)]
        for t, part in enumerate(invert_rows(parts, lane)):
            inverse_out[row + 8 * t : row + 8 * t + 8, :] = part
    copies["inv_perm"].wait()
    copies["material"].wait()
    table = jnp.zeros((8, width), jnp.float32)
    for kind in range(inv_perm.shape[0]):
        table = jnp.where(lane == kind, TIME_STEP * inv_perm[kind], table)
    for row in range(0, material.shape[0], 8):
        scale_out[row : row + 8, :] = jnp.take_along_axis(table, material[row : row + 8, :], axis=1)
    for name in ("decay", "restore", "drive", "e", "cur", "pol"):
        copies[name].wait()
    copy.wait()
    advance_blocks(
        e, ROWS, cells, inverse_out, runs, count, decay, restore, drive, pol, cur, pol_out, cur_out, rows, j_rows
    )
    for comp in range(3):
        a_out[comp] = e[comp] - scale_out[...] * j_rows[comp]
    copies["h"].wait()

    def plane(f, x):
        at = pl.ds(x, SLABS, stride=ROWS)
        if f == 9:
            return scale_out[at, :]
        return (e, h, a_out)[f // 3][f % 3, at, :]

    for out, planes in ((up_out, UP_X), (down_out, DOWN_X)):
        for i, (f, x, _) in enumerate(planes):
            out[i] = plane(f, x)


def pack_tiles(tile, tiles):
    lane = lane_ids(8)
    z_at, slot = packed_places(8)
    low = jnp.logical_or(slot == 2, slot == 3)
    inside = jnp.logical_and(z_at >= 1, z_at <= SLABS)
    low, high = jnp.logical_and(low, inside), jnp.logical_and(slot >= 5, inside)
    tops = [jnp.zeros((8, LANES), jnp.float32) for _ in range(tiles)]
    bottoms = list(tops)
    for z in range(SLABS):
        place = (z + 1) * COLUMNS + 5
        top_at, bottom_at = lane >= place, lane >= place + 2
        for t in range(tiles):
            moved = lanes_by(tile(z, t), place - (LANES - 2))
            tops[t] = jnp.where(top_at, moved, tops[t])
            bottoms[t] = jnp.where(bottom_at, moved, bottoms[t])
    return [
        jnp.where(high, top, jnp.where(low, lanes_by(bottom, -5), 0.0)) for top, bottom in zip(tops, bottoms)
    ]


def own_kernel(e, h, a, scale, own_out):
    for f in range(FIELDS):
        def tile(z, t):
            at = slice(z * ROWS + t * 8, z * ROWS + t * 8 + 8)
            return scale[at, :] if f == 9 else (e, h, a)[f // 3][f % 3, at, :]

        for t, value in enumerate(pack_tiles(tile, ROWS // 8)):
            own_out[f, t * 8 : t * 8 + 8, :] = value


UP_E0X, UP_E0Y, UP_E0Y_2, UP_H1Y = 1, 2, 3, 4
DOWN_H1Y = 1


def faces_kernel(from_below, from_above, own, flags, halo_out, pe_out, pscale_out, ph1_out, pe1_out, up_out, down_out):
    halo_out[...] = jnp.zeros_like(halo_out)
    for got, planes in ((from_below, UP_X), (from_above, DOWN_X)):
        for i, (f, _, row) in enumerate(planes):
            halo_out[f, pl.ds(row, SLABS, stride=HALO), :] = got[i]
    packed = []
    for f in range(FIELDS):
        (tile,) = pack_tiles(lambda z, t: halo_out[f, z * HALO : z * HALO + 8, :], 1)
        packed.append(jnp.concatenate([own[f], tile], axis=0))
    z_at, slot = packed_places()
    inside = jnp.logical_and(z_at >= 1, z_at <= SLABS)
    factor = jnp.where(inside, row_factor(flags), 0.0)
    factor = jnp.where(jnp.logical_or(slot >= 5, jnp.logical_or(slot == 2, slot == 3)), factor, 0.0)
    pe, pscale = packed[0:3], packed[9]
    ph1 = packed_h(packed[3:6], pe, factor)
    pe1 = e_slab(
        packed[6:9], pscale, ph1, (lanes_by(ph1[0], COLUMNS), lanes_by(ph1[1], COLUMNS)),
        (lanes_by(ph1[0], 1), lanes_by(ph1[2], 1)),
    )
    for c in range(3):
        pe_out[c], ph1_out[c], pe1_out[c] = pe[c], ph1[c], pe1[c]
    pscale_out[...] = pscale
    up = jnp.zeros((EXT, LANES), jnp.float32)
    for i, value in enumerate((ph1[0], ph1[2], *pe1, pscale)):
        up = jnp.where(slot == i, lanes_by(value, i - 6), up)
    for z_to, value, slot_from, z_from in (
        (UP_E0X, pe[0], 6, 1), (UP_E0Y, pe[1], 6, 1), (UP_E0Y_2, pe[1], 5, 1), (UP_H1Y, ph1[1], 6, SLABS),
    ):
        here = jnp.logical_and(slot == 6, z_at == z_to)
        up = jnp.where(here, lanes_by(value, 6 - slot_from + (z_to - z_from) * COLUMNS), up)
    up_out[...] = up
    low = jnp.zeros((EXT, LANES), jnp.float32)
    for i, value in enumerate((pe1[0], pe1[2], pscale, pe[0], pe[2], pe[1])):
        low = jnp.where(slot == i, lanes_by(value, i - 2), low)
    here = jnp.logical_and(slot == 6, z_at == DOWN_H1Y)
    down_out[...] = jnp.where(here, lanes_by(ph1[1], 4 + (DOWN_H1Y - SLABS) * COLUMNS), low)


def slab_reader(e, h, a, scale, halo):
    def read(f, z):
        if f == 9:
            own = scale[z * ROWS : (z + 1) * ROWS, :]
        else:
            own = (e, h, a)[f // 3][f % 3, z * ROWS : (z + 1) * ROWS, :]
        return jnp.concatenate([own, halo[f, z * HALO : (z + 1) * HALO, :]], axis=0)

    return read


def packed_h(h, e, factor):
    return h_slab(
        h, e, (lanes_by(e[0], -COLUMNS), lanes_by(e[1], -COLUMNS)), (lanes_by(e[0], -1), lanes_by(e[2], -1)), factor
    )


END_H = (0, 14, 15)
END_E = (0, 15)


def ends_kernel(
    e, h, a, scale, halo, pe_in, pscale_in, ph1_in, pe1_in, from_below, from_above, flags,
    pe_out, pscale_out, ph1_out, pe1_out, h1_out, e1_out, up_out, down_out,
):
    z_at, slot = packed_places()
    inside = jnp.logical_and(z_at >= 1, z_at <= SLABS)
    factor = row_factor(flags)
    packed_factor = jnp.where(slot < 2, factor * flags[1], factor)
    packed_factor = jnp.where(inside, packed_factor, 0.0)
    up_got, down_got = from_below[...], from_above[...]
    last_low, first_high = slot == 1, slot == 5

    def columns(value, low=None, high=None):
        value = jnp.where(slot == 2, value, jnp.where(slot == 4, lanes_by(value, -2), 0.0))
        if low is not None:
            value = jnp.where(last_low, lanes_by(up_got, 1 - low), value)
        if high is not None:
            value = jnp.where(first_high, lanes_by(down_got, 5 - high), value)
        return jnp.where(inside, value, 0.0)

    def single(got, slot_to, z_to, z_from, value):
        here = jnp.logical_and(slot == slot_to, z_at == z_to)
        return jnp.where(here, lanes_by(got, slot_to - 6 + (z_to - z_from) * COLUMNS), value)

    pe = [columns(pe_in[0], None, 3), columns(pe_in[1], None, 5), columns(pe_in[2], None, 4)]
    pe[0] = single(up_got, 1, 1, UP_E0X, pe[0])
    pe[1] = single(up_got, 1, 1, UP_E0Y, pe[1])
    pe[1] = single(up_got, 0, 1, UP_E0Y_2, pe[1])
    pscale = columns(pscale_in[...], 5, 2)
    ph1 = [columns(ph1_in[0], 0), columns(ph1_in[1]), columns(ph1_in[2], 1)]
    ph1[1] = single(up_got, 1, SLABS, UP_H1Y, ph1[1])
    ph1[1] = single(down_got, 5, SLABS, DOWN_H1Y, ph1[1])
    pe1 = [columns(pe1_in[0], 2, 0), columns(pe1_in[1], 3), columns(pe1_in[2], 4, 1)]
    upper = jnp.logical_or(slot == 1, slot == 4)
    lower = jnp.logical_or(slot == 2, slot == 5)
    step = jnp.where(upper, packed_factor, 0.0)
    pdx = -(step * lanes_by(pe[2], -1))
    pdz = step * lanes_by(pe[0], -1)
    ph1[0], ph1[2] = ph1[0] + pdx, ph1[2] + pdz
    px = jnp.where(lower, lanes_by(ph1[0], 1), 0.0)
    pz = jnp.where(lower, lanes_by(ph1[2], 1), 0.0)
    pe1[0] = pe1[0] + pscale * (pdz - pz)
    pe1[1] = pe1[1] + pscale * ((pdx - lanes_by(pdx, COLUMNS)) - (pdz - x_before(pdz)))
    pe1[2] = pe1[2] + pscale * (px - pdx)
    for c in range(3):
        pe_out[c], ph1_out[c], pe1_out[c] = pe[c], ph1[c], pe1[c]
    pscale_out[...] = pscale
    read = slab_reader(e, h, a, scale, halo)
    lane = lane_ids()
    first, last = lane == 0, lane == LANES - 1
    zero = jnp.zeros((EXT, LANES), jnp.float32)
    made = {}
    for i, z in enumerate(END_H):
        ez = [read(c, z) for c in range(3)]
        above = (read(0, z + 1), read(1, z + 1)) if z < SLABS - 1 else (zero, zero)
        made[z] = h_slab([read(3 + c, z) for c in range(3)], ez, above, y_next_pair(ez, pe, z, last), factor)
        for c in range(3):
            h1_out[c, i] = made[z][c]
    ends = {}
    for i, z in enumerate(END_E):
        below = made[z - 1][:2] if z else (zero, zero)
        ends[z] = e_slab(
            [read(6 + c, z) for c in range(3)], read(9, z), made[z], below, y_before_pair(made[z], ph1, z, first)
        )
        for c in range(3):
            e1_out[c, i] = ends[z][c]
    top = SLABS - 1
    up = [made[top][0], made[top][1], *ends[top], read(9, top)]
    packed_up = [ph1[0], ph1[1], *pe1, pscale]
    low = [ends[0][0], ends[0][1], read(9, 0), read(0, 0), read(1, 0)]
    packed_down = [pe1[0], pe1[1], pscale, pe[0], pe[1]]
    for out, slabs, columns, z_from in ((up_out, up, packed_up, SLABS), (down_out, low, packed_down, 1)):
        together = zero
        for i, (slab, column) in enumerate(zip(slabs, columns)):
            out[i] = slab
            together = jnp.where(z_at == i, lanes_by(column, (i - z_from) * COLUMNS), together)
        out[len(slabs)] = together


def middle_kernel(
    e, h, a, scale, halo, pe_in, pscale, ph1_in, pe1_in, h1_in, flags,
    e1_out, h2_out, e2_out, h1, h2,
):
    z_at, slot = packed_places()
    factor = row_factor(flags)
    packed_factor = jnp.where(slot < 2, factor * flags[1], factor)
    pe, ph1, pe1 = ([ref[c] for c in range(3)] for ref in (pe_in, ph1_in, pe1_in))
    read = slab_reader(e, h, a, scale, halo)
    lane = lane_ids()
    first, last = lane == 0, lane == LANES - 1
    zero = jnp.zeros((EXT, LANES), jnp.float32)

    def h1_of(c, z):
        return h1_in[c, END_H.index(z)] if z in END_H else h1[c, z]

    for z in range(1, 14):
        ez = [read(c, z) for c in range(3)]
        new = h_slab(
            [read(3 + c, z) for c in range(3)], ez, (read(0, z + 1), read(1, z + 1)), y_next_pair(ez, pe, z, last), factor
        )
        for c in range(3):
            h1[c, z] = new[c]
    for z in range(1, 15):
        hz = [h1_of(c, z) for c in range(3)]
        new = e_slab(
            [read(6 + c, z) for c in range(3)], read(9, z), hz, (h1_of(0, z - 1), h1_of(1, z - 1)),
            y_before_pair(hz, ph1, z, first),
        )
        for c in range(3):
            e1_out[c, z] = new[c]
    ph2 = packed_h(ph1, pe1, packed_factor)
    for z in range(1, 14):
        ez = [e1_out[c, z] for c in range(3)]
        new = h_slab(
            [h1[c, z] for c in range(3)], ez, (e1_out[0, z + 1], e1_out[1, z + 1]), y_next_pair(ez, pe1, z, last), factor
        )
        for c in range(3):
            h2[c, z] = new[c]
            h2_out[c, z * ROWS : (z + 1) * ROWS, :] = new[c][:ROWS]
    for z in range(1, 14):
        hz = [h2[c, z] for c in range(3)]
        below = (h2[0, z - 1], h2[1, z - 1]) if z > 1 else (zero, zero)
        new = e_slab(
            [e1_out[c, z] for c in range(3)], read(9, z), hz, below, y_before_pair(hz, ph2, z, first)
        )
        for c in range(3):
            e2_out[c, z * ROWS : (z + 1) * ROWS, :] = new[c][:ROWS]


def last_kernel(
    e, scale, halo, from_below, from_above, flags, pe_in, pscale_in, ph1_in, pe1_in, h1_in, e1_ends, e1_in, h2_in, e2_in,
    inverse, runs, cells, count, decay, restore, drive, pol, cur,
    e_to, h_to, pol_to, cur_to, e_out, h_out, pol_out, cur_out, e1, rows, j_rows, sems,
):
    started = []

    def send(source, target):
        copy = pltpu.make_async_copy(source, target, sems.at[len(started)])
        copy.start()
        started.append(copy)

    middle = pl.ds(ROWS, 13 * ROWS)
    send(h2_in.at[:, middle, :], h_to.at[:, middle, :])
    z_at, slot = packed_places()
    factor = row_factor(flags)
    below_factor = factor * flags[2]
    packed_factor = jnp.where(slot < 2, factor * flags[1], factor)
    packed_factor = jnp.where(z_at == 0, packed_factor * flags[2], packed_factor)
    packed_factor = jnp.where(z_at <= SLABS, packed_factor, 0.0)
    lane = lane_ids()
    first, last = lane == 0, lane == LANES - 1
    top = SLABS - 1

    def field(f, z):
        if f == 9:
            own = scale[z * ROWS : (z + 1) * ROWS, :]
        else:
            own = e[f, z * ROWS : (z + 1) * ROWS, :]
        return jnp.concatenate([own, halo[f, z * HALO : (z + 1) * HALO, :]], axis=0)

    def columns_below(i):
        return jnp.where(z_at == 0, lanes_by(from_below[6], -i * COLUMNS), 0.0)

    def columns_above(i):
        return jnp.where(z_at == SLABS + 1, lanes_by(from_above[5], (SLABS + 1 - i) * COLUMNS), 0.0)

    in_z = jnp.logical_and(z_at >= 1, z_at <= SLABS)
    far_e = [columns_above(3 + c) + jnp.where(z_at == 1, pe_in[c], 0.0) for c in range(2)]
    pdx = packed_factor * lanes_by(far_e[1], -COLUMNS)
    pdy = -(packed_factor * lanes_by(far_e[0], -COLUMNS))
    ph1 = [
        jnp.where(in_z, ph1_in[0], columns_below(0)) + pdx,
        jnp.where(in_z, ph1_in[1], columns_below(1)) + pdy,
        ph1_in[2],
    ]
    pscale = jnp.where(in_z, pscale_in[...], columns_below(5) + columns_above(2))
    edge = jnp.logical_or(z_at == 1, z_at == SLABS + 1)
    px = jnp.where(edge, lanes_by(ph1[0], COLUMNS), 0.0)
    py = jnp.where(edge, lanes_by(ph1[1], COLUMNS), 0.0)
    pe1 = [
        jnp.where(in_z, pe1_in[0], columns_below(2) + columns_above(0)) + pscale * (py - pdy),
        jnp.where(in_z, pe1_in[1], columns_below(3) + columns_above(1)) + pscale * (pdx - px),
        jnp.where(in_z, pe1_in[2], columns_below(4))
        + pscale * ((pdy - x_before(pdy)) - (pdx - lanes_by(pdx, 1))),
    ]
    ph2 = packed_h(ph1, pe1, packed_factor)

    def shifted_curl(dx, dy, z):
        dx_before = jnp.where(first, column_of(pdx, z, 1, 0), lanes_by(dx, 1))
        return (dy - x_before(dy)) - (dx - dx_before)

    dx, dy = factor * from_above[4], -(factor * from_above[3])
    h1_top = [h1_in[0, 2] + dx, h1_in[1, 2] + dy, h1_in[2, 2]]
    scale_top = field(9, top)
    e1_top = [
        e1_ends[0, 1] - scale_top * dy,
        e1_ends[1, 1] + scale_top * dx,
        e1_ends[2, 1] + scale_top * shifted_curl(dx, dy, top),
    ]
    e1_over = (from_above[0] + from_above[2] * h1_top[1], from_above[1] - from_above[2] * h1_top[0])
    dx, dy = below_factor * field(1, 0), -(below_factor * field(0, 0))
    h1_under = (from_below[0] + dx, from_below[1] + dy)
    scale_under = from_below[5]
    e1_under = [
        from_below[2] - scale_under * dy,
        from_below[3] + scale_under * dx,
        from_below[4] + scale_under * shifted_curl(dx, dy, -1),
    ]
    scale_0 = field(9, 0)
    e1_0 = [
        e1_ends[0, 0] + scale_0 * h1_under[1],
        e1_ends[1, 0] - scale_0 * h1_under[0],
        e1_ends[2, 0],
    ]
    for c in range(3):
        e1[c, 0:EXT, :] = e1_0[c]
        e1[c, top * EXT : (top + 1) * EXT, :] = e1_top[c]
        for z in range(1, top):
            e1[c, z * EXT : z * EXT + ROWS, :] = e1_in[c, z][:ROWS]
    advance_blocks(
        e1, EXT, cells, inverse, runs, count, decay, restore, drive, pol, cur, pol_out, cur_out, rows, j_rows
    )

    e1_1, e1_14 = ([e1_in[c, z] for c in range(3)] for z in (1, 14))
    under = h_slab(
        (*h1_under, h1_under[0]), e1_under, e1_0[:2], y_next_pair(e1_under, pe1, -1, last), below_factor
    )[:2]
    h2_0 = h_slab([h1_in[c, 0] for c in range(3)], e1_0, e1_1[:2], y_next_pair(e1_0, pe1, 0, last), factor)
    h2_14 = h_slab([h1_in[c, 1] for c in range(3)], e1_14, e1_top[:2], y_next_pair(e1_14, pe1, 14, last), factor)
    h2_top = h_slab(h1_top, e1_top, e1_over, y_next_pair(e1_top, pe1, top, last), factor)
    pad = jnp.zeros((HALO, LANES), jnp.float32)
    h2_13 = tuple(jnp.concatenate([h2_in[c, 13 * ROWS : 14 * ROWS, :], pad], axis=0) for c in range(2))
    e2 = {
        0: e_slab(e1_0, scale_0, h2_0, under, y_before_pair(h2_0, ph2, 0, first)),
        14: e_slab(e1_14, field(9, 14), h2_14, h2_13, y_before_pair(h2_14, ph2, 14, first)),
        top: e_slab(e1_top, scale_top, h2_top, h2_14[:2], y_before_pair(h2_top, ph2, top, first)),
    }
    ends = {0: (h2_0, slice(0, ROWS)), 14: (h2_14, slice(ROWS, 2 * ROWS)), top: (h2_top, slice(2 * ROWS, 3 * ROWS))}
    for value, at in ends.values():
        for c in range(3):
            h_out[c, at, :] = value[c][:ROWS]
    send(h_out.at[:, pl.ds(0, ROWS), :], h_to.at[:, pl.ds(0, ROWS), :])
    send(h_out.at[:, pl.ds(ROWS, 2 * ROWS), :], h_to.at[:, pl.ds(14 * ROWS, 2 * ROWS), :])
    send(pol_out, pol_to)
    send(cur_out, cur_to)
    for z in range(SLABS):
        at = slice(z * ROWS, (z + 1) * ROWS)
        own_scale = scale[at, :]
        for c in range(3):
            value = e2[z][c][:ROWS] if z in e2 else e2_in[c, at, :]
            if z == 1 and c == 0:
                value = value + own_scale * h2_0[1][:ROWS]
            if z == 1 and c == 1:
                value = value - own_scale * h2_0[0][:ROWS]
            e_out[c, at, :] = value - own_scale * j_rows[c, at, :]
        if z % 4 == 3:
            part = pl.ds((z - 3) * ROWS, 4 * ROWS)
            send(e_out.at[:, part, :], e_to.at[:, part, :])
    for copy in started:
        copy.wait()


def on_device(
    e_field, h_field, material, inv_permittivity, block_cells, block_count,
    block_decay, block_restore, block_drive, polarization, current,
):
    slots, width = block_cells.shape
    shape = e_field.shape
    runs_all = SLABS * ROWS
    f32, i32 = jnp.float32, jnp.int32
    vmem, smem, hbm = (pl.BlockSpec(memory_space=space) for space in (pltpu.VMEM, pltpu.SMEM, pltpu.HBM))
    params = pltpu.CompilerParams(vmem_limit_bytes=VMEM_LIMIT)

    def arr(*dims, dtype=f32):
        return jax.ShapeDtypeStruct(dims, dtype)

    def call(kernel, outs, ins, name, scratch=(), in_space=vmem, out_space=vmem):
        specs = [smem if id(v) in scalars else in_space for v in ins]
        return pl.pallas_call(
            kernel, out_shape=outs, in_specs=specs, out_specs=[out_space] * len(outs), scratch_shapes=list(scratch),
            compiler_params=params, name=name,
        )(*ins)

    e, h = (v.reshape(3, runs_all, width) for v in (e_field, h_field))
    coefficients = [v.reshape(1, slots) for v in (block_decay, block_restore, block_drive)]
    flags = jnp.stack([lax.axis_index(name) > 0 for name in ("gx", "gy", "gz")]).astype(f32)
    scalars = {id(flags), id(block_count)}
    blocks, flat, ext, tile = arr(3, slots, width), arr(3, runs_all, width), arr(3, EXT, width), arr(EXT, width)
    row = arr(1, slots)
    blocks_vmem, flat_vmem = pltpu.VMEM((3, slots, width), f32), pltpu.VMEM((3, runs_all, width), f32)
    e, h, pol1, cur1, a, scale, inverse, cells, runs, decay, restore, drive, x_up, x_down = call(
        first_kernel,
        [
            flat, flat, blocks, blocks, flat, arr(runs_all, width), arr(slots, width, dtype=i32),
            arr(slots, width, dtype=i32), arr(1, slots, dtype=i32), row, row, row,
            arr(len(UP_X), SLABS, width), arr(len(DOWN_X), SLABS, width),
        ],
        [
            e, h, material.reshape(runs_all, width), inv_permittivity, block_cells, block_count, *coefficients,
            polarization, current,
        ],
        "first",
        [
            pltpu.VMEM((runs_all, width), i32), pltpu.SMEM(inv_permittivity.shape, f32), blocks_vmem, blocks_vmem,
            blocks_vmem, flat_vmem, pltpu.VMEM((1, slots), i32), pltpu.SMEM((1, slots), i32),
            pltpu.SemaphoreType.DMA((11,)),
        ],
        in_space=hbm,
    )
    x_below, x_above = passed_along(x_up, "gx", 1), passed_along(x_down, "gx", -1)
    (own,) = call(own_kernel, [arr(FIELDS, ROWS, width)], [e, h, a, scale], "own")
    halo, pe, pscale, ph1, pe1, y_up, y_down = call(
        faces_kernel,
        [arr(FIELDS, SLABS * HALO, width), ext, tile, ext, ext, tile, tile],
        [x_below, x_above, own, flags],
        "faces",
    )
    y_below, y_above = passed_along(y_up, "gy", 1), passed_along(y_down, "gy", -1)
    pe, pscale, ph1, pe1, h1_ends, e1_ends, z_up, z_down = call(
        ends_kernel,
        [ext, tile, ext, ext, arr(3, 3, EXT, width), arr(3, 2, EXT, width), arr(7, EXT, width), arr(6, EXT, width)],
        [e, h, a, scale, halo, pe, pscale, ph1, pe1, y_below, y_above, flags],
        "ends",
    )
    z_below, z_above = passed_along(z_up, "gz", 1), passed_along(z_down, "gz", -1)
    slabs = (3, SLABS, EXT, width)
    e1, h2, e2 = call(
        middle_kernel,
        [arr(*slabs), flat, flat],
        [e, h, a, scale, halo, pe, pscale, ph1, pe1, h1_ends, flags],
        "middle",
        [pltpu.VMEM(slabs, f32), pltpu.VMEM(slabs, f32)],
    )
    scalars.add(id(runs))
    e_out, h_out, pol2, cur2 = call(
        last_kernel,
        [flat, flat, blocks, blocks],
        [
            e, scale, halo, z_below, z_above, flags, pe, pscale, ph1, pe1, h1_ends, e1_ends, e1, h2, e2,
            inverse, runs, cells, block_count, decay, restore, drive, pol1, cur1,
        ],
        "last",
        [
            flat_vmem, pltpu.VMEM((3, 3 * ROWS, width), f32), blocks_vmem, blocks_vmem,
            pltpu.VMEM((3, SLABS * EXT, width), f32), blocks_vmem, flat_vmem, pltpu.SemaphoreType.DMA((9,)),
        ],
        out_space=hbm,
    )
    return e_out.reshape(shape), h_out.reshape(shape), pol2, cur2


def solution(mesh):
    grid = P(None, "gz", "gx", "gy")
    rows = ("gx", "gy", "gz")
    return jax.shard_map(
        on_device,
        mesh=mesh,
        in_specs=(
            grid, grid, P("gz", "gx", "gy"), P(), P(rows, None), P(rows), P(rows), P(rows), P(rows),
            P(None, rows, None), P(None, rows, None),
        ),
        out_specs=(grid, grid, P(None, rows, None), P(None, rows, None)),
        check_vma=False,
    )
```

time: 81.7 us -> 51.7 us (0.63)
  the two profiles are of different devices: /device:TPU:102 before, /device:TPU:121 now
where the time goes in v2:
time: 51.7 us; the launch traced here: 51.2 us
  starting transfers between devices  18.2 us (35%)
  waiting for transfers between devices  12.9 us (25%)
  Pallas kernels  12 us (23%)
  local copies, waits for them, and re-layouts  6.58 us (13%)
  between operations  1.42 us (3%)
    ppermute x6, starting transfers between devices, passed_along(): lax.ppermute(value, axis, [(source, source + steps) for source in range(f...  18.2 us
    ppermute x6, waiting for transfers between devices, passed_along(): lax.ppermute(value, axis, [(source, source + steps) for source in range(f...  12.9 us
    pallas_call x6, Pallas kernels, call(): pl.pallas_call(kernel, out_shape=outs, in_specs=specs, out_specs=[out_spa...  12 us
    unnamed x20, local copies, waits for them, and re-layouts  6.58 us
  transfers between devices with their start and end apart: 6, of which 3 were waited for; matrix products, arithmetic and copies ran while one was open for 0% of the time, Pallas kernels for 6%

profile of v2, /device:TPU:121, one launch (start us, length us, event | category | flops | bytes accessed | tf_op | source)
XLA Modules:
  0.0 51.2 jit_solution(9716755489710903468)
XLA Ops:
  1.3 0.0 copy-start.9
  1.3 0.0 copy-start.6
  1.3 0.0 copy-start.7
  1.3 0.0 copy-start.8
  1.3 0.6 %copy-done.9 = f32[128]{0:T(128)S(1)} copy-done((f32[128]{0:T(128)S(1)}, f32[128]{0:T(128)}, u32[]{:S(2)}) %copy-start.9) | copy-done | bytes 536
  1.9 0.0 copy-done.6
  2.0 0.0 copy-done.7
  2.0 0.0 copy-done.8
  2.0 0.0 copy-start
  2.0 1.1 %copy-done = f32[3,16,32,128]{3,2,1,0:T(8,128)S(1)} copy-done((f32[3,16,32,128]{3,2,1,0:T(8,128)S(1)}, f32[3,16,32,128]{3,2,1,0:T(8,128)}, u32[]{:S(2)}) %copy-start) | copy-done | bytes 786456
  3.1 0.0 copy-start.1
  3.1 1.1 %copy-done.1 = f32[3,16,32,128]{3,2,1,0:T(8,128)S(1)} copy-done((f32[3,16,32,128]{3,2,1,0:T(8,128)S(1)}, f32[3,16,32,128]{3,2,1,0:T(8,128)}, u32[]{:S(2)}) %copy-start.1) | copy-done | bytes 786456
  4.3 0.0 copy-start.2
  4.3 0.9 %copy-done.2 = s32[16,32,128]{2,1,0:T(8,128)S(1)} copy-done((s32[16,32,128]{2,1,0:T(8,128)S(1)}, s32[16,32,128]{2,1,0:T(8,128)}, u32[]{:S(2)}) %copy-start.2) | copy-done | bytes 262168
  5.2 0.0 copy-start.3
  5.2 0.9 %copy-done.3 = f32[3,128,128]{2,1,0:T(8,128)S(1)} copy-done((f32[3,128,128]{2,1,0:T(8,128)S(1)}, f32[3,128,128]{2,1,0:T(8,128)}, u32[]{:S(2)}) %copy-start.3) | copy-done | bytes 196632
  6.1 0.0 copy-start.4
  6.1 0.9 %copy-done.4 = f32[3,128,128]{2,1,0:T(8,128)S(1)} copy-done((f32[3,128,128]{2,1,0:T(8,128)S(1)}, f32[3,128,128]{2,1,0:T(8,128)}, u32[]{:S(2)}) %copy-start.4) | copy-done | bytes 196632
  7.1 0.0 copy-start.5
  7.1 0.8 %copy-done.5 = s32[128,128]{1,0:T(8,128)S(1)} copy-done((s32[128,128]{1,0:T(8,128)S(1)}, s32[128,128]{1,0:T(8,128)}, u32[]{:S(2)}) %copy-start.5) | copy-done | bytes 65560
  7.9 3.5 %first.1 = (f32[3,512,128]{2,1,0:T(8,128)S(1)}, f32[3,512,128]{2,1,0:T(8,128)S(1)}, f32[3,128,128]{2,1,0:T(8,128)S(1)}, f32[3,128,128]{2,1,0:T(8,128)S(1)}, f32[...) custom-call(f32[3,512,128]{2,1,0:T(8,128)S(1)} %bitcast.11, ...), custom_call_target="tpu_custom_call" | custom-call | tf_op jit(solution)/shard_map/first/pallas_call | solution.py:571
  11.4 3.7 %collective-permute-start = (f32[15,16,128]{2,1,0:T(8,128)S(1)}, f32[15,16,128]{2,1,0:T(8,128)S(1)}, u32[]{:S(2)}, u32[]{:S(2)}) collective-permute-start(f32[15,16,128]{2,1,0:T(8,128)S(1)} %get-tuple-element.42), channel_id=1, source_target_pairs={{0,128},{128,256},{256,384},{1,129},{129,257},{257,385},{2,130},{1... | collective-permute-start | bytes 368648 | tf_op jit(solution)/shard_map/ppermute | solution.py:22
  15.1 1.9 %collective-permute-start.1 = (f32[11,16,128]{2,1,0:T(8,128)}, f32[11,16,128]{2,1,0:T(8,128)S(1)}, u32[]{:S(2)}, u32[]{:S(2)}) collective-permute-start(f32[11,16,128]{2,1,0:T(8,128)} %get-tuple-element.43), channel_id=1, source_target_pairs={{128,0},{256,128},{384,256},{129,1},{257,129},{385,257},{130,2},{2... | collective-permute-start | bytes 270344 | tf_op jit(solution)/shard_map/ppermute | solution.py:22
  17.0 1.3 %own.1 = f32[10,32,128]{2,1,0:T(8,128)S(1)} custom-call(f32[3,512,128]{2,1,0:T(8,128)S(1)} %get-tuple-element.40.e, f32[3,512,128]{2,1,0:T(8,128)S(1)} %get-tuple-element.44.h, f32[3,512,128]{2,1,0:T(8,128)S(1)} %get-tuple-element.45.a, f32[512,128]{1,0:T(8,128)S(1)} %get-tuple-element.41.scale), custom_call_target="tpu_custom_call" | custom-call | tf_op jit(solution)/shard_map/own/pallas_call | solution.py:571
  18.3 0.1 add_convert_fusion.flags
  18.4 2.7 %collective-permute-done.1.from_above = f32[11,16,128]{2,1,0:T(8,128)S(1)} collective-permute-done((f32[11,16,128]{2,1,0:T(8,128)}, f32[11,16,128]{2,1,0:T(8,128)S(1)}, u32[]{:S(2)}, u32[]{:S(2)}) %collective-permute-start.1) | collective-permute-done | bytes 90144 | tf_op jit(solution)/shard_map/ppermute | solution.py:22
  21.1 0.0 collective-permute-done.from_below
  21.1 1.5 %faces.1 = (f32[10,128,128]{2,1,0:T(8,128)S(1)}, f32[3,40,128]{2,1,0:T(8,128)S(1)}, f32[40,128]{1,0:T(8,128)S(1)}, f32[3,40,128]{2,1,0:T(8,128)S(1)}, f32[3,40,1...) custom-call(f32[15,16,128]{2,1,0:T(8,128)S(1)} %collective-permute-done.from_below, ...), custom_call_target="tpu_custom_call" | custom-call | tf_op jit(solution)/shard_map/faces/pallas_call | solution.py:571
  22.7 4.0 %collective-permute-start.2 = (f32[40,128]{1,0:T(8,128)S(1)}, f32[40,128]{1,0:T(8,128)S(1)}, u32[]{:S(2)}, u32[]{:S(2)}) collective-permute-start(f32[40,128]{1,0:T(8,128)S(1)} %get-tuple-element.51), channel_id=1, source_target_pairs={{0,16},{16,32},{32,48},{48,64},{64,80},{80,96},{96,112},{1,17},{17... | collective-permute-start | bytes 61448 | tf_op jit(solution)/shard_map/ppermute | solution.py:22
  26.7 1.9 %collective-permute-start.3 = (f32[40,128]{1,0:T(8,128)S(1)}, f32[40,128]{1,0:T(8,128)S(1)}, u32[]{:S(2)}, u32[]{:S(2)}) collective-permute-start(f32[40,128]{1,0:T(8,128)S(1)} %get-tuple-element.52), channel_id=1, source_target_pairs={{16,0},{32,16},{48,32},{64,48},{80,64},{96,80},{112,96},{17,1},{33... | collective-permute-start | bytes 61448 | tf_op jit(solution)/shard_map/ppermute | solution.py:22
  28.6 0.0 collective-permute-done.2.from_below
  28.6 6.2 %collective-permute-done.3.from_above = f32[40,128]{1,0:T(8,128)S(1)} collective-permute-done((f32[40,128]{1,0:T(8,128)S(1)}, f32[40,128]{1,0:T(8,128)S(1)}, u32[]{:S(2)}, u32[]{:S(2)}) %collective-permute-start.3) | collective-permute-done | bytes 20512 | tf_op jit(solution)/shard_map/ppermute | solution.py:22
  34.8 1.0 %ends.1 = (f32[3,40,128]{2,1,0:T(8,128)S(1)}, f32[40,128]{1,0:T(8,128)S(1)}, f32[3,40,128]{2,1,0:T(8,128)S(1)}, f32[3,40,128]{2,1,0:T(8,128)S(1)}, f32[3,3,40,12...) custom-call(f32[3,512,128]{2,1,0:T(8,128)S(1)} %get-tuple-element.40.e,, ...), custom_call_target="tpu_custom_call" | custom-call | tf_op jit(solution)/shard_map/ends/pallas_call | solution.py:571
  35.9 4.8 %collective-permute-start.4 = (f32[7,40,128]{2,1,0:T(8,128)S(1)}, f32[7,40,128]{2,1,0:T(8,128)S(1)}, u32[]{:S(2)}, u32[]{:S(2)}) collective-permute-start(f32[7,40,128]{2,1,0:T(8,128)S(1)} %get-tuple-element.53), channel_id=1, source_target_pairs={{0,1},{1,2},{2,3},{3,4},{4,5},{5,6},{6,7},{7,8},{8,9},{9,10},{10,1... | collective-permute-start | bytes 430088 | tf_op jit(solution)/shard_map/ppermute | solution.py:22
  40.6 1.9 %collective-permute-start.5 = (f32[6,40,128]{2,1,0:T(8,128)S(1)}, f32[6,40,128]{2,1,0:T(8,128)S(1)}, u32[]{:S(2)}, u32[]{:S(2)}) collective-permute-start(f32[6,40,128]{2,1,0:T(8,128)S(1)} %get-tuple-element.54), channel_id=1, source_target_pairs={{1,0},{2,1},{3,2},{4,3},{5,4},{6,5},{7,6},{8,7},{9,8},{10,9},{11,1... | collective-permute-start | bytes 368648 | tf_op jit(solution)/shard_map/ppermute | solution.py:22
  42.6 1.7 %middle.1 = (f32[3,16,40,128]{3,2,1,0:T(8,128)S(1)}, f32[3,512,128]{2,1,0:T(8,128)S(1)}, f32[3,512,128]{2,1,0:T(8,128)S(1)}) custom-call(f32[3,512,128]{2,1,0:T(8,128)S(1)} %get-tuple-element.40.e, f32[3,512,128]{2,1,0:T(8,128)S(1)} %get-tuple-element.44.h, f32[3,512,128]{2,1,0:T(8,128)S(1)} %get-tuple-element.45.a, f32[512,128]{1,0:T(8,128)S(1)} %get-tuple-element.41.scale, ...), custom_call_target="tpu_custom_call" | custom-call | tf_op jit(solution)/shard_map/middle/pallas_call | solution.py:571
  44.3 4.0 %collective-permute-done.5.from_above = f32[6,40,128]{2,1,0:T(8,128)S(1)} collective-permute-done((f32[6,40,128]{2,1,0:T(8,128)S(1)}, f32[6,40,128]{2,1,0:T(8,128)S(1)}, u32[]{:S(2)}, u32[]{:S(2)}) %collective-permute-start.5) | collective-permute-done | bytes 122912 | tf_op jit(solution)/shard_map/ppermute | solution.py:22
  48.3 0.0 collective-permute-done.4.from_below
  48.3 2.9 %last.1 = (f32[3,512,128]{2,1,0:T(8,128)}, f32[3,512,128]{2,1,0:T(8,128)}, f32[3,128,128]{2,1,0:T(8,128)}, f32[3,128,128]{2,1,0:T(8,128)}) custom-call(f32[3,512,128]{2,1,0:T(8,128)S(1)} %get-tuple-element.40.e, f32[512,128]{1,0:T(8,128)S(1)} %get-tuple-element.41.scale, f32[10,128,128]{2,1,0:T(8,128)S(1)} %get-tuple-element.46.halo, ...), custom_call_target="tpu_custom_call" | custom-call | tf_op jit(solution)/shard_map/last/pallas_call | solution.py:571
Async XLA Ops:
  1.3 0.7 %copy-start.9 = (f32[128]{0:T(128)S(1)}, f32[128]{0:T(128)}, u32[]{:S(2)}) copy-start(f32[128]{0:T(128)} %param.19) | copy-start | bytes 1540
  1.3 0.7 %copy-start.6 = (f32[8]{0:T(128)S(1)}, f32[8]{0:T(128)}, u32[]{:S(2)}) copy-start(f32[8]{0:T(128)} %inv_perm_in.1) | copy-start | bytes 100
  1.3 0.7 %copy-start.7 = (f32[128]{0:T(128)S(1)}, f32[128]{0:T(128)}, u32[]{:S(2)}) copy-start(f32[128]{0:T(128)} %param.17) | copy-start | bytes 1540
  1.3 0.7 %copy-start.8 = (f32[128]{0:T(128)S(1)}, f32[128]{0:T(128)}, u32[]{:S(2)}) copy-start(f32[128]{0:T(128)} %param.18) | copy-start | bytes 1540
  2.0 1.1 %copy-start = (f32[3,16,32,128]{3,2,1,0:T(8,128)S(1)}, f32[3,16,32,128]{3,2,1,0:T(8,128)}, u32[]{:S(2)}) copy-start(f32[3,16,32,128]{3,2,1,0:T(8,128)} %param.11) | copy-start | bytes 2359300
  3.1 1.1 %copy-start.1 = (f32[3,16,32,128]{3,2,1,0:T(8,128)S(1)}, f32[3,16,32,128]{3,2,1,0:T(8,128)}, u32[]{:S(2)}) copy-start(f32[3,16,32,128]{3,2,1,0:T(8,128)} %param.12) | copy-start | bytes 2359300
  4.3 0.9 %copy-start.2 = (s32[16,32,128]{2,1,0:T(8,128)S(1)}, s32[16,32,128]{2,1,0:T(8,128)}, u32[]{:S(2)}) copy-start(s32[16,32,128]{2,1,0:T(8,128)} %param.13) | copy-start | bytes 786436
  5.2 0.9 %copy-start.3 = (f32[3,128,128]{2,1,0:T(8,128)S(1)}, f32[3,128,128]{2,1,0:T(8,128)}, u32[]{:S(2)}) copy-start(f32[3,128,128]{2,1,0:T(8,128)} %pol_in.1) | copy-start | bytes 589828
  6.1 0.9 %copy-start.4 = (f32[3,128,128]{2,1,0:T(8,128)S(1)}, f32[3,128,128]{2,1,0:T(8,128)}, u32[]{:S(2)}) copy-start(f32[3,128,128]{2,1,0:T(8,128)} %cur_in.1) | copy-start | bytes 589828
  7.1 0.8 %copy-start.5 = (s32[128,128]{1,0:T(8,128)S(1)}, s32[128,128]{1,0:T(8,128)}, u32[]{:S(2)}) copy-start(s32[128,128]{1,0:T(8,128)} %cells_in.1) | copy-start | bytes 196612
  11.4 9.8 %collective-permute-start = (f32[15,16,128]{2,1,0:T(8,128)S(1)}, f32[15,16,128]{2,1,0:T(8,128)S(1)}, u32[]{:S(2)}, u32[]{:S(2)}) collective-permute-start(f32[15,16,128]{2,1,0:T(8,128)S(1)} %get-tuple-element.42), channel_id=1, source_target_pairs={{0,128},{128,256},{256,384},{1,129},{129,257},{257,385},{2,130},{1... | collective-permute-start | bytes 368648 | tf_op jit(solution)/shard_map/ppermute | solution.py:22
  15.1 6.1 %collective-permute-start.1 = (f32[11,16,128]{2,1,0:T(8,128)}, f32[11,16,128]{2,1,0:T(8,128)S(1)}, u32[]{:S(2)}, u32[]{:S(2)}) collective-permute-start(f32[11,16,128]{2,1,0:T(8,128)} %get-tuple-element.43), channel_id=1, source_target_pairs={{128,0},{256,128},{384,256},{129,1},{257,129},{385,257},{130,2},{2... | collective-permute-start | bytes 270344 | tf_op jit(solution)/shard_map/ppermute | solution.py:22
  22.7 6.0 %collective-permute-start.2 = (f32[40,128]{1,0:T(8,128)S(1)}, f32[40,128]{1,0:T(8,128)S(1)}, u32[]{:S(2)}, u32[]{:S(2)}) collective-permute-start(f32[40,128]{1,0:T(8,128)S(1)} %get-tuple-element.51), channel_id=1, source_target_pairs={{0,16},{16,32},{32,48},{48,64},{64,80},{80,96},{96,112},{1,17},{17... | collective-permute-start | bytes 61448 | tf_op jit(solution)/shard_map/ppermute | solution.py:22
  26.7 8.1 %collective-permute-start.3 = (f32[40,128]{1,0:T(8,128)S(1)}, f32[40,128]{1,0:T(8,128)S(1)}, u32[]{:S(2)}, u32[]{:S(2)}) collective-permute-start(f32[40,128]{1,0:T(8,128)S(1)} %get-tuple-element.52), channel_id=1, source_target_pairs={{16,0},{32,16},{48,32},{64,48},{80,64},{96,80},{112,96},{17,1},{33... | collective-permute-start | bytes 61448 | tf_op jit(solution)/shard_map/ppermute | solution.py:22
  35.9 12.4 %collective-permute-start.4 = (f32[7,40,128]{2,1,0:T(8,128)S(1)}, f32[7,40,128]{2,1,0:T(8,128)S(1)}, u32[]{:S(2)}, u32[]{:S(2)}) collective-permute-start(f32[7,40,128]{2,1,0:T(8,128)S(1)} %get-tuple-element.53), channel_id=1, source_target_pairs={{0,1},{1,2},{2,3},{3,4},{4,5},{5,6},{6,7},{7,8},{8,9},{9,10},{10,1... | collective-permute-start | bytes 430088 | tf_op jit(solution)/shard_map/ppermute | solution.py:22
  40.6 7.7 %collective-permute-start.5 = (f32[6,40,128]{2,1,0:T(8,128)S(1)}, f32[6,40,128]{2,1,0:T(8,128)S(1)}, u32[]{:S(2)}, u32[]{:S(2)}) collective-permute-start(f32[6,40,128]{2,1,0:T(8,128)S(1)} %get-tuple-element.54), channel_id=1, source_target_pairs={{1,0},{2,1},{3,2},{4,3},{5,4},{6,5},{7,6},{8,7},{9,8},{10,9},{11,1... | collective-permute-start | bytes 368648 | tf_op jit(solution)/shard_map/ppermute | solution.py:22

commit v3 on v2

--- a/solution.py
+++ b/solution.py
@@ -16,10 +16,31 @@
 DOWN_X = [(f, 0, 0) for f in (0, 1, 2, 3, 4, 5, 7, 8, 9)] + [(f, 1, 1) for f in (1, 2)]
 
 
-def passed_along(value, axis, steps):
-    count = lax.axis_size(axis)
-    first, last = (max(0, -steps), min(count, count - steps))
-    return lax.ppermute(value, axis, [(source, source + steps) for source in range(first, last)])
+def swapped(value, axis, first):
+    pairs = [(k, k + 1) for k in range(first, lax.axis_size(axis) - 1, 2)]
+    return lax.ppermute(value, axis, pairs + [(upper, lower) for lower, upper in pairs])
+
+
+def is_even(flags, axis):
+    return flags[3 + axis] > 0.5
+
+
+def to_swap(even, even_out, odd_out, up, down):
+    for i, value in enumerate(up):
+        if i < len(down):
+            even_out[i] = jnp.where(even, value, down[i])
+            odd_out[i] = jnp.where(even, down[i], value)
+        else:
+            even_out[i] = value
+            odd_out[i] = value
+
+
+class Swapped:
+    def __init__(self, even, when_even, when_odd):
+        self.even, self.when_even, self.when_odd = even, when_even, when_odd
+
+    def __getitem__(self, at):
+        return jnp.where(self.even, self.when_even[at], self.when_odd[at])
 
 
 def lanes_by(value, shift):
@@ -141,7 +162,7 @@
 
 
 def first_kernel(
-    e_in, h_in, material_in, inv_perm_in, cells_in, count, decay_in, restore_in, drive_in, pol_in, cur_in,
+    e_in, h_in, material_in, inv_perm_in, cells_in, count, decay_in, restore_in, drive_in, pol_in, cur_in, flags,
     e, h, pol_out, cur_out, a_out, scale_out, inverse_out, cells, runs_out, decay, restore, drive, up_out, down_out,
     material, inv_perm, pol, cur, rows, j_rows, run_row, runs, sems,
 ):
@@ -192,9 +213,8 @@
             return scale_out[at, :]
         return (e, h, a_out)[f // 3][f % 3, at, :]
 
-    for out, planes in ((up_out, UP_X), (down_out, DOWN_X)):
-        for i, (f, x, _) in enumerate(planes):
-            out[i] = plane(f, x)
+    up, down = ([plane(f, x) for f, x, _ in planes] for planes in (UP_X, DOWN_X))
+    to_swap(is_even(flags, 0), up_out, down_out, up, down)
 
 
 def pack_tiles(tile, tiles):
@@ -231,7 +251,9 @@
 DOWN_H1Y = 1
 
 
-def faces_kernel(from_below, from_above, own, flags, halo_out, pe_out, pscale_out, ph1_out, pe1_out, up_out, down_out):
+def faces_kernel(got_first, got_second, own, flags, halo_out, pe_out, pscale_out, ph1_out, pe1_out, up_out, down_out):
+    even = is_even(flags, 0)
+    from_above, from_below = Swapped(even, got_first, got_second), Swapped(even, got_second, got_first)
     halo_out[...] = jnp.zeros_like(halo_out)
     for got, planes in ((from_below, UP_X), (from_above, DOWN_X)):
         for i, (f, _, row) in enumerate(planes):
@@ -261,12 +283,12 @@
     ):
         here = jnp.logical_and(slot == 6, z_at == z_to)
         up = jnp.where(here, lanes_by(value, 6 - slot_from + (z_to - z_from) * COLUMNS), up)
-    up_out[...] = up
     low = jnp.zeros((EXT, LANES), jnp.float32)
     for i, value in enumerate((pe1[0], pe1[2], pscale, pe[0], pe[2], pe[1])):
         low = jnp.where(slot == i, lanes_by(value, i - 2), low)
     here = jnp.logical_and(slot == 6, z_at == DOWN_H1Y)
-    down_out[...] = jnp.where(here, lanes_by(ph1[1], 4 + (DOWN_H1Y - SLABS) * COLUMNS), low)
+    low = jnp.where(here, lanes_by(ph1[1], 4 + (DOWN_H1Y - SLABS) * COLUMNS), low)
+    to_swap(is_even(flags, 1), up_out, down_out, [up], [low])
 
 
 def slab_reader(e, h, a, scale, halo):
@@ -291,7 +313,7 @@
 
 
 def ends_kernel(
-    e, h, a, scale, halo, pe_in, pscale_in, ph1_in, pe1_in, from_below, from_above, flags,
+    e, h, a, scale, halo, pe_in, pscale_in, ph1_in, pe1_in, got_first, got_second, flags,
     pe_out, pscale_out, ph1_out, pe1_out, h1_out, e1_out, up_out, down_out,
 ):
     z_at, slot = packed_places()
@@ -299,7 +321,8 @@
     factor = row_factor(flags)
     packed_factor = jnp.where(slot < 2, factor * flags[1], factor)
     packed_factor = jnp.where(inside, packed_factor, 0.0)
-    up_got, down_got = from_below[...], from_above[...]
+    even = is_even(flags, 1)
+    up_got, down_got = Swapped(even, got_second, got_first)[0], Swapped(even, got_first, got_second)[0]
     last_low, first_high = slot == 1, slot == 5
 
     def columns(value, low=None, high=None):
@@ -361,12 +384,12 @@
     packed_up = [ph1[0], ph1[1], *pe1, pscale]
     low = [ends[0][0], ends[0][1], read(9, 0), read(0, 0), read(1, 0)]
     packed_down = [pe1[0], pe1[1], pscale, pe[0], pe[1]]
-    for out, slabs, columns, z_from in ((up_out, up, packed_up, SLABS), (down_out, low, packed_down, 1)):
+    for slabs, columns, z_from in ((up, packed_up, SLABS), (low, packed_down, 1)):
         together = zero
-        for i, (slab, column) in enumerate(zip(slabs, columns)):
-            out[i] = slab
+        for i, column in enumerate(columns):
             together = jnp.where(z_at == i, lanes_by(column, (i - z_from) * COLUMNS), together)
-        out[len(slabs)] = together
+        slabs.insert(0, together)
+    to_swap(is_even(flags, 2), up_out, down_out, up, low)
 
 
 def middle_kernel(
@@ -420,7 +443,7 @@
 
 
 def last_kernel(
-    e, scale, halo, from_below, from_above, flags, pe_in, pscale_in, ph1_in, pe1_in, h1_in, e1_ends, e1_in, h2_in, e2_in,
+    e, scale, halo, got_first, got_second, flags, pe_in, pscale_in, ph1_in, pe1_in, h1_in, e1_ends, e1_in, h2_in, e2_in,
     inverse, runs, cells, count, decay, restore, drive, pol, cur,
     e_to, h_to, pol_to, cur_to, e_out, h_out, pol_out, cur_out, e1, rows, j_rows, sems,
 ):
@@ -431,6 +454,8 @@
         copy.start()
         started.append(copy)
 
+    even = is_even(flags, 2)
+    from_above, from_below = Swapped(even, got_first, got_second), Swapped(even, got_second, got_first)
     middle = pl.ds(ROWS, 13 * ROWS)
     send(h2_in.at[:, middle, :], h_to.at[:, middle, :])
     z_at, slot = packed_places()
@@ -450,11 +475,13 @@
             own = e[f, z * ROWS : (z + 1) * ROWS, :]
         return jnp.concatenate([own, halo[f, z * HALO : (z + 1) * HALO, :]], axis=0)
 
+    below_columns, above_columns = from_below[0], from_above[0]
+
     def columns_below(i):
-        return jnp.where(z_at == 0, lanes_by(from_below[6], -i * COLUMNS), 0.0)
+        return jnp.where(z_at == 0, lanes_by(below_columns, -i * COLUMNS), 0.0)
 
     def columns_above(i):
-        return jnp.where(z_at == SLABS + 1, lanes_by(from_above[5], (SLABS + 1 - i) * COLUMNS), 0.0)
+        return jnp.where(z_at == SLABS + 1, lanes_by(above_columns, (SLABS + 1 - i) * COLUMNS), 0.0)
 
     in_z = jnp.logical_and(z_at >= 1, z_at <= SLABS)
     far_e = [columns_above(3 + c) + jnp.where(z_at == 1, pe_in[c], 0.0) for c in range(2)]
@@ -481,7 +508,7 @@
         dx_before = jnp.where(first, column_of(pdx, z, 1, 0), lanes_by(dx, 1))
         return (dy - x_before(dy)) - (dx - dx_before)
 
-    dx, dy = factor * from_above[4], -(factor * from_above[3])
+    dx, dy = factor * from_above[5], -(factor * from_above[4])
     h1_top = [h1_in[0, 2] + dx, h1_in[1, 2] + dy, h1_in[2, 2]]
     scale_top = field(9, top)
     e1_top = [
@@ -489,14 +516,14 @@
         e1_ends[1, 1] + scale_top * dx,
         e1_ends[2, 1] + scale_top * shifted_curl(dx, dy, top),
     ]
-    e1_over = (from_above[0] + from_above[2] * h1_top[1], from_above[1] - from_above[2] * h1_top[0])
+    e1_over = (from_above[1] + from_above[3] * h1_top[1], from_above[2] - from_above[3] * h1_top[0])
     dx, dy = below_factor * field(1, 0), -(below_factor * field(0, 0))
-    h1_under = (from_below[0] + dx, from_below[1] + dy)
-    scale_under = from_below[5]
+    h1_under = (from_below[1] + dx, from_below[2] + dy)
+    scale_under = from_below[6]
     e1_under = [
-        from_below[2] - scale_under * dy,
-        from_below[3] + scale_under * dx,
-        from_below[4] + scale_under * shifted_curl(dx, dy, -1),
+        from_below[3] - scale_under * dy,
+        from_below[4] + scale_under * dx,
+        from_below[5] + scale_under * shifted_curl(dx, dy, -1),
     ]
     scale_0 = field(9, 0)
     e1_0 = [
@@ -573,23 +600,27 @@
             compiler_params=params, name=name,
         )(*ins)
 
+    def in_hbm(value):
+        return pltpu.with_memory_space_constraint(value, pltpu.HBM)
+
     e, h = (v.reshape(3, runs_all, width) for v in (e_field, h_field))
     coefficients = [v.reshape(1, slots) for v in (block_decay, block_restore, block_drive)]
-    flags = jnp.stack([lax.axis_index(name) > 0 for name in ("gx", "gy", "gz")]).astype(f32)
+    place = [lax.axis_index(name) for name in ("gx", "gy", "gz")]
+    flags = jnp.stack([k > 0 for k in place] + [k % 2 == 0 for k in place]).astype(f32)
     scalars = {id(flags), id(block_count)}
     blocks, flat, ext, tile = arr(3, slots, width), arr(3, runs_all, width), arr(3, EXT, width), arr(EXT, width)
     row = arr(1, slots)
     blocks_vmem, flat_vmem = pltpu.VMEM((3, slots, width), f32), pltpu.VMEM((3, runs_all, width), f32)
-    e, h, pol1, cur1, a, scale, inverse, cells, runs, decay, restore, drive, x_up, x_down = call(
+    e, h, pol1, cur1, a, scale, inverse, cells, runs, decay, restore, drive, x_first, x_second = call(
         first_kernel,
         [
             flat, flat, blocks, blocks, flat, arr(runs_all, width), arr(slots, width, dtype=i32),
             arr(slots, width, dtype=i32), arr(1, slots, dtype=i32), row, row, row,
-            arr(len(UP_X), SLABS, width), arr(len(DOWN_X), SLABS, width),
+            arr(len(UP_X), SLABS, width), arr(len(UP_X), SLABS, width),
         ],
         [
-            e, h, material.reshape(runs_all, width), inv_permittivity, block_cells, block_count, *coefficients,
-            polarization, current,
+            *(in_hbm(v) for v in (e, h, material.reshape(runs_all, width), inv_permittivity, block_cells)), block_count,
+            *(in_hbm(v) for v in (*coefficients, polarization, current)), flags,
         ],
         "first",
         [
@@ -599,22 +630,22 @@
         ],
         in_space=hbm,
     )
-    x_below, x_above = passed_along(x_up, "gx", 1), passed_along(x_down, "gx", -1)
+    x_first, x_second = swapped(x_first, "gx", 0), swapped(x_second, "gx", 1)
     (own,) = call(own_kernel, [arr(FIELDS, ROWS, width)], [e, h, a, scale], "own")
-    halo, pe, pscale, ph1, pe1, y_up, y_down = call(
+    halo, pe, pscale, ph1, pe1, y_first, y_second = call(
         faces_kernel,
-        [arr(FIELDS, SLABS * HALO, width), ext, tile, ext, ext, tile, tile],
-        [x_below, x_above, own, flags],
+        [arr(FIELDS, SLABS * HALO, width), ext, tile, ext, ext, arr(1, EXT, width), arr(1, EXT, width)],
+        [x_first, x_second, own, flags],
         "faces",
     )
-    y_below, y_above = passed_along(y_up, "gy", 1), passed_along(y_down, "gy", -1)
-    pe, pscale, ph1, pe1, h1_ends, e1_ends, z_up, z_down = call(
+    y_first, y_second = swapped(y_first, "gy", 0), swapped(y_second, "gy", 1)
+    pe, pscale, ph1, pe1, h1_ends, e1_ends, z_first, z_second = call(
         ends_kernel,
-        [ext, tile, ext, ext, arr(3, 3, EXT, width), arr(3, 2, EXT, width), arr(7, EXT, width), arr(6, EXT, width)],
-        [e, h, a, scale, halo, pe, pscale, ph1, pe1, y_below, y_above, flags],
+        [ext, tile, ext, ext, arr(3, 3, EXT, width), arr(3, 2, EXT, width), arr(7, EXT, width), arr(7, EXT, width)],
+        [e, h, a, scale, halo, pe, pscale, ph1, pe1, y_first, y_second, flags],
         "ends",
     )
-    z_below, z_above = passed_along(z_up, "gz", 1), passed_along(z_down, "gz", -1)
+    z_first, z_second = swapped(z_first, "gz", 0), swapped(z_second, "gz", 1)
     slabs = (3, SLABS, EXT, width)
     e1, h2, e2 = call(
         middle_kernel,
@@ -628,7 +659,7 @@
         last_kernel,
         [flat, flat, blocks, blocks],
         [
-            e, scale, halo, z_below, z_above, flags, pe, pscale, ph1, pe1, h1_ends, e1_ends, e1, h2, e2,
+            e, scale, halo, z_first, z_second, flags, pe, pscale, ph1, pe1, h1_ends, e1_ends, e1, h2, e2,
             inverse, runs, cells, block_count, decay, restore, drive, pol1, cur1,
         ],
         "last",

time: 51.7 us -> 43.5 us (0.84)
  the two profiles are of different devices: /device:TPU:121 before, /device:TPU:102 now
where the time goes in v3:
time: 43.5 us; the launch traced here: 43.2 us
  starting transfers between devices  22 us (51%)
  Pallas kernels  12 us (28%)
  waiting for transfers between devices  7.6 us (17%)
  between operations  1.41 us (3%)
    ppermute x6, starting transfers between devices, swapped(): lax.ppermute(value, axis, pairs + [(upper, lower) for lower, upper in pai...  22 us
    pallas_call x6, Pallas kernels, call(): pl.pallas_call(kernel, out_shape=outs, in_specs=specs, out_specs=[out_spa...  12 us
    ppermute x6, waiting for transfers between devices, swapped(): lax.ppermute(value, axis, pairs + [(upper, lower) for lower, upper in pai...  7.6 us
  transfers between devices with their start and end apart: 6, of which 3 were waited for; matrix products, arithmetic and copies ran while one was open for 0% of the time, Pallas kernels for 7%

profile of v3, /device:TPU:102, one launch (start us, length us, event | category | flops | bytes accessed | tf_op | source)
XLA Modules:
  0.0 43.2 jit_solution(10142829714848003342)
XLA Ops:
  1.3 0.1 stack.27
  1.4 3.5 %first.1 = (f32[3,512,128]{2,1,0:T(8,128)S(1)}, f32[3,512,128]{2,1,0:T(8,128)S(1)}, f32[3,128,128]{2,1,0:T(8,128)S(1)}, f32[3,128,128]{2,1,0:T(8,128)S(1)}, f32[...) custom-call(f32[3,512,128]{2,1,0:T(8,128)} %bitcast.14, ...), custom_call_target="tpu_custom_call" | custom-call | tf_op jit(solution)/shard_map/first/pallas_call | solution.py:598
  4.9 1.9 %collective-permute-start = (f32[15,16,128]{2,1,0:T(8,128)S(1)}, f32[15,16,128]{2,1,0:T(8,128)S(1)}, u32[]{:S(2)}, u32[]{:S(2)}) collective-permute-start(f32[15,16,128]{2,1,0:T(8,128)S(1)} %get-tuple-element.42), channel_id=1, source_target_pairs={{0,128},{256,384},{128,0},{384,256},{1,129},{257,385},{129,1},{385... | collective-permute-start | bytes 368648 | tf_op jit(solution)/shard_map/ppermute | solution.py:21
  6.8 2.8 %collective-permute-start.1 = (f32[15,16,128]{2,1,0:T(8,128)S(1)}, f32[15,16,128]{2,1,0:T(8,128)S(1)}, u32[]{:S(2)}, u32[]{:S(2)}) collective-permute-start(f32[15,16,128]{2,1,0:T(8,128)S(1)} %get-tuple-element.43), channel_id=1, source_target_pairs={{128,256},{256,128},{129,257},{257,129},{130,258},{258,130},{131,2... | collective-permute-start | bytes 368648 | tf_op jit(solution)/shard_map/ppermute | solution.py:21
  9.7 1.3 %own.1 = f32[10,32,128]{2,1,0:T(8,128)S(1)} custom-call(f32[3,512,128]{2,1,0:T(8,128)S(1)} %get-tuple-element.40.e, f32[3,512,128]{2,1,0:T(8,128)S(1)} %get-tuple-element.44.h, f32[3,512,128]{2,1,0:T(8,128)S(1)} %get-tuple-element.45.a, f32[512,128]{1,0:T(8,128)S(1)} %get-tuple-element.41.scale), custom_call_target="tpu_custom_call" | custom-call | tf_op jit(solution)/shard_map/own/pallas_call | solution.py:598
  11.0 0.0 collective-permute-done.got_first
  11.0 2.0 %collective-permute-done.1.got_second = f32[15,16,128]{2,1,0:T(8,128)S(1)} collective-permute-done((f32[15,16,128]{2,1,0:T(8,128)S(1)}, f32[15,16,128]{2,1,0:T(8,128)S(1)}, u32[]{:S(2)}, u32[]{:S(2)}) %collective-permute-start.1) | collective-permute-done | bytes 122912 | tf_op jit(solution)/shard_map/ppermute | solution.py:21
  13.0 1.5 %faces.1 = (f32[10,128,128]{2,1,0:T(8,128)S(1)}, f32[3,40,128]{2,1,0:T(8,128)S(1)}, f32[40,128]{1,0:T(8,128)S(1)}, f32[3,40,128]{2,1,0:T(8,128)S(1)}, f32[3,40,1...) custom-call(f32[15,16,128]{2,1,0:T(8,128)S(1)} %collective-permute-done.got_first, ...), custom_call_target="tpu_custom_call" | custom-call | tf_op jit(solution)/shard_map/faces/pallas_call | solution.py:598
  14.5 3.5 %collective-permute-start.2 = (f32[1,40,128]{2,1,0:T(8,128)S(1)}, f32[1,40,128]{2,1,0:T(8,128)S(1)}, u32[]{:S(2)}, u32[]{:S(2)}) collective-permute-start(f32[1,40,128]{2,1,0:T(8,128)S(1)} %get-tuple-element.51), channel_id=1, source_target_pairs={{0,16},{32,48},{64,80},{96,112},{16,0},{48,32},{80,64},{112,96},{1... | collective-permute-start | bytes 61448 | tf_op jit(solution)/shard_map/ppermute | solution.py:21
  18.0 4.9 %collective-permute-start.3 = (f32[1,40,128]{2,1,0:T(8,128)S(1)}, f32[1,40,128]{2,1,0:T(8,128)S(1)}, u32[]{:S(2)}, u32[]{:S(2)}) collective-permute-start(f32[1,40,128]{2,1,0:T(8,128)S(1)} %get-tuple-element.52), channel_id=1, source_target_pairs={{16,32},{48,64},{80,96},{32,16},{64,48},{96,80},{17,33},{49,65},{8... | collective-permute-start | bytes 61448 | tf_op jit(solution)/shard_map/ppermute | solution.py:21
  23.0 0.0 collective-permute-done.2.got_first
  23.0 4.3 %collective-permute-done.3.got_second = f32[1,40,128]{2,1,0:T(8,128)S(1)} collective-permute-done((f32[1,40,128]{2,1,0:T(8,128)S(1)}, f32[1,40,128]{2,1,0:T(8,128)S(1)}, u32[]{:S(2)}, u32[]{:S(2)}) %collective-permute-start.3) | collective-permute-done | bytes 20512 | tf_op jit(solution)/shard_map/ppermute | solution.py:21
  27.3 1.0 %ends.1 = (f32[3,40,128]{2,1,0:T(8,128)S(1)}, f32[40,128]{1,0:T(8,128)S(1)}, f32[3,40,128]{2,1,0:T(8,128)S(1)}, f32[3,40,128]{2,1,0:T(8,128)S(1)}, f32[3,3,40,12...) custom-call(f32[3,512,128]{2,1,0:T(8,128)S(1)} %get-tuple-element.40.e,, ...), custom_call_target="tpu_custom_call" | custom-call | tf_op jit(solution)/shard_map/ends/pallas_call | solution.py:598
  28.3 2.0 %collective-permute-start.4 = (f32[7,40,128]{2,1,0:T(8,128)S(1)}, f32[7,40,128]{2,1,0:T(8,128)S(1)}, u32[]{:S(2)}, u32[]{:S(2)}) collective-permute-start(f32[7,40,128]{2,1,0:T(8,128)S(1)} %get-tuple-element.53), channel_id=1, source_target_pairs={{0,1},{2,3},{4,5},{6,7},{8,9},{10,11},{12,13},{14,15},{1,0},{3,2},... | collective-permute-start | bytes 430088 | tf_op jit(solution)/shard_map/ppermute | solution.py:21
  30.4 6.8 %collective-permute-start.5 = (f32[7,40,128]{2,1,0:T(8,128)S(1)}, f32[7,40,128]{2,1,0:T(8,128)S(1)}, u32[]{:S(2)}, u32[]{:S(2)}) collective-permute-start(f32[7,40,128]{2,1,0:T(8,128)S(1)} %get-tuple-element.54), channel_id=1, source_target_pairs={{1,2},{3,4},{5,6},{7,8},{9,10},{11,12},{13,14},{2,1},{4,3},{6,5},{... | collective-permute-start | bytes 430088 | tf_op jit(solution)/shard_map/ppermute | solution.py:21
  37.2 1.8 %middle.1 = (f32[3,16,40,128]{3,2,1,0:T(8,128)S(1)}, f32[3,512,128]{2,1,0:T(8,128)S(1)}, f32[3,512,128]{2,1,0:T(8,128)S(1)}) custom-call(f32[3,512,128]{2,1,0:T(8,128)S(1)} %get-tuple-element.40.e, f32[3,512,128]{2,1,0:T(8,128)S(1)} %get-tuple-element.44.h, f32[3,512,128]{2,1,0:T(8,128)S(1)} %get-tuple-element.45.a, f32[512,128]{1,0:T(8,128)S(1)} %get-tuple-element.41.scale, ...), custom_call_target="tpu_custom_call" | custom-call | tf_op jit(solution)/shard_map/middle/pallas_call | solution.py:598
  39.0 0.0 collective-permute-done.4.got_first
  39.0 1.3 %collective-permute-done.5.got_second = f32[7,40,128]{2,1,0:T(8,128)S(1)} collective-permute-done((f32[7,40,128]{2,1,0:T(8,128)S(1)}, f32[7,40,128]{2,1,0:T(8,128)S(1)}, u32[]{:S(2)}, u32[]{:S(2)}) %collective-permute-start.5) | collective-permute-done | bytes 143392 | tf_op jit(solution)/shard_map/ppermute | solution.py:21
  40.3 2.9 %last.1 = (f32[3,512,128]{2,1,0:T(8,128)}, f32[3,512,128]{2,1,0:T(8,128)}, f32[3,128,128]{2,1,0:T(8,128)}, f32[3,128,128]{2,1,0:T(8,128)}) custom-call(f32[3,512,128]{2,1,0:T(8,128)S(1)} %get-tuple-element.40.e, f32[512,128]{1,0:T(8,128)S(1)} %get-tuple-element.41.scale, f32[10,128,128]{2,1,0:T(8,128)S(1)} %get-tuple-element.46.halo, ...), custom_call_target="tpu_custom_call" | custom-call | tf_op jit(solution)/shard_map/last/pallas_call | solution.py:598
  (1 shorter events, 0.0 us)
Async XLA Ops:
  4.9 6.1 %collective-permute-start = (f32[15,16,128]{2,1,0:T(8,128)S(1)}, f32[15,16,128]{2,1,0:T(8,128)S(1)}, u32[]{:S(2)}, u32[]{:S(2)}) collective-permute-start(f32[15,16,128]{2,1,0:T(8,128)S(1)} %get-tuple-element.42), channel_id=1, source_target_pairs={{0,128},{256,384},{128,0},{384,256},{1,129},{257,385},{129,1},{385... | collective-permute-start | bytes 368648 | tf_op jit(solution)/shard_map/ppermute | solution.py:21
  6.8 6.2 %collective-permute-start.1 = (f32[15,16,128]{2,1,0:T(8,128)S(1)}, f32[15,16,128]{2,1,0:T(8,128)S(1)}, u32[]{:S(2)}, u32[]{:S(2)}) collective-permute-start(f32[15,16,128]{2,1,0:T(8,128)S(1)} %get-tuple-element.43), channel_id=1, source_target_pairs={{128,256},{256,128},{129,257},{257,129},{130,258},{258,130},{131,2... | collective-permute-start | bytes 368648 | tf_op jit(solution)/shard_map/ppermute | solution.py:21
  14.5 8.4 %collective-permute-start.2 = (f32[1,40,128]{2,1,0:T(8,128)S(1)}, f32[1,40,128]{2,1,0:T(8,128)S(1)}, u32[]{:S(2)}, u32[]{:S(2)}) collective-permute-start(f32[1,40,128]{2,1,0:T(8,128)S(1)} %get-tuple-element.51), channel_id=1, source_target_pairs={{0,16},{32,48},{64,80},{96,112},{16,0},{48,32},{80,64},{112,96},{1... | collective-permute-start | bytes 61448 | tf_op jit(solution)/shard_map/ppermute | solution.py:21
  18.0 9.3 %collective-permute-start.3 = (f32[1,40,128]{2,1,0:T(8,128)S(1)}, f32[1,40,128]{2,1,0:T(8,128)S(1)}, u32[]{:S(2)}, u32[]{:S(2)}) collective-permute-start(f32[1,40,128]{2,1,0:T(8,128)S(1)} %get-tuple-element.52), channel_id=1, source_target_pairs={{16,32},{48,64},{80,96},{32,16},{64,48},{96,80},{17,33},{49,65},{8... | collective-permute-start | bytes 61448 | tf_op jit(solution)/shard_map/ppermute | solution.py:21
  28.3 10.7 %collective-permute-start.4 = (f32[7,40,128]{2,1,0:T(8,128)S(1)}, f32[7,40,128]{2,1,0:T(8,128)S(1)}, u32[]{:S(2)}, u32[]{:S(2)}) collective-permute-start(f32[7,40,128]{2,1,0:T(8,128)S(1)} %get-tuple-element.53), channel_id=1, source_target_pairs={{0,1},{2,3},{4,5},{6,7},{8,9},{10,11},{12,13},{14,15},{1,0},{3,2},... | collective-permute-start | bytes 430088 | tf_op jit(solution)/shard_map/ppermute | solution.py:21
  30.4 9.9 %collective-permute-start.5 = (f32[7,40,128]{2,1,0:T(8,128)S(1)}, f32[7,40,128]{2,1,0:T(8,128)S(1)}, u32[]{:S(2)}, u32[]{:S(2)}) collective-permute-start(f32[7,40,128]{2,1,0:T(8,128)S(1)} %get-tuple-element.54), channel_id=1, source_target_pairs={{1,2},{3,4},{5,6},{7,8},{9,10},{11,12},{13,14},{2,1},{4,3},{6,5},{... | collective-permute-start | bytes 430088 | tf_op jit(solution)/shard_map/ppermute | solution.py:21

commit v4 on v3

--- a/solution.py
+++ b/solution.py
@@ -105,14 +105,16 @@
     return jnp.sum(jnp.where(eye, row_ref[...], 0.0), axis=1, keepdims=True)
 
 
-def advance_blocks(e, pitch, cells, inverse, runs, count, decay, restore, drive, pol, cur, pol_out, cur_out, rows, j_rows):
-    slots, width = cells.shape
-    for b in range(slots):
+def gather_rows(e, pitch, runs, rows):
+    for b in range(rows.shape[1]):
         run = runs[0, b]
         at = run + lax.shift_right_logical(run, 5) * (pitch - ROWS)
         for comp in range(3):
             rows[comp, pl.ds(b, 1), :] = e[comp, pl.ds(at, 1), :]
-    j_rows[...] = jnp.zeros_like(j_rows)
+
+
+def advance_blocks(cells, inverse, runs, count, decay, restore, drive, pol, cur, pol_out, cur_out, rows, j_rows):
+    slots, width = cells.shape
     offsets = lax.bitwise_and(cells[...], width - 1)
     down = lax.broadcasted_iota(jnp.int32, (slots, width), 0)
     across = lax.broadcasted_iota(jnp.int32, (slots, width), 1)
@@ -131,6 +133,7 @@
         run = runs[0, b]
         for comp in range(3):
             j_rows[comp, pl.ds(run, 1), :] = rows[comp, pl.ds(b, 1), :]
+    return jnp.where(live, drive_c, 0.0)
 
 
 def spread(value):
@@ -180,16 +183,25 @@
     down = lax.broadcasted_iota(jnp.int32, (slots, width), 0)
     across = lax.broadcasted_iota(jnp.int32, (slots, width), 1)
     lane = lane_ids(8)
+    j_rows[...] = jnp.zeros_like(j_rows)
     copies["cells"].wait()
     run_of = lax.shift_right_logical(cells[...], 7)
     run_row[...] = jnp.sum(jnp.where(down == across, run_of, 0), axis=0, keepdims=True)
     runs_out[...] = run_row[...]
     copy = pltpu.make_async_copy(run_row, runs, sems.at[10])
     copy.start()
-    for row in range(0, slots, 32):
+    def invert(row):
         parts = [lax.bitwise_and(cells[row + 8 * t : row + 8 * t + 8, :], width - 1) for t in range(4)]
         for t, part in enumerate(invert_rows(parts, lane)):
             inverse_out[row + 8 * t : row + 8 * t + 8, :] = part
+
+    for row in range(0, slots // 2, 32):
+        invert(row)
+    copies["e"].wait()
+    copy.wait()
+    gather_rows(e, ROWS, runs, rows)
+    for row in range(slots // 2, slots, 32):
+        invert(row)
     copies["inv_perm"].wait()
     copies["material"].wait()
     table = jnp.zeros((8, width), jnp.float32)
@@ -197,11 +209,10 @@
         table = jnp.where(lane == kind, TIME_STEP * inv_perm[kind], table)
     for row in range(0, material.shape[0], 8):
         scale_out[row : row + 8, :] = jnp.take_along_axis(table, material[row : row + 8, :], axis=1)
-    for name in ("decay", "restore", "drive", "e", "cur", "pol"):
+    for name in ("decay", "restore", "drive", "cur", "pol"):
         copies[name].wait()
-    copy.wait()
     advance_blocks(
-        e, ROWS, cells, inverse_out, runs, count, decay, restore, drive, pol, cur, pol_out, cur_out, rows, j_rows
+        cells, inverse_out, runs, count, decay, restore, drive, pol, cur, pol_out, cur_out, rows, j_rows
     )
     for comp in range(3):
         a_out[comp] = e[comp] - scale_out[...] * j_rows[comp]
@@ -393,7 +404,7 @@
 
 
 def middle_kernel(
-    e, h, a, scale, halo, pe_in, pscale, ph1_in, pe1_in, h1_in, flags,
+    e, h, a, scale, halo, pe_in, pscale, ph1_in, pe1_in, h1_in, e1_in, flags,
     e1_out, h2_out, e2_out, h1, h2,
 ):
     z_at, slot = packed_places()
@@ -423,6 +434,9 @@
         )
         for c in range(3):
             e1_out[c, z] = new[c]
+    for i, z in enumerate(END_E):
+        for c in range(3):
+            e1_out[c, z] = e1_in[c, i]
     ph2 = packed_h(ph1, pe1, packed_factor)
     for z in range(1, 14):
         ez = [e1_out[c, z] for c in range(3)]
@@ -442,10 +456,44 @@
             e2_out[c, z * ROWS : (z + 1) * ROWS, :] = new[c][:ROWS]
 
 
+def blocks_kernel(
+    scale, e1, h2, e2, inverse, runs, cells, count, decay, restore, drive, pol, cur,
+    e_to, h_to, pol_out, cur_out, e_rest, j_rest, gain_out, e_out, rows, j_rows, gain_rows, sems,
+):
+    middle = pl.ds(ROWS, 13 * ROWS)
+    h_copy = pltpu.make_async_copy(h2.at[:, middle, :], h_to.at[:, middle, :], sems.at[0])
+    h_copy.start()
+    gather_rows(e1, EXT, runs, rows)
+    j_rows[...] = jnp.zeros_like(j_rows)
+    gain = advance_blocks(
+        cells, inverse, runs, count, decay, restore, drive, pol, cur, pol_out, cur_out, rows, j_rows
+    )
+    gain_rows[...] = jnp.broadcast_to(gain, gain_rows.shape)
+    gain_out[...] = jnp.zeros_like(gain_out)
+    for b in range(gain_rows.shape[0]):
+        gain_out[pl.ds(runs[0, b], 1), :] = gain_rows[pl.ds(b, 1), :]
+    for c in range(3):
+        for z in range(2, 14):
+            at = slice(z * ROWS, (z + 1) * ROWS)
+            e_out[c, at, :] = e2[c, at, :] - scale[at, :] * j_rows[c, at, :]
+        for i, z in enumerate(END_SLABS):
+            at = slice(z * ROWS, (z + 1) * ROWS)
+            j_rest[c, i] = j_rows[c, at, :]
+        e_rest[c] = e2[c, ROWS : 2 * ROWS, :]
+    most = pl.ds(2 * ROWS, 12 * ROWS)
+    e_copy = pltpu.make_async_copy(e_out.at[:, most, :], e_to.at[:, most, :], sems.at[1])
+    e_copy.start()
+    h_copy.wait()
+    e_copy.wait()
+
+
+END_SLABS = (0, 1, 14, 15)
+
+
 def last_kernel(
-    e, scale, halo, got_first, got_second, flags, pe_in, pscale_in, ph1_in, pe1_in, h1_in, e1_ends, e1_in, h2_in, e2_in,
-    inverse, runs, cells, count, decay, restore, drive, pol, cur,
-    e_to, h_to, pol_to, cur_to, e_out, h_out, pol_out, cur_out, e1, rows, j_rows, sems,
+    e, scale, halo, got_first, got_second, flags, pe_in, pscale_in, ph1_in, pe1_in, h1_in, e1_ends, e1_in, h2_in,
+    e_most, h_most, e_rest, j_rest, gains, runs, cells, pol, cur,
+    e_to, h_to, pol_to, cur_to, e_out, h_out, pol_out, cur_out, late, rows, gain_rows, sems,
 ):
     started = []
 
@@ -456,8 +504,6 @@
 
     even = is_even(flags, 2)
     from_above, from_below = Swapped(even, got_first, got_second), Swapped(even, got_second, got_first)
-    middle = pl.ds(ROWS, 13 * ROWS)
-    send(h2_in.at[:, middle, :], h_to.at[:, middle, :])
     z_at, slot = packed_places()
     factor = row_factor(flags)
     below_factor = factor * flags[2]
@@ -511,11 +557,8 @@
     dx, dy = factor * from_above[5], -(factor * from_above[4])
     h1_top = [h1_in[0, 2] + dx, h1_in[1, 2] + dy, h1_in[2, 2]]
     scale_top = field(9, top)
-    e1_top = [
-        e1_ends[0, 1] - scale_top * dy,
-        e1_ends[1, 1] + scale_top * dx,
-        e1_ends[2, 1] + scale_top * shifted_curl(dx, dy, top),
-    ]
+    late_top = (-(scale_top * dy), scale_top * dx, scale_top * shifted_curl(dx, dy, top))
+    e1_top = [e1_ends[c, 1] + late_top[c] for c in range(3)]
     e1_over = (from_above[1] + from_above[3] * h1_top[1], from_above[2] - from_above[3] * h1_top[0])
     dx, dy = below_factor * field(1, 0), -(below_factor * field(0, 0))
     h1_under = (from_below[1] + dx, from_below[2] + dy)
@@ -526,19 +569,27 @@
         from_below[5] + scale_under * shifted_curl(dx, dy, -1),
     ]
     scale_0 = field(9, 0)
-    e1_0 = [
-        e1_ends[0, 0] + scale_0 * h1_under[1],
-        e1_ends[1, 0] - scale_0 * h1_under[0],
-        e1_ends[2, 0],
-    ]
+    late_0 = (scale_0 * h1_under[1], -(scale_0 * h1_under[0]))
+    e1_0 = [e1_ends[0, 0] + late_0[0], e1_ends[1, 0] + late_0[1], e1_ends[2, 0]]
+
+    late[...] = jnp.zeros_like(late)
     for c in range(3):
-        e1[c, 0:EXT, :] = e1_0[c]
-        e1[c, top * EXT : (top + 1) * EXT, :] = e1_top[c]
-        for z in range(1, top):
-            e1[c, z * EXT : z * EXT + ROWS, :] = e1_in[c, z][:ROWS]
-    advance_blocks(
-        e1, EXT, cells, inverse, runs, count, decay, restore, drive, pol, cur, pol_out, cur_out, rows, j_rows
-    )
+        if c < 2:
+            late[c, 0:ROWS, :] = late_0[c][:ROWS]
+        late[c, ROWS : 2 * ROWS, :] = late_top[c][:ROWS]
+    for b in range(rows.shape[1]):
+        run = runs[0, b]
+        at = jnp.where(run < ROWS, run, jnp.where(run >= top * ROWS, run - (top - 1) * ROWS, 2 * ROWS))
+        gain_rows[pl.ds(b, 1), :] = gains[pl.ds(run, 1), :]
+        for c in range(3):
+            rows[c, pl.ds(b, 1), :] = late[c, pl.ds(at, 1), :]
+    offsets = lax.bitwise_and(cells[...], LANES - 1)
+    for c in range(3):
+        more = gain_rows[...] * jnp.take_along_axis(rows[c], offsets, axis=1)
+        cur_out[c] = cur[c] + more
+        pol_out[c] = pol[c] + TIME_STEP * more
+    send(pol_out, pol_to)
+    send(cur_out, cur_to)
 
     e1_1, e1_14 = ([e1_in[c, z] for c in range(3)] for z in (1, 14))
     under = h_slab(
@@ -560,21 +611,23 @@
             h_out[c, at, :] = value[c][:ROWS]
     send(h_out.at[:, pl.ds(0, ROWS), :], h_to.at[:, pl.ds(0, ROWS), :])
     send(h_out.at[:, pl.ds(ROWS, 2 * ROWS), :], h_to.at[:, pl.ds(14 * ROWS, 2 * ROWS), :])
-    send(pol_out, pol_to)
-    send(cur_out, cur_to)
-    for z in range(SLABS):
+    for i, z in enumerate(END_SLABS):
         at = slice(z * ROWS, (z + 1) * ROWS)
         own_scale = scale[at, :]
         for c in range(3):
-            value = e2[z][c][:ROWS] if z in e2 else e2_in[c, at, :]
+            value = e2[z][c][:ROWS] if z in e2 else e_rest[c]
+            placed = j_rest[c, i]
+            if z == 0 and c < 2:
+                placed = placed + gains[at, :] * late_0[c][:ROWS]
+            if z == top:
+                placed = placed + gains[at, :] * late_top[c][:ROWS]
             if z == 1 and c == 0:
                 value = value + own_scale * h2_0[1][:ROWS]
             if z == 1 and c == 1:
                 value = value - own_scale * h2_0[0][:ROWS]
-            e_out[c, at, :] = value - own_scale * j_rows[c, at, :]
-        if z % 4 == 3:
-            part = pl.ds((z - 3) * ROWS, 4 * ROWS)
-            send(e_out.at[:, part, :], e_to.at[:, part, :])
+            e_out[c, i * ROWS : (i + 1) * ROWS, :] = value - own_scale * placed
+    send(e_out.at[:, pl.ds(0, 2 * ROWS), :], e_to.at[:, pl.ds(0, 2 * ROWS), :])
+    send(e_out.at[:, pl.ds(2 * ROWS, 2 * ROWS), :], e_to.at[:, pl.ds(14 * ROWS, 2 * ROWS), :])
     for copy in started:
         copy.wait()
 
@@ -593,15 +646,14 @@
     def arr(*dims, dtype=f32):
         return jax.ShapeDtypeStruct(dims, dtype)
 
-    def call(kernel, outs, ins, name, scratch=(), in_space=vmem, out_space=vmem):
-        specs = [smem if id(v) in scalars else in_space for v in ins]
+    def call(kernel, outs, ins, name, scratch=(), in_hbm=(), out_hbm=(), aliases={}):
+        specs = [smem if id(v) in scalars else hbm if i in in_hbm else vmem for i, v in enumerate(ins)]
+        ins = [pltpu.with_memory_space_constraint(v, pltpu.HBM) if i in in_hbm else v for i, v in enumerate(ins)]
+        out_specs = [hbm if i in out_hbm else vmem for i in range(len(outs))]
         return pl.pallas_call(
-            kernel, out_shape=outs, in_specs=specs, out_specs=[out_space] * len(outs), scratch_shapes=list(scratch),
-            compiler_params=params, name=name,
+            kernel, out_shape=outs, in_specs=specs, out_specs=out_specs, scratch_shapes=list(scratch),
+            input_output_aliases=aliases, compiler_params=params, name=name,
         )(*ins)
-
-    def in_hbm(value):
-        return pltpu.with_memory_space_constraint(value, pltpu.HBM)
 
     e, h = (v.reshape(3, runs_all, width) for v in (e_field, h_field))
     coefficients = [v.reshape(1, slots) for v in (block_decay, block_restore, block_drive)]
@@ -619,8 +671,8 @@
             arr(len(UP_X), SLABS, width), arr(len(UP_X), SLABS, width),
         ],
         [
-            *(in_hbm(v) for v in (e, h, material.reshape(runs_all, width), inv_permittivity, block_cells)), block_count,
-            *(in_hbm(v) for v in (*coefficients, polarization, current)), flags,
+            e, h, material.reshape(runs_all, width), inv_permittivity, block_cells, block_count, *coefficients,
+            polarization, current, flags,
         ],
         "first",
         [
@@ -628,7 +680,7 @@
             blocks_vmem, flat_vmem, pltpu.VMEM((1, slots), i32), pltpu.SMEM((1, slots), i32),
             pltpu.SemaphoreType.DMA((11,)),
         ],
-        in_space=hbm,
+        in_hbm=(0, 1, 2, 3, 4, 6, 7, 8, 9, 10),
     )
     x_first, x_second = swapped(x_first, "gx", 0), swapped(x_second, "gx", 1)
     (own,) = call(own_kernel, [arr(FIELDS, ROWS, width)], [e, h, a, scale], "own")
@@ -650,24 +702,38 @@
     e1, h2, e2 = call(
         middle_kernel,
         [arr(*slabs), flat, flat],
-        [e, h, a, scale, halo, pe, pscale, ph1, pe1, h1_ends, flags],
+        [e, h, a, scale, halo, pe, pscale, ph1, pe1, h1_ends, e1_ends, flags],
         "middle",
         [pltpu.VMEM(slabs, f32), pltpu.VMEM(slabs, f32)],
     )
     scalars.add(id(runs))
+    dma = pltpu.SemaphoreType.DMA
+    e_most, h_most, pol2, cur2, e_rest, j_rest, gains = call(
+        blocks_kernel,
+        [flat, flat, blocks, blocks, arr(3, ROWS, width), arr(3, len(END_SLABS), ROWS, width), arr(runs_all, width)],
+        [
+            scale, e1.reshape(3, SLABS * EXT, width), h2, e2, inverse, runs, cells, block_count,
+            decay, restore, drive, pol1, cur1,
+        ],
+        "blocks",
+        [flat_vmem, blocks_vmem, flat_vmem, pltpu.VMEM((slots, width), f32), dma((2,))],
+        out_hbm=(0, 1),
+    )
     e_out, h_out, pol2, cur2 = call(
         last_kernel,
         [flat, flat, blocks, blocks],
         [
-            e, scale, halo, z_first, z_second, flags, pe, pscale, ph1, pe1, h1_ends, e1_ends, e1, h2, e2,
-            inverse, runs, cells, block_count, decay, restore, drive, pol1, cur1,
+            e, scale, halo, z_first, z_second, flags, pe, pscale, ph1, pe1, h1_ends, e1_ends, e1, h2,
+            e_most, h_most, e_rest, j_rest, gains, runs, cells, pol2, cur2,
         ],
         "last",
         [
-            flat_vmem, pltpu.VMEM((3, 3 * ROWS, width), f32), blocks_vmem, blocks_vmem,
-            pltpu.VMEM((3, SLABS * EXT, width), f32), blocks_vmem, flat_vmem, pltpu.SemaphoreType.DMA((9,)),
+            pltpu.VMEM((3, 4 * ROWS, width), f32), pltpu.VMEM((3, 3 * ROWS, width), f32), blocks_vmem, blocks_vmem,
+            pltpu.VMEM((3, 2 * ROWS + 8, width), f32), blocks_vmem, pltpu.VMEM((slots, width), f32), dma((6,)),
         ],
-        out_space=hbm,
+        in_hbm=(14, 15),
+        out_hbm=(0, 1, 2, 3),
+        aliases={14: 0, 15: 1},
     )
     return e_out.reshape(shape), h_out.reshape(shape), pol2, cur2
 

time: 43.5 us -> 44.3 us (1.018)
  Pallas kernels: 12 us -> 14.1 us
  waiting for transfers between devices: 7.6 us -> 6.34 us
    pallas_call x6 -> x7, Pallas kernels: 12 us -> 14.1 us  [call(): pl.pallas_call(kernel, out_shape=outs, in_specs=specs, out_specs=out_spec...]
    ppermute x6, waiting for transfers between devices: 7.6 us -> 6.34 us  [swapped(): lax.ppermute(value, axis, pairs + [(upper, lower) for lower, upper in pai...]
  transfers between devices with their start and end apart: 6 -> 6, of which waited for: 3 -> 2; matrix products, arithmetic and copies ran while one was open for 0% -> 0% of each run, Pallas kernels for 7% -> 12%
where the time goes in v4:
time: 44.3 us; the launch traced here: 44 us
  starting transfers between devices  22 us (50%)
  Pallas kernels  14.1 us (32%)
  waiting for transfers between devices  6.34 us (14%)
  between operations  1.43 us (3%)
    ppermute x6, starting transfers between devices, swapped(): lax.ppermute(value, axis, pairs + [(upper, lower) for lower, upper in pai...  22 us
    pallas_call x7, Pallas kernels, call(): pl.pallas_call(kernel, out_shape=outs, in_specs=specs, out_specs=out_spec...  14.1 us
    ppermute x6, waiting for transfers between devices, swapped(): lax.ppermute(value, axis, pairs + [(upper, lower) for lower, upper in pai...  6.34 us
  transfers between devices with their start and end apart: 6, of which 2 were waited for; matrix products, arithmetic and copies ran while one was open for 0% of the time, Pallas kernels for 12%

profile of v4, /device:TPU:102, one launch (start us, length us, event | category | flops | bytes accessed | tf_op | source)
XLA Modules:
  0.0 44.0 jit_solution(13404994097733897815)
XLA Ops:
  1.3 0.1 stack.27
  1.4 3.9 %first.1 = (f32[3,512,128]{2,1,0:T(8,128)S(1)}, f32[3,512,128]{2,1,0:T(8,128)S(1)}, f32[3,128,128]{2,1,0:T(8,128)S(1)}, f32[3,128,128]{2,1,0:T(8,128)S(1)}, f32[...) custom-call(f32[3,512,128]{2,1,0:T(8,128)} %bitcast.18, ...), custom_call_target="tpu_custom_call" | custom-call | tf_op jit(solution)/shard_map/first/pallas_call | solution.py:653
  5.3 1.9 %collective-permute-start = (f32[15,16,128]{2,1,0:T(8,128)S(1)}, f32[15,16,128]{2,1,0:T(8,128)S(1)}, u32[]{:S(2)}, u32[]{:S(2)}) collective-permute-start(f32[15,16,128]{2,1,0:T(8,128)S(1)} %get-tuple-element.49), channel_id=1, source_target_pairs={{0,128},{256,384},{128,0},{384,256},{1,129},{257,385},{129,1},{385... | collective-permute-start | bytes 368648 | tf_op jit(solution)/shard_map/ppermute | solution.py:21
  7.3 2.8 %collective-permute-start.1 = (f32[15,16,128]{2,1,0:T(8,128)S(1)}, f32[15,16,128]{2,1,0:T(8,128)S(1)}, u32[]{:S(2)}, u32[]{:S(2)}) collective-permute-start(f32[15,16,128]{2,1,0:T(8,128)S(1)} %get-tuple-element.50), channel_id=1, source_target_pairs={{128,256},{256,128},{129,257},{257,129},{130,258},{258,130},{131,2... | collective-permute-start | bytes 368648 | tf_op jit(solution)/shard_map/ppermute | solution.py:21
  10.1 1.4 %own.1 = f32[10,32,128]{2,1,0:T(8,128)S(1)} custom-call(f32[3,512,128]{2,1,0:T(8,128)S(1)} %get-tuple-element.47.e, f32[3,512,128]{2,1,0:T(8,128)S(1)} %get-tuple-element.51.h, f32[3,512,128]{2,1,0:T(8,128)S(1)} %get-tuple-element.52.a, f32[512,128]{1,0:T(8,128)S(1)} %get-tuple-element.48.scale), custom_call_target="tpu_custom_call" | custom-call | tf_op jit(solution)/shard_map/own/pallas_call | solution.py:653
  11.5 0.0 collective-permute-done.got_first
  11.5 2.0 %collective-permute-done.1.got_second = f32[15,16,128]{2,1,0:T(8,128)S(1)} collective-permute-done((f32[15,16,128]{2,1,0:T(8,128)S(1)}, f32[15,16,128]{2,1,0:T(8,128)S(1)}, u32[]{:S(2)}, u32[]{:S(2)}) %collective-permute-start.1) | collective-permute-done | bytes 122912 | tf_op jit(solution)/shard_map/ppermute | solution.py:21
  13.5 1.5 %faces.1 = (f32[10,128,128]{2,1,0:T(8,128)S(1)}, f32[3,40,128]{2,1,0:T(8,128)S(1)}, f32[40,128]{1,0:T(8,128)S(1)}, f32[3,40,128]{2,1,0:T(8,128)S(1)}, f32[3,40,1...) custom-call(f32[15,16,128]{2,1,0:T(8,128)S(1)} %collective-permute-done.got_first, ...), custom_call_target="tpu_custom_call" | custom-call | tf_op jit(solution)/shard_map/faces/pallas_call | solution.py:653
  15.0 3.5 %collective-permute-start.2 = (f32[1,40,128]{2,1,0:T(8,128)S(1)}, f32[1,40,128]{2,1,0:T(8,128)S(1)}, u32[]{:S(2)}, u32[]{:S(2)}) collective-permute-start(f32[1,40,128]{2,1,0:T(8,128)S(1)} %get-tuple-element.58), channel_id=1, source_target_pairs={{0,16},{32,48},{64,80},{96,112},{16,0},{48,32},{80,64},{112,96},{1... | collective-permute-start | bytes 61448 | tf_op jit(solution)/shard_map/ppermute | solution.py:21
  18.5 4.9 %collective-permute-start.3 = (f32[1,40,128]{2,1,0:T(8,128)S(1)}, f32[1,40,128]{2,1,0:T(8,128)S(1)}, u32[]{:S(2)}, u32[]{:S(2)}) collective-permute-start(f32[1,40,128]{2,1,0:T(8,128)S(1)} %get-tuple-element.59), channel_id=1, source_target_pairs={{16,32},{48,64},{80,96},{32,16},{64,48},{96,80},{17,33},{49,65},{8... | collective-permute-start | bytes 61448 | tf_op jit(solution)/shard_map/ppermute | solution.py:21
  23.4 0.0 collective-permute-done.2.got_first
  23.4 4.3 %collective-permute-done.3.got_second = f32[1,40,128]{2,1,0:T(8,128)S(1)} collective-permute-done((f32[1,40,128]{2,1,0:T(8,128)S(1)}, f32[1,40,128]{2,1,0:T(8,128)S(1)}, u32[]{:S(2)}, u32[]{:S(2)}) %collective-permute-start.3) | collective-permute-done | bytes 20512 | tf_op jit(solution)/shard_map/ppermute | solution.py:21
  27.7 1.0 %ends.1 = (f32[3,40,128]{2,1,0:T(8,128)S(1)}, f32[40,128]{1,0:T(8,128)S(1)}, f32[3,40,128]{2,1,0:T(8,128)S(1)}, f32[3,40,128]{2,1,0:T(8,128)S(1)}, f32[3,3,40,12...) custom-call(f32[3,512,128]{2,1,0:T(8,128)S(1)} %get-tuple-element.47.e,, ...), custom_call_target="tpu_custom_call" | custom-call | tf_op jit(solution)/shard_map/ends/pallas_call | solution.py:653
  28.8 2.0 %collective-permute-start.4 = (f32[7,40,128]{2,1,0:T(8,128)S(1)}, f32[7,40,128]{2,1,0:T(8,128)S(1)}, u32[]{:S(2)}, u32[]{:S(2)}) collective-permute-start(f32[7,40,128]{2,1,0:T(8,128)S(1)} %get-tuple-element.60), channel_id=1, source_target_pairs={{0,1},{2,3},{4,5},{6,7},{8,9},{10,11},{12,13},{14,15},{1,0},{3,2},... | collective-permute-start | bytes 430088 | tf_op jit(solution)/shard_map/ppermute | solution.py:21
  30.8 6.8 %collective-permute-start.5 = (f32[7,40,128]{2,1,0:T(8,128)S(1)}, f32[7,40,128]{2,1,0:T(8,128)S(1)}, u32[]{:S(2)}, u32[]{:S(2)}) collective-permute-start(f32[7,40,128]{2,1,0:T(8,128)S(1)} %get-tuple-element.61), channel_id=1, source_target_pairs={{1,2},{3,4},{5,6},{7,8},{9,10},{11,12},{13,14},{2,1},{4,3},{6,5},{... | collective-permute-start | bytes 430088 | tf_op jit(solution)/shard_map/ppermute | solution.py:21
  37.7 1.8 %middle.1 = (f32[3,16,40,128]{3,2,1,0:T(8,128)S(1)}, f32[3,512,128]{2,1,0:T(8,128)S(1)}, f32[3,512,128]{2,1,0:T(8,128)S(1)}) custom-call(f32[3,512,128]{2,1,0:T(8,128)S(1)} %get-tuple-element.47.e, f32[3,512,128]{2,1,0:T(8,128)S(1)} %get-tuple-element.51.h, f32[3,512,128]{2,1,0:T(8,128)S(1)} %get-tuple-element.52.a, f32[512,128]{1,0:T(8,128)S(1)} %get-tuple-element.48.scale, ...), custom_call_target="tpu_custom_call" | custom-call | tf_op jit(solution)/shard_map/middle/pallas_call | solution.py:653
  39.5 2.2 %blocks.1 = (f32[3,512,128]{2,1,0:T(8,128)}, f32[3,512,128]{2,1,0:T(8,128)}, f32[3,128,128]{2,1,0:T(8,128)S(1)}, f32[3,128,128]{2,1,0:T(8,128)S(1)}, f32[3,32,12...) custom-call(f32[512,128]{1,0:T(8,128)S(1)} %get-tuple-element.48.scale, ...), custom_call_target="tpu_custom_call" | custom-call | tf_op jit(solution)/shard_map/blocks/pallas_call | solution.py:653
  41.7 0.0 collective-permute-done.4.got_first
  41.7 0.0 collective-permute-done.5.got_second
  41.7 2.3 %last.1 = (f32[3,512,128]{2,1,0:T(8,128)}, f32[3,512,128]{2,1,0:T(8,128)}, f32[3,128,128]{2,1,0:T(8,128)}, f32[3,128,128]{2,1,0:T(8,128)}) custom-call(f32[3,512,128]{2,1,0:T(8,128)S(1)} %get-tuple-element.47.e, f32[512,128]{1,0:T(8,128)S(1)} %get-tuple-element.48.scale, ...), custom_call_target="tpu_custom_call", output_to_operand_aliasing={{0}: (14, {}), {1}: (15, {})} | custom-call | tf_op jit(solution)/shard_map/last/pallas_call | solution.py:653
  (1 shorter events, 0.0 us)
Async XLA Ops:
  5.3 6.1 %collective-permute-start = (f32[15,16,128]{2,1,0:T(8,128)S(1)}, f32[15,16,128]{2,1,0:T(8,128)S(1)}, u32[]{:S(2)}, u32[]{:S(2)}) collective-permute-start(f32[15,16,128]{2,1,0:T(8,128)S(1)} %get-tuple-element.49), channel_id=1, source_target_pairs={{0,128},{256,384},{128,0},{384,256},{1,129},{257,385},{129,1},{385... | collective-permute-start | bytes 368648 | tf_op jit(solution)/shard_map/ppermute | solution.py:21
  7.3 6.2 %collective-permute-start.1 = (f32[15,16,128]{2,1,0:T(8,128)S(1)}, f32[15,16,128]{2,1,0:T(8,128)S(1)}, u32[]{:S(2)}, u32[]{:S(2)}) collective-permute-start(f32[15,16,128]{2,1,0:T(8,128)S(1)} %get-tuple-element.50), channel_id=1, source_target_pairs={{128,256},{256,128},{129,257},{257,129},{130,258},{258,130},{131,2... | collective-permute-start | bytes 368648 | tf_op jit(solution)/shard_map/ppermute | solution.py:21
  15.0 8.4 %collective-permute-start.2 = (f32[1,40,128]{2,1,0:T(8,128)S(1)}, f32[1,40,128]{2,1,0:T(8,128)S(1)}, u32[]{:S(2)}, u32[]{:S(2)}) collective-permute-start(f32[1,40,128]{2,1,0:T(8,128)S(1)} %get-tuple-element.58), channel_id=1, source_target_pairs={{0,16},{32,48},{64,80},{96,112},{16,0},{48,32},{80,64},{112,96},{1... | collective-permute-start | bytes 61448 | tf_op jit(solution)/shard_map/ppermute | solution.py:21
  18.5 9.3 %collective-permute-start.3 = (f32[1,40,128]{2,1,0:T(8,128)S(1)}, f32[1,40,128]{2,1,0:T(8,128)S(1)}, u32[]{:S(2)}, u32[]{:S(2)}) collective-permute-start(f32[1,40,128]{2,1,0:T(8,128)S(1)} %get-tuple-element.59), channel_id=1, source_target_pairs={{16,32},{48,64},{80,96},{32,16},{64,48},{96,80},{17,33},{49,65},{8... | collective-permute-start | bytes 61448 | tf_op jit(solution)/shard_map/ppermute | solution.py:21
  28.8 12.9 %collective-permute-start.4 = (f32[7,40,128]{2,1,0:T(8,128)S(1)}, f32[7,40,128]{2,1,0:T(8,128)S(1)}, u32[]{:S(2)}, u32[]{:S(2)}) collective-permute-start(f32[7,40,128]{2,1,0:T(8,128)S(1)} %get-tuple-element.60), channel_id=1, source_target_pairs={{0,1},{2,3},{4,5},{6,7},{8,9},{10,11},{12,13},{14,15},{1,0},{3,2},... | collective-permute-start | bytes 430088 | tf_op jit(solution)/shard_map/ppermute | solution.py:21
  30.8 10.9 %collective-permute-start.5 = (f32[7,40,128]{2,1,0:T(8,128)S(1)}, f32[7,40,128]{2,1,0:T(8,128)S(1)}, u32[]{:S(2)}, u32[]{:S(2)}) collective-permute-start(f32[7,40,128]{2,1,0:T(8,128)S(1)} %get-tuple-element.61), channel_id=1, source_target_pairs={{1,2},{3,4},{5,6},{7,8},{9,10},{11,12},{13,14},{2,1},{4,3},{6,5},{... | collective-permute-start | bytes 430088 | tf_op jit(solution)/shard_map/ppermute | solution.py:21

commit v5 on v4

--- a/solution.py
+++ b/solution.py
@@ -190,18 +190,11 @@
     runs_out[...] = run_row[...]
     copy = pltpu.make_async_copy(run_row, runs, sems.at[10])
     copy.start()
-    def invert(row):
+    for row in range(0, slots, 32):
         parts = [lax.bitwise_and(cells[row + 8 * t : row + 8 * t + 8, :], width - 1) for t in range(4)]
         for t, part in enumerate(invert_rows(parts, lane)):
             inverse_out[row + 8 * t : row + 8 * t + 8, :] = part
 
-    for row in range(0, slots // 2, 32):
-        invert(row)
-    copies["e"].wait()
-    copy.wait()
-    gather_rows(e, ROWS, runs, rows)
-    for row in range(slots // 2, slots, 32):
-        invert(row)
     copies["inv_perm"].wait()
     copies["material"].wait()
     table = jnp.zeros((8, width), jnp.float32)
@@ -209,8 +202,10 @@
         table = jnp.where(lane == kind, TIME_STEP * inv_perm[kind], table)
     for row in range(0, material.shape[0], 8):
         scale_out[row : row + 8, :] = jnp.take_along_axis(table, material[row : row + 8, :], axis=1)
-    for name in ("decay", "restore", "drive", "cur", "pol"):
+    for name in ("decay", "restore", "drive", "e", "cur", "pol"):
         copies[name].wait()
+    copy.wait()
+    gather_rows(e, ROWS, runs, rows)
     advance_blocks(
         cells, inverse_out, runs, count, decay, restore, drive, pol, cur, pol_out, cur_out, rows, j_rows
     )
@@ -262,7 +257,7 @@
 DOWN_H1Y = 1
 
 
-def faces_kernel(got_first, got_second, own, flags, halo_out, pe_out, pscale_out, ph1_out, pe1_out, up_out, down_out):
+def faces_kernel(got_second, got_first, own, flags, halo_out, pe_out, pscale_out, ph1_out, pe1_out, up_out, down_out):
     even = is_even(flags, 0)
     from_above, from_below = Swapped(even, got_first, got_second), Swapped(even, got_second, got_first)
     halo_out[...] = jnp.zeros_like(halo_out)
@@ -324,7 +319,7 @@
 
 
 def ends_kernel(
-    e, h, a, scale, halo, pe_in, pscale_in, ph1_in, pe1_in, got_first, got_second, flags,
+    e, h, a, scale, halo, pe_in, pscale_in, ph1_in, pe1_in, got_second, got_first, flags,
     pe_out, pscale_out, ph1_out, pe1_out, h1_out, e1_out, up_out, down_out,
 ):
     z_at, slot = packed_places()
@@ -457,12 +452,9 @@
 
 
 def blocks_kernel(
-    scale, e1, h2, e2, inverse, runs, cells, count, decay, restore, drive, pol, cur,
-    e_to, h_to, pol_out, cur_out, e_rest, j_rest, gain_out, e_out, rows, j_rows, gain_rows, sems,
+    scale, e1, e2, inverse, runs, cells, count, decay, restore, drive, pol, cur,
+    e_most, pol_out, cur_out, j_rest, gain_out, rows, j_rows, gain_rows,
 ):
-    middle = pl.ds(ROWS, 13 * ROWS)
-    h_copy = pltpu.make_async_copy(h2.at[:, middle, :], h_to.at[:, middle, :], sems.at[0])
-    h_copy.start()
     gather_rows(e1, EXT, runs, rows)
     j_rows[...] = jnp.zeros_like(j_rows)
     gain = advance_blocks(
@@ -475,24 +467,18 @@
     for c in range(3):
         for z in range(2, 14):
             at = slice(z * ROWS, (z + 1) * ROWS)
-            e_out[c, at, :] = e2[c, at, :] - scale[at, :] * j_rows[c, at, :]
+            e_most[c, (z - 2) * ROWS : (z - 1) * ROWS, :] = e2[c, at, :] - scale[at, :] * j_rows[c, at, :]
         for i, z in enumerate(END_SLABS):
             at = slice(z * ROWS, (z + 1) * ROWS)
             j_rest[c, i] = j_rows[c, at, :]
-        e_rest[c] = e2[c, ROWS : 2 * ROWS, :]
-    most = pl.ds(2 * ROWS, 12 * ROWS)
-    e_copy = pltpu.make_async_copy(e_out.at[:, most, :], e_to.at[:, most, :], sems.at[1])
-    e_copy.start()
-    h_copy.wait()
-    e_copy.wait()
 
 
 END_SLABS = (0, 1, 14, 15)
 
 
 def last_kernel(
-    e, scale, halo, got_first, got_second, flags, pe_in, pscale_in, ph1_in, pe1_in, h1_in, e1_ends, e1_in, h2_in,
-    e_most, h_most, e_rest, j_rest, gains, runs, cells, pol, cur,
+    e, scale, halo, got_first, got_second, flags, pe_in, pscale_in, ph1_in, pe1_in, h1_in, e1_ends, e1_in, h2_in, e2_in,
+    e_most, j_rest, gains, runs, cells, pol, cur,
     e_to, h_to, pol_to, cur_to, e_out, h_out, pol_out, cur_out, late, rows, gain_rows, sems,
 ):
     started = []
@@ -502,6 +488,8 @@
         copy.start()
         started.append(copy)
 
+    send(h2_in.at[:, pl.ds(ROWS, 13 * ROWS), :], h_to.at[:, pl.ds(ROWS, 13 * ROWS), :])
+    send(e_most, e_to.at[:, pl.ds(2 * ROWS, 12 * ROWS), :])
     even = is_even(flags, 2)
     from_above, from_below = Swapped(even, got_first, got_second), Swapped(even, got_second, got_first)
     z_at, slot = packed_places()
@@ -615,7 +603,7 @@
         at = slice(z * ROWS, (z + 1) * ROWS)
         own_scale = scale[at, :]
         for c in range(3):
-            value = e2[z][c][:ROWS] if z in e2 else e_rest[c]
+            value = e2[z][c][:ROWS] if z in e2 else e2_in[c, at, :]
             placed = j_rest[c, i]
             if z == 0 and c < 2:
                 placed = placed + gains[at, :] * late_0[c][:ROWS]
@@ -646,13 +634,13 @@
     def arr(*dims, dtype=f32):
         return jax.ShapeDtypeStruct(dims, dtype)
 
-    def call(kernel, outs, ins, name, scratch=(), in_hbm=(), out_hbm=(), aliases={}):
+    def call(kernel, outs, ins, name, scratch=(), in_hbm=(), out_hbm=()):
         specs = [smem if id(v) in scalars else hbm if i in in_hbm else vmem for i, v in enumerate(ins)]
         ins = [pltpu.with_memory_space_constraint(v, pltpu.HBM) if i in in_hbm else v for i, v in enumerate(ins)]
         out_specs = [hbm if i in out_hbm else vmem for i in range(len(outs))]
         return pl.pallas_call(
             kernel, out_shape=outs, in_specs=specs, out_specs=out_specs, scratch_shapes=list(scratch),
-            input_output_aliases=aliases, compiler_params=params, name=name,
+            compiler_params=params, name=name,
         )(*ins)
 
     e, h = (v.reshape(3, runs_all, width) for v in (e_field, h_field))
@@ -682,19 +670,21 @@
         ],
         in_hbm=(0, 1, 2, 3, 4, 6, 7, 8, 9, 10),
     )
-    x_first, x_second = swapped(x_first, "gx", 0), swapped(x_second, "gx", 1)
+    x_second = swapped(x_second, "gx", 1)
+    x_first = swapped(x_first, "gx", 0)
     (own,) = call(own_kernel, [arr(FIELDS, ROWS, width)], [e, h, a, scale], "own")
     halo, pe, pscale, ph1, pe1, y_first, y_second = call(
         faces_kernel,
         [arr(FIELDS, SLABS * HALO, width), ext, tile, ext, ext, arr(1, EXT, width), arr(1, EXT, width)],
-        [x_first, x_second, own, flags],
+        [x_second, x_first, own, flags],
         "faces",
     )
-    y_first, y_second = swapped(y_first, "gy", 0), swapped(y_second, "gy", 1)
+    y_second = swapped(y_second, "gy", 1)
+    y_first = swapped(y_first, "gy", 0)
     pe, pscale, ph1, pe1, h1_ends, e1_ends, z_first, z_second = call(
         ends_kernel,
         [ext, tile, ext, ext, arr(3, 3, EXT, width), arr(3, 2, EXT, width), arr(7, EXT, width), arr(7, EXT, width)],
-        [e, h, a, scale, halo, pe, pscale, ph1, pe1, y_first, y_second, flags],
+        [e, h, a, scale, halo, pe, pscale, ph1, pe1, y_second, y_first, flags],
         "ends",
     )
     z_first, z_second = swapped(z_first, "gz", 0), swapped(z_second, "gz", 1)
@@ -708,32 +698,30 @@
     )
     scalars.add(id(runs))
     dma = pltpu.SemaphoreType.DMA
-    e_most, h_most, pol2, cur2, e_rest, j_rest, gains = call(
+    e_most, pol2, cur2, j_rest, gains = call(
         blocks_kernel,
-        [flat, flat, blocks, blocks, arr(3, ROWS, width), arr(3, len(END_SLABS), ROWS, width), arr(runs_all, width)],
+        [arr(3, 12 * ROWS, width), blocks, blocks, arr(3, len(END_SLABS), ROWS, width), arr(runs_all, width)],
         [
-            scale, e1.reshape(3, SLABS * EXT, width), h2, e2, inverse, runs, cells, block_count,
+            scale, e1.reshape(3, SLABS * EXT, width), e2, inverse, runs, cells, block_count,
             decay, restore, drive, pol1, cur1,
         ],
         "blocks",
-        [flat_vmem, blocks_vmem, flat_vmem, pltpu.VMEM((slots, width), f32), dma((2,))],
-        out_hbm=(0, 1),
+        [blocks_vmem, flat_vmem, pltpu.VMEM((slots, width), f32)],
     )
     e_out, h_out, pol2, cur2 = call(
         last_kernel,
         [flat, flat, blocks, blocks],
         [
-            e, scale, halo, z_first, z_second, flags, pe, pscale, ph1, pe1, h1_ends, e1_ends, e1, h2,
-            e_most, h_most, e_rest, j_rest, gains, runs, cells, pol2, cur2,
+            e, scale, halo, z_first, z_second, flags, pe, pscale, ph1, pe1, h1_ends, e1_ends, e1, h2, e2,
+            e_most, j_rest, gains, runs, cells, pol2, cur2,
         ],
         "last",
         [
             pltpu.VMEM((3, 4 * ROWS, width), f32), pltpu.VMEM((3, 3 * ROWS, width), f32), blocks_vmem, blocks_vmem,
-            pltpu.VMEM((3, 2 * ROWS + 8, width), f32), blocks_vmem, pltpu.VMEM((slots, width), f32), dma((6,)),
+            pltpu.VMEM((3, 2 * ROWS + 8, width), f32), blocks_vmem, pltpu.VMEM((slots, width), f32),
+            pltpu.SemaphoreType.DMA((8,)),
         ],
-        in_hbm=(14, 15),
         out_hbm=(0, 1, 2, 3),
-        aliases={14: 0, 15: 1},
     )
     return e_out.reshape(shape), h_out.reshape(shape), pol2, cur2
 

time: 44.3 us -> 40.1 us (0.905)
  waiting for transfers between devices: 6.34 us -> 4.49 us
  starting transfers between devices: 22 us -> 20.6 us
  Pallas kernels: 14.1 us -> 13.2 us
    ppermute x6, waiting for transfers between devices: 6.34 us -> 4.49 us  [swapped(): lax.ppermute(value, axis, pairs + [(upper, lower) for lower, upper in pai...]
    ppermute x6, starting transfers between devices: 22 us -> 20.6 us  [swapped(): lax.ppermute(value, axis, pairs + [(upper, lower) for lower, upper in pai...]
    pallas_call x7, Pallas kernels: 14.1 us -> 13.2 us  [call(): pl.pallas_call(kernel, out_shape=outs, in_specs=specs, out_specs=out_spec...]
  transfers between devices with their start and end apart: 6 -> 6, of which waited for: 2 -> 3; matrix products, arithmetic and copies ran while one was open for 0% -> 0% of each run, Pallas kernels for 12% -> 11%
where the time goes in v5:
time: 40.1 us; the launch traced here: 39.8 us
  starting transfers between devices  20.6 us (51%)
  Pallas kernels  13.2 us (33%)
  waiting for transfers between devices  4.49 us (11%)
  between operations  1.41 us (4%)
    ppermute x6, starting transfers between devices, swapped(): lax.ppermute(value, axis, pairs + [(upper, lower) for lower, upper in pai...  20.6 us
    pallas_call x7, Pallas kernels, call(): pl.pallas_call(kernel, out_shape=outs, in_specs=specs, out_specs=out_spec...  13.2 us
    ppermute x6, waiting for transfers between devices, swapped(): lax.ppermute(value, axis, pairs + [(upper, lower) for lower, upper in pai...  4.49 us
  transfers between devices with their start and end apart: 6, of which 3 were waited for; matrix products, arithmetic and copies ran while one was open for 0% of the time, Pallas kernels for 11%

profile of v5, /device:TPU:102, one launch (start us, length us, event | category | flops | bytes accessed | tf_op | source)
XLA Modules:
  0.0 39.8 jit_solution(9238370005921578548)
XLA Ops:
  1.3 0.1 stack.27
  1.4 3.4 %first.1 = (f32[3,512,128]{2,1,0:T(8,128)S(1)}, f32[3,512,128]{2,1,0:T(8,128)S(1)}, f32[3,128,128]{2,1,0:T(8,128)S(1)}, f32[3,128,128]{2,1,0:T(8,128)S(1)}, f32[...) custom-call(f32[3,512,128]{2,1,0:T(8,128)} %bitcast.16, ...), custom_call_target="tpu_custom_call" | custom-call | tf_op jit(solution)/shard_map/first/pallas_call | solution.py:641
  4.9 2.2 %collective-permute-start = (f32[15,16,128]{2,1,0:T(8,128)S(1)}, f32[15,16,128]{2,1,0:T(8,128)S(1)}, u32[]{:S(2)}, u32[]{:S(2)}) collective-permute-start(f32[15,16,128]{2,1,0:T(8,128)S(1)} %get-tuple-element.47), channel_id=1, source_target_pairs={{128,256},{256,128},{129,257},{257,129},{130,258},{258,130},{131,2... | collective-permute-start | bytes 368648 | tf_op jit(solution)/shard_map/ppermute | solution.py:21
  7.1 1.9 %collective-permute-start.1 = (f32[15,16,128]{2,1,0:T(8,128)S(1)}, f32[15,16,128]{2,1,0:T(8,128)S(1)}, u32[]{:S(2)}, u32[]{:S(2)}) collective-permute-start(f32[15,16,128]{2,1,0:T(8,128)S(1)} %get-tuple-element.48), channel_id=1, source_target_pairs={{0,128},{256,384},{128,0},{384,256},{1,129},{257,385},{129,1},{385... | collective-permute-start | bytes 368648 | tf_op jit(solution)/shard_map/ppermute | solution.py:21
  9.0 1.4 %own.1 = f32[10,32,128]{2,1,0:T(8,128)S(1)} custom-call(f32[3,512,128]{2,1,0:T(8,128)S(1)} %get-tuple-element.45.e, f32[3,512,128]{2,1,0:T(8,128)S(1)} %get-tuple-element.49.h, f32[3,512,128]{2,1,0:T(8,128)S(1)} %get-tuple-element.50.a, f32[512,128]{1,0:T(8,128)S(1)} %get-tuple-element.46.scale), custom_call_target="tpu_custom_call" | custom-call | tf_op jit(solution)/shard_map/own/pallas_call | solution.py:641
  10.3 0.7 %collective-permute-done.got_second = f32[15,16,128]{2,1,0:T(8,128)S(1)} collective-permute-done((f32[15,16,128]{2,1,0:T(8,128)S(1)}, f32[15,16,128]{2,1,0:T(8,128)S(1)}, u32[]{:S(2)}, u32[]{:S(2)}) %collective-permute-start) | collective-permute-done | bytes 122912 | tf_op jit(solution)/shard_map/ppermute | solution.py:21
  11.1 0.0 collective-permute-done.1.got_first
  11.1 1.5 %faces.1 = (f32[10,128,128]{2,1,0:T(8,128)S(1)}, f32[3,40,128]{2,1,0:T(8,128)S(1)}, f32[40,128]{1,0:T(8,128)S(1)}, f32[3,40,128]{2,1,0:T(8,128)S(1)}, f32[3,40,1...) custom-call(f32[15,16,128]{2,1,0:T(8,128)S(1)} %collective-permute-done.got_second, ...), custom_call_target="tpu_custom_call" | custom-call | tf_op jit(solution)/shard_map/faces/pallas_call | solution.py:641
  12.6 5.8 %collective-permute-start.2 = (f32[1,40,128]{2,1,0:T(8,128)S(1)}, f32[1,40,128]{2,1,0:T(8,128)S(1)}, u32[]{:S(2)}, u32[]{:S(2)}) collective-permute-start(f32[1,40,128]{2,1,0:T(8,128)S(1)} %get-tuple-element.56), channel_id=1, source_target_pairs={{16,32},{48,64},{80,96},{32,16},{64,48},{96,80},{17,33},{49,65},{8... | collective-permute-start | bytes 61448 | tf_op jit(solution)/shard_map/ppermute | solution.py:21
  18.3 1.9 %collective-permute-start.3 = (f32[1,40,128]{2,1,0:T(8,128)S(1)}, f32[1,40,128]{2,1,0:T(8,128)S(1)}, u32[]{:S(2)}, u32[]{:S(2)}) collective-permute-start(f32[1,40,128]{2,1,0:T(8,128)S(1)} %get-tuple-element.57), channel_id=1, source_target_pairs={{0,16},{32,48},{64,80},{96,112},{16,0},{48,32},{80,64},{112,96},{1... | collective-permute-start | bytes 61448 | tf_op jit(solution)/shard_map/ppermute | solution.py:21
  20.3 1.6 %collective-permute-done.2.got_second = f32[1,40,128]{2,1,0:T(8,128)S(1)} collective-permute-done((f32[1,40,128]{2,1,0:T(8,128)S(1)}, f32[1,40,128]{2,1,0:T(8,128)S(1)}, u32[]{:S(2)}, u32[]{:S(2)}) %collective-permute-start.2) | collective-permute-done | bytes 20512 | tf_op jit(solution)/shard_map/ppermute | solution.py:21
  21.9 2.2 %collective-permute-done.3.got_first = f32[1,40,128]{2,1,0:T(8,128)S(1)} collective-permute-done((f32[1,40,128]{2,1,0:T(8,128)S(1)}, f32[1,40,128]{2,1,0:T(8,128)S(1)}, u32[]{:S(2)}, u32[]{:S(2)}) %collective-permute-start.3) | collective-permute-done | bytes 20512 | tf_op jit(solution)/shard_map/ppermute | solution.py:21
  24.0 1.0 %ends.1 = (f32[3,40,128]{2,1,0:T(8,128)S(1)}, f32[40,128]{1,0:T(8,128)S(1)}, f32[3,40,128]{2,1,0:T(8,128)S(1)}, f32[3,40,128]{2,1,0:T(8,128)S(1)}, f32[3,3,40,12...) custom-call(f32[3,512,128]{2,1,0:T(8,128)S(1)} %get-tuple-element.45.e,, ...), custom_call_target="tpu_custom_call" | custom-call | tf_op jit(solution)/shard_map/ends/pallas_call | solution.py:641
  25.0 2.0 %collective-permute-start.4 = (f32[7,40,128]{2,1,0:T(8,128)S(1)}, f32[7,40,128]{2,1,0:T(8,128)S(1)}, u32[]{:S(2)}, u32[]{:S(2)}) collective-permute-start(f32[7,40,128]{2,1,0:T(8,128)S(1)} %get-tuple-element.58), channel_id=1, source_target_pairs={{0,1},{2,3},{4,5},{6,7},{8,9},{10,11},{12,13},{14,15},{1,0},{3,2},... | collective-permute-start | bytes 430088 | tf_op jit(solution)/shard_map/ppermute | solution.py:21
  27.1 6.8 %collective-permute-start.5 = (f32[7,40,128]{2,1,0:T(8,128)S(1)}, f32[7,40,128]{2,1,0:T(8,128)S(1)}, u32[]{:S(2)}, u32[]{:S(2)}) collective-permute-start(f32[7,40,128]{2,1,0:T(8,128)S(1)} %get-tuple-element.59), channel_id=1, source_target_pairs={{1,2},{3,4},{5,6},{7,8},{9,10},{11,12},{13,14},{2,1},{4,3},{6,5},{... | collective-permute-start | bytes 430088 | tf_op jit(solution)/shard_map/ppermute | solution.py:21
  33.9 1.8 %middle.1 = (f32[3,16,40,128]{3,2,1,0:T(8,128)S(1)}, f32[3,512,128]{2,1,0:T(8,128)S(1)}, f32[3,512,128]{2,1,0:T(8,128)S(1)}) custom-call(f32[3,512,128]{2,1,0:T(8,128)S(1)} %get-tuple-element.45.e, f32[3,512,128]{2,1,0:T(8,128)S(1)} %get-tuple-element.49.h, f32[3,512,128]{2,1,0:T(8,128)S(1)} %get-tuple-element.50.a, f32[512,128]{1,0:T(8,128)S(1)} %get-tuple-element.46.scale, ...), custom_call_target="tpu_custom_call" | custom-call | tf_op jit(solution)/shard_map/middle/pallas_call | solution.py:641
  35.7 1.4 %blocks.1 = (f32[3,384,128]{2,1,0:T(8,128)S(1)}, f32[3,128,128]{2,1,0:T(8,128)S(1)}, f32[3,128,128]{2,1,0:T(8,128)S(1)}, f32[3,4,32,128]{3,2,1,0:T(8,128)S(1)}, f32[512,128]{1,0:T(8,128)S(1)}) custom-call(f32[512,128]{1,0:T(8,128)S(1)} %get-tuple-element.46.scale, f32[3,640,128]{2,1,0:T(8,128)S(1)} %bitcast.15, ...), custom_call_target="tpu_custom_call" | custom-call | tf_op jit(solution)/shard_map/blocks/pallas_call | solution.py:641
  37.1 0.0 collective-permute-done.4.got_first
  37.1 0.0 collective-permute-done.5.got_second
  37.1 2.7 %last.1 = (f32[3,512,128]{2,1,0:T(8,128)}, f32[3,512,128]{2,1,0:T(8,128)}, f32[3,128,128]{2,1,0:T(8,128)}, f32[3,128,128]{2,1,0:T(8,128)}) custom-call(f32[3,512,128]{2,1,0:T(8,128)S(1)} %get-tuple-element.45.e, f32[512,128]{1,0:T(8,128)S(1)} %get-tuple-element.46.scale, f32[10,128,128]{2,1,0:T(8,128)S(1)} %get-tuple-element.51.halo, ...), custom_call_target="tpu_custom_call" | custom-call | tf_op jit(solution)/shard_map/last/pallas_call | solution.py:641
  (1 shorter events, 0.0 us)
Async XLA Ops:
  4.9 6.2 %collective-permute-start = (f32[15,16,128]{2,1,0:T(8,128)S(1)}, f32[15,16,128]{2,1,0:T(8,128)S(1)}, u32[]{:S(2)}, u32[]{:S(2)}) collective-permute-start(f32[15,16,128]{2,1,0:T(8,128)S(1)} %get-tuple-element.47), channel_id=1, source_target_pairs={{128,256},{256,128},{129,257},{257,129},{130,258},{258,130},{131,2... | collective-permute-start | bytes 368648 | tf_op jit(solution)/shard_map/ppermute | solution.py:21
  7.1 4.0 %collective-permute-start.1 = (f32[15,16,128]{2,1,0:T(8,128)S(1)}, f32[15,16,128]{2,1,0:T(8,128)S(1)}, u32[]{:S(2)}, u32[]{:S(2)}) collective-permute-start(f32[15,16,128]{2,1,0:T(8,128)S(1)} %get-tuple-element.48), channel_id=1, source_target_pairs={{0,128},{256,384},{128,0},{384,256},{1,129},{257,385},{129,1},{385... | collective-permute-start | bytes 368648 | tf_op jit(solution)/shard_map/ppermute | solution.py:21
  12.6 9.3 %collective-permute-start.2 = (f32[1,40,128]{2,1,0:T(8,128)S(1)}, f32[1,40,128]{2,1,0:T(8,128)S(1)}, u32[]{:S(2)}, u32[]{:S(2)}) collective-permute-start(f32[1,40,128]{2,1,0:T(8,128)S(1)} %get-tuple-element.56), channel_id=1, source_target_pairs={{16,32},{48,64},{80,96},{32,16},{64,48},{96,80},{17,33},{49,65},{8... | collective-permute-start | bytes 61448 | tf_op jit(solution)/shard_map/ppermute | solution.py:21
  18.3 5.7 %collective-permute-start.3 = (f32[1,40,128]{2,1,0:T(8,128)S(1)}, f32[1,40,128]{2,1,0:T(8,128)S(1)}, u32[]{:S(2)}, u32[]{:S(2)}) collective-permute-start(f32[1,40,128]{2,1,0:T(8,128)S(1)} %get-tuple-element.57), channel_id=1, source_target_pairs={{0,16},{32,48},{64,80},{96,112},{16,0},{48,32},{80,64},{112,96},{1... | collective-permute-start | bytes 61448 | tf_op jit(solution)/shard_map/ppermute | solution.py:21
  25.0 12.0 %collective-permute-start.4 = (f32[7,40,128]{2,1,0:T(8,128)S(1)}, f32[7,40,128]{2,1,0:T(8,128)S(1)}, u32[]{:S(2)}, u32[]{:S(2)}) collective-permute-start(f32[7,40,128]{2,1,0:T(8,128)S(1)} %get-tuple-element.58), channel_id=1, source_target_pairs={{0,1},{2,3},{4,5},{6,7},{8,9},{10,11},{12,13},{14,15},{1,0},{3,2},... | collective-permute-start | bytes 430088 | tf_op jit(solution)/shard_map/ppermute | solution.py:21
  27.1 10.0 %collective-permute-start.5 = (f32[7,40,128]{2,1,0:T(8,128)S(1)}, f32[7,40,128]{2,1,0:T(8,128)S(1)}, u32[]{:S(2)}, u32[]{:S(2)}) collective-permute-start(f32[7,40,128]{2,1,0:T(8,128)S(1)} %get-tuple-element.59), channel_id=1, source_target_pairs={{1,2},{3,4},{5,6},{7,8},{9,10},{11,12},{13,14},{2,1},{4,3},{6,5},{... | collective-permute-start | bytes 430088 | tf_op jit(solution)/shard_map/ppermute | solution.py:21

commit v6 on v5

--- a/solution.py
+++ b/solution.py
@@ -477,7 +477,7 @@
 
 
 def last_kernel(
-    e, scale, halo, got_first, got_second, flags, pe_in, pscale_in, ph1_in, pe1_in, h1_in, e1_ends, e1_in, h2_in, e2_in,
+    e, scale, halo, got_second, got_first, flags, pe_in, pscale_in, ph1_in, pe1_in, h1_in, e1_ends, e1_in, h2_in, e2_in,
     e_most, j_rest, gains, runs, cells, pol, cur,
     e_to, h_to, pol_to, cur_to, e_out, h_out, pol_out, cur_out, late, rows, gain_rows, sems,
 ):
@@ -687,7 +687,8 @@
         [e, h, a, scale, halo, pe, pscale, ph1, pe1, y_second, y_first, flags],
         "ends",
     )
-    z_first, z_second = swapped(z_first, "gz", 0), swapped(z_second, "gz", 1)
+    z_second = swapped(z_second, "gz", 1)
+    z_first = swapped(z_first, "gz", 0)
     slabs = (3, SLABS, EXT, width)
     e1, h2, e2 = call(
         middle_kernel,
@@ -712,7 +713,7 @@
         last_kernel,
         [flat, flat, blocks, blocks],
         [
-            e, scale, halo, z_first, z_second, flags, pe, pscale, ph1, pe1, h1_ends, e1_ends, e1, h2, e2,
+            e, scale, halo, z_second, z_first, flags, pe, pscale, ph1, pe1, h1_ends, e1_ends, e1, h2, e2,
             e_most, j_rest, gains, runs, cells, pol2, cur2,
         ],
         "last",

time: 40.1 us -> 40.1 us (level)
  the two profiles are of different devices: /device:TPU:102 before, /device:TPU:70 now
where the time goes in v6:
time: 40.1 us; the launch traced here: 39.8 us
  starting transfers between devices  20.6 us (51%)
  Pallas kernels  13.2 us (33%)
  waiting for transfers between devices  4.49 us (11%)
  between operations  1.41 us (4%)
    ppermute x6, starting transfers between devices, swapped(): lax.ppermute(value, axis, pairs + [(upper, lower) for lower, upper in pai...  20.6 us
    pallas_call x7, Pallas kernels, call(): pl.pallas_call(kernel, out_shape=outs, in_specs=specs, out_specs=out_spec...  13.2 us
    ppermute x6, waiting for transfers between devices, swapped(): lax.ppermute(value, axis, pairs + [(upper, lower) for lower, upper in pai...  4.49 us
  transfers between devices with their start and end apart: 6, of which 3 were waited for; matrix products, arithmetic and copies ran while one was open for 0% of the time, Pallas kernels for 11%

profile of v6, /device:TPU:70, one launch (start us, length us, event | category | flops | bytes accessed | tf_op | source)
XLA Modules:
  0.0 39.8 jit_solution(12877766266309144586)
XLA Ops:
  1.3 0.1 stack.27
  1.4 3.4 %first.1 = (f32[3,512,128]{2,1,0:T(8,128)S(1)}, f32[3,512,128]{2,1,0:T(8,128)S(1)}, f32[3,128,128]{2,1,0:T(8,128)S(1)}, f32[3,128,128]{2,1,0:T(8,128)S(1)}, f32[...) custom-call(f32[3,512,128]{2,1,0:T(8,128)} %bitcast.16, ...), custom_call_target="tpu_custom_call" | custom-call | tf_op jit(solution)/shard_map/first/pallas_call | solution.py:641
  4.9 2.2 %collective-permute-start = (f32[15,16,128]{2,1,0:T(8,128)S(1)}, f32[15,16,128]{2,1,0:T(8,128)S(1)}, u32[]{:S(2)}, u32[]{:S(2)}) collective-permute-start(f32[15,16,128]{2,1,0:T(8,128)S(1)} %get-tuple-element.47), channel_id=1, source_target_pairs={{128,256},{256,128},{129,257},{257,129},{130,258},{258,130},{131,2... | collective-permute-start | bytes 368648 | tf_op jit(solution)/shard_map/ppermute | solution.py:21
  7.0 1.9 %collective-permute-start.1 = (f32[15,16,128]{2,1,0:T(8,128)S(1)}, f32[15,16,128]{2,1,0:T(8,128)S(1)}, u32[]{:S(2)}, u32[]{:S(2)}) collective-permute-start(f32[15,16,128]{2,1,0:T(8,128)S(1)} %get-tuple-element.48), channel_id=1, source_target_pairs={{0,128},{256,384},{128,0},{384,256},{1,129},{257,385},{129,1},{385... | collective-permute-start | bytes 368648 | tf_op jit(solution)/shard_map/ppermute | solution.py:21
  9.0 1.4 %own.1 = f32[10,32,128]{2,1,0:T(8,128)S(1)} custom-call(f32[3,512,128]{2,1,0:T(8,128)S(1)} %get-tuple-element.45.e, f32[3,512,128]{2,1,0:T(8,128)S(1)} %get-tuple-element.49.h, f32[3,512,128]{2,1,0:T(8,128)S(1)} %get-tuple-element.50.a, f32[512,128]{1,0:T(8,128)S(1)} %get-tuple-element.46.scale), custom_call_target="tpu_custom_call" | custom-call | tf_op jit(solution)/shard_map/own/pallas_call | solution.py:641
  10.3 0.7 %collective-permute-done.got_second = f32[15,16,128]{2,1,0:T(8,128)S(1)} collective-permute-done((f32[15,16,128]{2,1,0:T(8,128)S(1)}, f32[15,16,128]{2,1,0:T(8,128)S(1)}, u32[]{:S(2)}, u32[]{:S(2)}) %collective-permute-start) | collective-permute-done | bytes 122912 | tf_op jit(solution)/shard_map/ppermute | solution.py:21
  11.1 0.0 collective-permute-done.1.got_first
  11.1 1.5 %faces.1 = (f32[10,128,128]{2,1,0:T(8,128)S(1)}, f32[3,40,128]{2,1,0:T(8,128)S(1)}, f32[40,128]{1,0:T(8,128)S(1)}, f32[3,40,128]{2,1,0:T(8,128)S(1)}, f32[3,40,1...) custom-call(f32[15,16,128]{2,1,0:T(8,128)S(1)} %collective-permute-done.got_second, ...), custom_call_target="tpu_custom_call" | custom-call | tf_op jit(solution)/shard_map/faces/pallas_call | solution.py:641
  12.6 5.8 %collective-permute-start.2 = (f32[1,40,128]{2,1,0:T(8,128)S(1)}, f32[1,40,128]{2,1,0:T(8,128)S(1)}, u32[]{:S(2)}, u32[]{:S(2)}) collective-permute-start(f32[1,40,128]{2,1,0:T(8,128)S(1)} %get-tuple-element.56), channel_id=1, source_target_pairs={{16,32},{48,64},{80,96},{32,16},{64,48},{96,80},{17,33},{49,65},{8... | collective-permute-start | bytes 61448 | tf_op jit(solution)/shard_map/ppermute | solution.py:21
  18.3 1.9 %collective-permute-start.3 = (f32[1,40,128]{2,1,0:T(8,128)S(1)}, f32[1,40,128]{2,1,0:T(8,128)S(1)}, u32[]{:S(2)}, u32[]{:S(2)}) collective-permute-start(f32[1,40,128]{2,1,0:T(8,128)S(1)} %get-tuple-element.57), channel_id=1, source_target_pairs={{0,16},{32,48},{64,80},{96,112},{16,0},{48,32},{80,64},{112,96},{1... | collective-permute-start | bytes 61448 | tf_op jit(solution)/shard_map/ppermute | solution.py:21
  20.3 1.6 %collective-permute-done.2.got_second = f32[1,40,128]{2,1,0:T(8,128)S(1)} collective-permute-done((f32[1,40,128]{2,1,0:T(8,128)S(1)}, f32[1,40,128]{2,1,0:T(8,128)S(1)}, u32[]{:S(2)}, u32[]{:S(2)}) %collective-permute-start.2) | collective-permute-done | bytes 20512 | tf_op jit(solution)/shard_map/ppermute | solution.py:21
  21.9 2.2 %collective-permute-done.3.got_first = f32[1,40,128]{2,1,0:T(8,128)S(1)} collective-permute-done((f32[1,40,128]{2,1,0:T(8,128)S(1)}, f32[1,40,128]{2,1,0:T(8,128)S(1)}, u32[]{:S(2)}, u32[]{:S(2)}) %collective-permute-start.3) | collective-permute-done | bytes 20512 | tf_op jit(solution)/shard_map/ppermute | solution.py:21
  24.0 1.0 %ends.1 = (f32[3,40,128]{2,1,0:T(8,128)S(1)}, f32[40,128]{1,0:T(8,128)S(1)}, f32[3,40,128]{2,1,0:T(8,128)S(1)}, f32[3,40,128]{2,1,0:T(8,128)S(1)}, f32[3,3,40,12...) custom-call(f32[3,512,128]{2,1,0:T(8,128)S(1)} %get-tuple-element.45.e,, ...), custom_call_target="tpu_custom_call" | custom-call | tf_op jit(solution)/shard_map/ends/pallas_call | solution.py:641
  25.0 2.0 %collective-permute-start.4 = (f32[7,40,128]{2,1,0:T(8,128)S(1)}, f32[7,40,128]{2,1,0:T(8,128)S(1)}, u32[]{:S(2)}, u32[]{:S(2)}) collective-permute-start(f32[7,40,128]{2,1,0:T(8,128)S(1)} %get-tuple-element.58), channel_id=1, source_target_pairs={{1,2},{3,4},{5,6},{7,8},{9,10},{11,12},{13,14},{2,1},{4,3},{6,5},{... | collective-permute-start | bytes 430088 | tf_op jit(solution)/shard_map/ppermute | solution.py:21
  27.1 6.8 %collective-permute-start.5 = (f32[7,40,128]{2,1,0:T(8,128)S(1)}, f32[7,40,128]{2,1,0:T(8,128)S(1)}, u32[]{:S(2)}, u32[]{:S(2)}) collective-permute-start(f32[7,40,128]{2,1,0:T(8,128)S(1)} %get-tuple-element.59), channel_id=1, source_target_pairs={{0,1},{2,3},{4,5},{6,7},{8,9},{10,11},{12,13},{14,15},{1,0},{3,2},... | collective-permute-start | bytes 430088 | tf_op jit(solution)/shard_map/ppermute | solution.py:21
  33.9 1.8 %middle.1 = (f32[3,16,40,128]{3,2,1,0:T(8,128)S(1)}, f32[3,512,128]{2,1,0:T(8,128)S(1)}, f32[3,512,128]{2,1,0:T(8,128)S(1)}) custom-call(f32[3,512,128]{2,1,0:T(8,128)S(1)} %get-tuple-element.45.e, f32[3,512,128]{2,1,0:T(8,128)S(1)} %get-tuple-element.49.h, f32[3,512,128]{2,1,0:T(8,128)S(1)} %get-tuple-element.50.a, f32[512,128]{1,0:T(8,128)S(1)} %get-tuple-element.46.scale, ...), custom_call_target="tpu_custom_call" | custom-call | tf_op jit(solution)/shard_map/middle/pallas_call | solution.py:641
  35.7 1.4 %blocks.1 = (f32[3,384,128]{2,1,0:T(8,128)S(1)}, f32[3,128,128]{2,1,0:T(8,128)S(1)}, f32[3,128,128]{2,1,0:T(8,128)S(1)}, f32[3,4,32,128]{3,2,1,0:T(8,128)S(1)}, f32[512,128]{1,0:T(8,128)S(1)}) custom-call(f32[512,128]{1,0:T(8,128)S(1)} %get-tuple-element.46.scale, f32[3,640,128]{2,1,0:T(8,128)S(1)} %bitcast.15, ...), custom_call_target="tpu_custom_call" | custom-call | tf_op jit(solution)/shard_map/blocks/pallas_call | solution.py:641
  37.1 0.0 collective-permute-done.4.got_second
  37.1 0.0 collective-permute-done.5.got_first
  37.1 2.7 %last.1 = (f32[3,512,128]{2,1,0:T(8,128)}, f32[3,512,128]{2,1,0:T(8,128)}, f32[3,128,128]{2,1,0:T(8,128)}, f32[3,128,128]{2,1,0:T(8,128)}) custom-call(f32[3,512,128]{2,1,0:T(8,128)S(1)} %get-tuple-element.45.e, f32[512,128]{1,0:T(8,128)S(1)} %get-tuple-element.46.scale, f32[10,128,128]{2,1,0:T(8,128)S(1)} %get-tuple-element.51.halo, ...), custom_call_target="tpu_custom_call" | custom-call | tf_op jit(solution)/shard_map/last/pallas_call | solution.py:641
  (1 shorter events, 0.0 us)
Async XLA Ops:
  4.9 6.2 %collective-permute-start = (f32[15,16,128]{2,1,0:T(8,128)S(1)}, f32[15,16,128]{2,1,0:T(8,128)S(1)}, u32[]{:S(2)}, u32[]{:S(2)}) collective-permute-start(f32[15,16,128]{2,1,0:T(8,128)S(1)} %get-tuple-element.47), channel_id=1, source_target_pairs={{128,256},{256,128},{129,257},{257,129},{130,258},{258,130},{131,2... | collective-permute-start | bytes 368648 | tf_op jit(solution)/shard_map/ppermute | solution.py:21
  7.0 4.0 %collective-permute-start.1 = (f32[15,16,128]{2,1,0:T(8,128)S(1)}, f32[15,16,128]{2,1,0:T(8,128)S(1)}, u32[]{:S(2)}, u32[]{:S(2)}) collective-permute-start(f32[15,16,128]{2,1,0:T(8,128)S(1)} %get-tuple-element.48), channel_id=1, source_target_pairs={{0,128},{256,384},{128,0},{384,256},{1,129},{257,385},{129,1},{385... | collective-permute-start | bytes 368648 | tf_op jit(solution)/shard_map/ppermute | solution.py:21
  12.6 9.3 %collective-permute-start.2 = (f32[1,40,128]{2,1,0:T(8,128)S(1)}, f32[1,40,128]{2,1,0:T(8,128)S(1)}, u32[]{:S(2)}, u32[]{:S(2)}) collective-permute-start(f32[1,40,128]{2,1,0:T(8,128)S(1)} %get-tuple-element.56), channel_id=1, source_target_pairs={{16,32},{48,64},{80,96},{32,16},{64,48},{96,80},{17,33},{49,65},{8... | collective-permute-start | bytes 61448 | tf_op jit(solution)/shard_map/ppermute | solution.py:21
  18.3 5.7 %collective-permute-start.3 = (f32[1,40,128]{2,1,0:T(8,128)S(1)}, f32[1,40,128]{2,1,0:T(8,128)S(1)}, u32[]{:S(2)}, u32[]{:S(2)}) collective-permute-start(f32[1,40,128]{2,1,0:T(8,128)S(1)} %get-tuple-element.57), channel_id=1, source_target_pairs={{0,16},{32,48},{64,80},{96,112},{16,0},{48,32},{80,64},{112,96},{1... | collective-permute-start | bytes 61448 | tf_op jit(solution)/shard_map/ppermute | solution.py:21
  25.0 12.0 %collective-permute-start.4 = (f32[7,40,128]{2,1,0:T(8,128)S(1)}, f32[7,40,128]{2,1,0:T(8,128)S(1)}, u32[]{:S(2)}, u32[]{:S(2)}) collective-permute-start(f32[7,40,128]{2,1,0:T(8,128)S(1)} %get-tuple-element.58), channel_id=1, source_target_pairs={{1,2},{3,4},{5,6},{7,8},{9,10},{11,12},{13,14},{2,1},{4,3},{6,5},{... | collective-permute-start | bytes 430088 | tf_op jit(solution)/shard_map/ppermute | solution.py:21
  27.1 10.0 %collective-permute-start.5 = (f32[7,40,128]{2,1,0:T(8,128)S(1)}, f32[7,40,128]{2,1,0:T(8,128)S(1)}, u32[]{:S(2)}, u32[]{:S(2)}) collective-permute-start(f32[7,40,128]{2,1,0:T(8,128)S(1)} %get-tuple-element.59), channel_id=1, source_target_pairs={{0,1},{2,3},{4,5},{6,7},{8,9},{10,11},{12,13},{14,15},{1,0},{3,2},... | collective-permute-start | bytes 430088 | tf_op jit(solution)/shard_map/ppermute | solution.py:21

commit v7 on v5

--- a/solution.py
+++ b/solution.py
@@ -453,7 +453,7 @@
 
 def blocks_kernel(
     scale, e1, e2, inverse, runs, cells, count, decay, restore, drive, pol, cur,
-    e_most, pol_out, cur_out, j_rest, gain_out, rows, j_rows, gain_rows,
+    e_most, pol_out, cur_out, j_rest, gain_out, gain_rows, rows, j_rows,
 ):
     gather_rows(e1, EXT, runs, rows)
     j_rows[...] = jnp.zeros_like(j_rows)
@@ -478,8 +478,8 @@
 
 def last_kernel(
     e, scale, halo, got_first, got_second, flags, pe_in, pscale_in, ph1_in, pe1_in, h1_in, e1_ends, e1_in, h2_in, e2_in,
-    e_most, j_rest, gains, runs, cells, pol, cur,
-    e_to, h_to, pol_to, cur_to, e_out, h_out, pol_out, cur_out, late, rows, gain_rows, sems,
+    e_most, j_rest, gains, gain_rows, runs, cells, pol, cur,
+    e_to, h_to, pol_to, cur_to, e_out, h_out, pol_out, cur_out, late, rows, sems,
 ):
     started = []
 
@@ -568,7 +568,6 @@
     for b in range(rows.shape[1]):
         run = runs[0, b]
         at = jnp.where(run < ROWS, run, jnp.where(run >= top * ROWS, run - (top - 1) * ROWS, 2 * ROWS))
-        gain_rows[pl.ds(b, 1), :] = gains[pl.ds(run, 1), :]
         for c in range(3):
             rows[c, pl.ds(b, 1), :] = late[c, pl.ds(at, 1), :]
     offsets = lax.bitwise_and(cells[...], LANES - 1)
@@ -698,27 +697,27 @@
     )
     scalars.add(id(runs))
     dma = pltpu.SemaphoreType.DMA
-    e_most, pol2, cur2, j_rest, gains = call(
+    e_most, pol2, cur2, j_rest, gains, gain_rows = call(
         blocks_kernel,
-        [arr(3, 12 * ROWS, width), blocks, blocks, arr(3, len(END_SLABS), ROWS, width), arr(runs_all, width)],
+        [arr(3, 12 * ROWS, width), blocks, blocks, arr(3, len(END_SLABS), ROWS, width), arr(runs_all, width), arr(slots, width)],
         [
             scale, e1.reshape(3, SLABS * EXT, width), e2, inverse, runs, cells, block_count,
             decay, restore, drive, pol1, cur1,
         ],
         "blocks",
-        [blocks_vmem, flat_vmem, pltpu.VMEM((slots, width), f32)],
+        [blocks_vmem, flat_vmem],
     )
     e_out, h_out, pol2, cur2 = call(
         last_kernel,
         [flat, flat, blocks, blocks],
         [
             e, scale, halo, z_first, z_second, flags, pe, pscale, ph1, pe1, h1_ends, e1_ends, e1, h2, e2,
-            e_most, j_rest, gains, runs, cells, pol2, cur2,
+            e_most, j_rest, gains, gain_rows, runs, cells, pol2, cur2,
         ],
         "last",
         [
             pltpu.VMEM((3, 4 * ROWS, width), f32), pltpu.VMEM((3, 3 * ROWS, width), f32), blocks_vmem, blocks_vmem,
-            pltpu.VMEM((3, 2 * ROWS + 8, width), f32), blocks_vmem, pltpu.VMEM((slots, width), f32),
+            pltpu.VMEM((3, 2 * ROWS + 8, width), f32), blocks_vmem,
             pltpu.SemaphoreType.DMA((8,)),
         ],
         out_hbm=(0, 1, 2, 3),

time: 40.1 us -> 40 us (level)
  no operation moved by 1% of the time
where the time goes in v7:
time: 40 us; the launch traced here: 39.8 us
  starting transfers between devices  20.7 us (52%)
  Pallas kernels  13.1 us (33%)
  waiting for transfers between devices  4.48 us (11%)
  between operations  1.41 us (4%)
    ppermute x6, starting transfers between devices, swapped(): lax.ppermute(value, axis, pairs + [(upper, lower) for lower, upper in pai...  20.7 us
    pallas_call x7, Pallas kernels, call(): pl.pallas_call(kernel, out_shape=outs, in_specs=specs, out_specs=out_spec...  13.1 us
    ppermute x6, waiting for transfers between devices, swapped(): lax.ppermute(value, axis, pairs + [(upper, lower) for lower, upper in pai...  4.48 us
  transfers between devices with their start and end apart: 6, of which 3 were waited for; matrix products, arithmetic and copies ran while one was open for 0% of the time, Pallas kernels for 11%

profile of v7, /device:TPU:102, one launch (start us, length us, event | category | flops | bytes accessed | tf_op | source)
XLA Modules:
  0.0 39.8 jit_solution(12758201941834225961)
XLA Ops:
  1.3 0.1 stack.27
  1.4 3.4 %first.1 = (f32[3,512,128]{2,1,0:T(8,128)S(1)}, f32[3,512,128]{2,1,0:T(8,128)S(1)}, f32[3,128,128]{2,1,0:T(8,128)S(1)}, f32[3,128,128]{2,1,0:T(8,128)S(1)}, f32[...) custom-call(f32[3,512,128]{2,1,0:T(8,128)} %bitcast.16, ...), custom_call_target="tpu_custom_call" | custom-call | tf_op jit(solution)/shard_map/first/pallas_call | solution.py:640
  4.9 2.2 %collective-permute-start = (f32[15,16,128]{2,1,0:T(8,128)S(1)}, f32[15,16,128]{2,1,0:T(8,128)S(1)}, u32[]{:S(2)}, u32[]{:S(2)}) collective-permute-start(f32[15,16,128]{2,1,0:T(8,128)S(1)} %get-tuple-element.48), channel_id=1, source_target_pairs={{128,256},{256,128},{129,257},{257,129},{130,258},{258,130},{131,2... | collective-permute-start | bytes 368648 | tf_op jit(solution)/shard_map/ppermute | solution.py:21
  7.1 1.9 %collective-permute-start.1 = (f32[15,16,128]{2,1,0:T(8,128)S(1)}, f32[15,16,128]{2,1,0:T(8,128)S(1)}, u32[]{:S(2)}, u32[]{:S(2)}) collective-permute-start(f32[15,16,128]{2,1,0:T(8,128)S(1)} %get-tuple-element.49), channel_id=1, source_target_pairs={{0,128},{256,384},{128,0},{384,256},{1,129},{257,385},{129,1},{385... | collective-permute-start | bytes 368648 | tf_op jit(solution)/shard_map/ppermute | solution.py:21
  9.0 1.4 %own.1 = f32[10,32,128]{2,1,0:T(8,128)S(1)} custom-call(f32[3,512,128]{2,1,0:T(8,128)S(1)} %get-tuple-element.46.e, f32[3,512,128]{2,1,0:T(8,128)S(1)} %get-tuple-element.50.h, f32[3,512,128]{2,1,0:T(8,128)S(1)} %get-tuple-element.51.a, f32[512,128]{1,0:T(8,128)S(1)} %get-tuple-element.47.scale), custom_call_target="tpu_custom_call" | custom-call | tf_op jit(solution)/shard_map/own/pallas_call | solution.py:640
  10.3 0.7 %collective-permute-done.got_second = f32[15,16,128]{2,1,0:T(8,128)S(1)} collective-permute-done((f32[15,16,128]{2,1,0:T(8,128)S(1)}, f32[15,16,128]{2,1,0:T(8,128)S(1)}, u32[]{:S(2)}, u32[]{:S(2)}) %collective-permute-start) | collective-permute-done | bytes 122912 | tf_op jit(solution)/shard_map/ppermute | solution.py:21
  11.1 0.0 collective-permute-done.1.got_first
  11.1 1.5 %faces.1 = (f32[10,128,128]{2,1,0:T(8,128)S(1)}, f32[3,40,128]{2,1,0:T(8,128)S(1)}, f32[40,128]{1,0:T(8,128)S(1)}, f32[3,40,128]{2,1,0:T(8,128)S(1)}, f32[3,40,1...) custom-call(f32[15,16,128]{2,1,0:T(8,128)S(1)} %collective-permute-done.got_second, ...), custom_call_target="tpu_custom_call" | custom-call | tf_op jit(solution)/shard_map/faces/pallas_call | solution.py:640
  12.6 5.8 %collective-permute-start.2 = (f32[1,40,128]{2,1,0:T(8,128)S(1)}, f32[1,40,128]{2,1,0:T(8,128)S(1)}, u32[]{:S(2)}, u32[]{:S(2)}) collective-permute-start(f32[1,40,128]{2,1,0:T(8,128)S(1)} %get-tuple-element.57), channel_id=1, source_target_pairs={{16,32},{48,64},{80,96},{32,16},{64,48},{96,80},{17,33},{49,65},{8... | collective-permute-start | bytes 61448 | tf_op jit(solution)/shard_map/ppermute | solution.py:21
  18.3 1.9 %collective-permute-start.3 = (f32[1,40,128]{2,1,0:T(8,128)S(1)}, f32[1,40,128]{2,1,0:T(8,128)S(1)}, u32[]{:S(2)}, u32[]{:S(2)}) collective-permute-start(f32[1,40,128]{2,1,0:T(8,128)S(1)} %get-tuple-element.58), channel_id=1, source_target_pairs={{0,16},{32,48},{64,80},{96,112},{16,0},{48,32},{80,64},{112,96},{1... | collective-permute-start | bytes 61448 | tf_op jit(solution)/shard_map/ppermute | solution.py:21
  20.3 1.6 %collective-permute-done.2.got_second = f32[1,40,128]{2,1,0:T(8,128)S(1)} collective-permute-done((f32[1,40,128]{2,1,0:T(8,128)S(1)}, f32[1,40,128]{2,1,0:T(8,128)S(1)}, u32[]{:S(2)}, u32[]{:S(2)}) %collective-permute-start.2) | collective-permute-done | bytes 20512 | tf_op jit(solution)/shard_map/ppermute | solution.py:21
  21.9 2.2 %collective-permute-done.3.got_first = f32[1,40,128]{2,1,0:T(8,128)S(1)} collective-permute-done((f32[1,40,128]{2,1,0:T(8,128)S(1)}, f32[1,40,128]{2,1,0:T(8,128)S(1)}, u32[]{:S(2)}, u32[]{:S(2)}) %collective-permute-start.3) | collective-permute-done | bytes 20512 | tf_op jit(solution)/shard_map/ppermute | solution.py:21
  24.0 1.0 %ends.1 = (f32[3,40,128]{2,1,0:T(8,128)S(1)}, f32[40,128]{1,0:T(8,128)S(1)}, f32[3,40,128]{2,1,0:T(8,128)S(1)}, f32[3,40,128]{2,1,0:T(8,128)S(1)}, f32[3,3,40,12...) custom-call(f32[3,512,128]{2,1,0:T(8,128)S(1)} %get-tuple-element.46.e,, ...), custom_call_target="tpu_custom_call" | custom-call | tf_op jit(solution)/shard_map/ends/pallas_call | solution.py:640
  25.0 2.0 %collective-permute-start.4 = (f32[7,40,128]{2,1,0:T(8,128)S(1)}, f32[7,40,128]{2,1,0:T(8,128)S(1)}, u32[]{:S(2)}, u32[]{:S(2)}) collective-permute-start(f32[7,40,128]{2,1,0:T(8,128)S(1)} %get-tuple-element.59), channel_id=1, source_target_pairs={{0,1},{2,3},{4,5},{6,7},{8,9},{10,11},{12,13},{14,15},{1,0},{3,2},... | collective-permute-start | bytes 430088 | tf_op jit(solution)/shard_map/ppermute | solution.py:21
  27.1 6.8 %collective-permute-start.5 = (f32[7,40,128]{2,1,0:T(8,128)S(1)}, f32[7,40,128]{2,1,0:T(8,128)S(1)}, u32[]{:S(2)}, u32[]{:S(2)}) collective-permute-start(f32[7,40,128]{2,1,0:T(8,128)S(1)} %get-tuple-element.60), channel_id=1, source_target_pairs={{1,2},{3,4},{5,6},{7,8},{9,10},{11,12},{13,14},{2,1},{4,3},{6,5},{... | collective-permute-start | bytes 430088 | tf_op jit(solution)/shard_map/ppermute | solution.py:21
  33.9 1.8 %middle.1 = (f32[3,16,40,128]{3,2,1,0:T(8,128)S(1)}, f32[3,512,128]{2,1,0:T(8,128)S(1)}, f32[3,512,128]{2,1,0:T(8,128)S(1)}) custom-call(f32[3,512,128]{2,1,0:T(8,128)S(1)} %get-tuple-element.46.e, f32[3,512,128]{2,1,0:T(8,128)S(1)} %get-tuple-element.50.h, f32[3,512,128]{2,1,0:T(8,128)S(1)} %get-tuple-element.51.a, f32[512,128]{1,0:T(8,128)S(1)} %get-tuple-element.47.scale, ...), custom_call_target="tpu_custom_call" | custom-call | tf_op jit(solution)/shard_map/middle/pallas_call | solution.py:640
  35.7 1.4 %blocks.1 = (f32[3,384,128]{2,1,0:T(8,128)S(1)}, f32[3,128,128]{2,1,0:T(8,128)S(1)}, f32[3,128,128]{2,1,0:T(8,128)S(1)}, f32[3,4,32,128]{3,2,1,0:T(8,128)S(1)}, ...) custom-call(f32[512,128]{1,0:T(8,128)S(1)} %get-tuple-element.47.scale, f32[3,640,128]{2,1,0:T(8,128)S(1)} %bitcast.15, ...), custom_call_target="tpu_custom_call" | custom-call | tf_op jit(solution)/shard_map/blocks/pallas_call | solution.py:640
  37.1 0.0 collective-permute-done.4.got_first
  37.1 0.0 collective-permute-done.5.got_second
  37.1 2.6 %last.1 = (f32[3,512,128]{2,1,0:T(8,128)}, f32[3,512,128]{2,1,0:T(8,128)}, f32[3,128,128]{2,1,0:T(8,128)}, f32[3,128,128]{2,1,0:T(8,128)}) custom-call(f32[3,512,128]{2,1,0:T(8,128)S(1)} %get-tuple-element.46.e, f32[512,128]{1,0:T(8,128)S(1)} %get-tuple-element.47.scale, f32[10,128,128]{2,1,0:T(8,128)S(1)} %get-tuple-element.52.halo, ...), custom_call_target="tpu_custom_call" | custom-call | tf_op jit(solution)/shard_map/last/pallas_call | solution.py:640
  (1 shorter events, 0.0 us)
Async XLA Ops:
  4.9 6.2 %collective-permute-start = (f32[15,16,128]{2,1,0:T(8,128)S(1)}, f32[15,16,128]{2,1,0:T(8,128)S(1)}, u32[]{:S(2)}, u32[]{:S(2)}) collective-permute-start(f32[15,16,128]{2,1,0:T(8,128)S(1)} %get-tuple-element.48), channel_id=1, source_target_pairs={{128,256},{256,128},{129,257},{257,129},{130,258},{258,130},{131,2... | collective-permute-start | bytes 368648 | tf_op jit(solution)/shard_map/ppermute | solution.py:21
  7.1 4.0 %collective-permute-start.1 = (f32[15,16,128]{2,1,0:T(8,128)S(1)}, f32[15,16,128]{2,1,0:T(8,128)S(1)}, u32[]{:S(2)}, u32[]{:S(2)}) collective-permute-start(f32[15,16,128]{2,1,0:T(8,128)S(1)} %get-tuple-element.49), channel_id=1, source_target_pairs={{0,128},{256,384},{128,0},{384,256},{1,129},{257,385},{129,1},{385... | collective-permute-start | bytes 368648 | tf_op jit(solution)/shard_map/ppermute | solution.py:21
  12.6 9.3 %collective-permute-start.2 = (f32[1,40,128]{2,1,0:T(8,128)S(1)}, f32[1,40,128]{2,1,0:T(8,128)S(1)}, u32[]{:S(2)}, u32[]{:S(2)}) collective-permute-start(f32[1,40,128]{2,1,0:T(8,128)S(1)} %get-tuple-element.57), channel_id=1, source_target_pairs={{16,32},{48,64},{80,96},{32,16},{64,48},{96,80},{17,33},{49,65},{8... | collective-permute-start | bytes 61448 | tf_op jit(solution)/shard_map/ppermute | solution.py:21
  18.3 5.7 %collective-permute-start.3 = (f32[1,40,128]{2,1,0:T(8,128)S(1)}, f32[1,40,128]{2,1,0:T(8,128)S(1)}, u32[]{:S(2)}, u32[]{:S(2)}) collective-permute-start(f32[1,40,128]{2,1,0:T(8,128)S(1)} %get-tuple-element.58), channel_id=1, source_target_pairs={{0,16},{32,48},{64,80},{96,112},{16,0},{48,32},{80,64},{112,96},{1... | collective-permute-start | bytes 61448 | tf_op jit(solution)/shard_map/ppermute | solution.py:21
  25.0 12.1 %collective-permute-start.4 = (f32[7,40,128]{2,1,0:T(8,128)S(1)}, f32[7,40,128]{2,1,0:T(8,128)S(1)}, u32[]{:S(2)}, u32[]{:S(2)}) collective-permute-start(f32[7,40,128]{2,1,0:T(8,128)S(1)} %get-tuple-element.59), channel_id=1, source_target_pairs={{0,1},{2,3},{4,5},{6,7},{8,9},{10,11},{12,13},{14,15},{1,0},{3,2},... | collective-permute-start | bytes 430088 | tf_op jit(solution)/shard_map/ppermute | solution.py:21
  27.1 10.0 %collective-permute-start.5 = (f32[7,40,128]{2,1,0:T(8,128)S(1)}, f32[7,40,128]{2,1,0:T(8,128)S(1)}, u32[]{:S(2)}, u32[]{:S(2)}) collective-permute-start(f32[7,40,128]{2,1,0:T(8,128)S(1)} %get-tuple-element.60), channel_id=1, source_target_pairs={{1,2},{3,4},{5,6},{7,8},{9,10},{11,12},{13,14},{2,1},{4,3},{6,5},{... | collective-permute-start | bytes 430088 | tf_op jit(solution)/shard_map/ppermute | solution.py:21
